TPU v7x, 32 devices: a whole 2x2x4 slice. The times are simulated.
32 devices in a mesh: dp: 8 (over z, x), dim: 4 (over y, core).
Axes of the slice: x: 2, y: 2, z: 4, core: 2. Of those that a mesh axis runs over, the one named last changes fastest.
Arguments:
- vectors: bfloat16 [768, 8192], P('dim', 'dp'), may hold values from -30 to 30
- codes: int32 [64, 8192], P('dim', 'dp'), may hold values from 0 to 255, as said below
- codebook: bfloat16 [256, 768], P(None, 'dim'), may hold values from -4 to 4
Outputs:
- rotation: float32 [768, 768], P('dim')
- new_codebook: float32 [256, 768], P('dp', 'dim')
Inputs may be any that keep to these rules, and one draw needn't show every extreme that they name: `codes`: each entry names a centroid of its subspace; in each subspace at least one centroid, which one is drawn from the seed, is named by no vector.
All inputs are finite; a program needn't handle non-finite values.
Results may differ from a plain program's by a relative error of at most 0.003.
Values may be sent and summed in bfloat16 or wider, within the bound.
No kernel may reach another device: no remote copies, remote signals or barrier semaphores. Data moves between devices by JAX's collectives and lax.ppermute only.
A program may use at most 64 MiB of HBM per device.

v0:
```python
import jax
import jax.numpy as jnp
from jax import lax
from jax.sharding import PartitionSpec as P

NS_STEPS = 4


def per_device(vectors, codes, codebook):
    local_width = vectors.shape[0]
    row_count = vectors.shape[1]
    sub_local = codes.shape[0]
    sub_width = local_width // sub_local
    centroid_count = codebook.shape[0]
    dp_count = lax.axis_size("dp")
    dim_count = lax.axis_size("dim")
    total_width = local_width * dim_count
    block_rows = min(512, row_count)
    block_count = row_count // block_rows
    levels = jnp.arange(centroid_count, dtype=jnp.int32)
    book_cube = codebook.reshape(centroid_count, sub_local, sub_width)
    gathered_rows = lax.all_gather(vectors, "dim", axis=0, tiled=True)

    def block_onehot(block_index):
        start = block_index * block_rows
        code_block = lax.dynamic_slice_in_dim(codes, start, block_rows, 1)
        onehot = (code_block[:, :, None] == levels[None, None, :]).astype(jnp.bfloat16)
        row_block = lax.dynamic_slice_in_dim(gathered_rows, start, block_rows, 1)
        return (onehot, row_block)

    def add_cross(block_index, cross_part):
        onehot, row_block = block_onehot(block_index)
        decoded = jnp.einsum("mnk,kmd->nmd", onehot, book_cube, preferred_element_type=jnp.float32)
        decoded = decoded.reshape(block_rows, local_width).astype(jnp.bfloat16)
        return cross_part + jnp.einsum(
            "nd,cn->dc", decoded, row_block, preferred_element_type=jnp.float32
        )

    cross_part = lax.fori_loop(
        0, block_count, add_cross, jnp.zeros((local_width, total_width), jnp.float32)
    )

    def newton_update(rows, whole):
        gram_rows = jnp.dot(rows, whole.T, precision=lax.Precision.HIGHEST)
        return 1.5 * rows - 0.5 * jnp.dot(gram_rows, whole, precision=lax.Precision.HIGHEST)

    own_rows = lax.psum_scatter(cross_part, "dp", scatter_dimension=0, tiled=True)
    thin_width = own_rows.shape[0]
    dim_index = lax.axis_index("dim")

    def gather_spread(rows):
        return lax.all_gather(rows, ("dp", "dim"), axis=0, tiled=True)

    gathered = gather_spread(own_rows)
    magnitude = jnp.sqrt(jnp.sum(gathered * gathered))
    gathered = gathered / magnitude
    own_rows = own_rows / magnitude

    def spread_step(iteration, carry):
        rows, whole = carry
        rows = newton_update(rows, whole)
        return (rows, gather_spread(rows))

    own_rows, gathered = lax.fori_loop(0, NS_STEPS - 1, spread_step, (own_rows, gathered))
    shaped = gathered.reshape(dp_count, dim_count, thin_width, total_width)
    block_part = lax.dynamic_slice_in_dim(shaped, dim_index, 1, 1).reshape(local_width, total_width)
    rotation = newton_update(block_part, gathered)
    rotation_low = rotation.astype(jnp.bfloat16)

    def add_centroids(block_index, carry):
        centroid_sums, counts = carry
        onehot, row_block = block_onehot(block_index)
        rotated = jnp.einsum(
            "cn,dc->nd", row_block, rotation_low, preferred_element_type=jnp.float32
        ).astype(jnp.bfloat16)
        rotated = rotated.reshape(block_rows, sub_local, sub_width)
        centroid_sums = centroid_sums + jnp.einsum(
            "mnk,nmd->kmd", onehot, rotated, preferred_element_type=jnp.float32
        )
        counts = counts + jnp.sum(onehot, axis=1, dtype=jnp.float32).T
        return (centroid_sums, counts)

    start_sums = jnp.zeros((centroid_count, sub_local, sub_width), jnp.float32)
    start_counts = jnp.zeros((centroid_count, sub_local), jnp.float32)
    centroid_sums, counts = lax.fori_loop(0, block_count, add_centroids, (start_sums, start_counts))
    owned_sums, owned_counts = (
        lax.psum_scatter(
            centroid_sums.reshape(centroid_count, local_width),
            "dp",
            scatter_dimension=0,
            tiled=True,
        ),
        lax.psum_scatter(counts, "dp", scatter_dimension=0, tiled=True),
    )
    divisor = jnp.repeat(jnp.maximum(owned_counts, 1.0), sub_width, axis=1)
    new_codebook = owned_sums / divisor
    return (rotation, new_codebook)


def solution(mesh):
    placed = (P("dim", "dp"), P("dim", "dp"), P(None, "dim"))
    return jax.shard_map(
        per_device,
        mesh=mesh,
        in_specs=placed,
        out_specs=(P("dim", None), P("dp", "dim")),
        check_vma=False,
    )
```

profile of v0, /device:TPU:0, one launch (start us, length us, event | category | flops | bytes accessed | tf_op | source)
XLA Modules:
  0.0 510.3 jit_solution(16556486879555019935)
XLA Ops:
  8.9 23.1 %all-gather.4.cloned.1.call-done = bf16[768,1024]{1,0:T(8,128)(2,1)} async-done(((bf16[192,1024]{1,0:T(8,128)(2,1)}), bf16[768,1024]{1,0:T(8,128)(2,1)}) %all-gather.4.cloned.1.call-update) | async-done | bytes 1572880 | tf_op jit(solution)/shard_map/all_gather | solution.py:22
  32.0 6.8 %while.43 = (s32[]{:T(128)}, f32[192,768]{1,0:T(8,128)S(1)}, s32[16,1024]{1,0:T(8,128)}, bf16[256,16,12]{0,2,1:T(8,128)(2,1)S(1)}, bf16[768,1024]{1,0:T(8,128)(2...) while((s32[]{:T(128)}, f32[192,768]{1,0:T(8,128)S(1)}, s32[16,1024]{1,0:T(8,128)}, ...), condition=%wide.region_1.0_spmd.clone, body=%wide.region_0.0_spmd.clone.sunk | while | flops 203816960 | bytes 9240761 | solution.py:39
  32.7 2.0 fusion.57
  36.1 2.0 fusion.57
  39.6 62.2 %reduce-scatter.8.cloned.1.call-done = f32[24,768]{1,0:T(8,128)} async-done(((f32[192,768]{1,0:T(8,128)}), f32[24,768]{1,0:T(8,128)}) %reduce-scatter.8.cloned.1.call-update) | async-done | bytes 73744 | tf_op jit(solution)/shard_map/reduce_scatter | solution.py:47
  101.8 59.7 %all-gather.6.cloned.1.call-done = f32[768,768]{1,0:T(8,128)} async-done(((f32[24,768]{1,0:T(8,128)}), f32[768,768]{1,0:T(8,128)}) %all-gather.6.cloned.1.call-update) | async-done | bytes 2359312 | tf_op jit(solution)/shard_map/all_gather | solution.py:52
  161.5 3.0 multiply_reduce_fusion
  167.5 190.8 %while.42 = (s32[]{:T(128)}, f32[24,768]{1,0:T(8,128)}, f32[768,768]{1,0:T(8,128)}, s32[]{:T(128)}) while((s32[]{:T(128)}, f32[24,768]{1,0:T(8,128)}, f32[768,768]{1,0:T(8,128)}, s32[]{:T(128)}) %tuple.82), condition=%wide.region_5.0_spmd, body=%wide.region_4.0_spmd.sunk | while | flops 339793920 | bytes 12386397 | solution.py:64
  167.5 3.7 fusion.52
  171.2 3.5 fusion.53
  174.8 56.3 %all-gather.8.cloned.1.call-done = f32[768,768]{1,0:T(8,128)} async-done(((f32[24,768]{1,0:T(8,128)}), f32[768,768]{1,0:T(8,128)}) %all-gather.8.cloned.1.call-update) | async-done | bytes 2359312 | tf_op jit(solution)/shard_map/while/body/eval_jaxpr/all_gather | solution.py:52
  231.1 3.7 fusion.52
  234.8 3.5 fusion.53
  238.4 56.3 %all-gather.8.cloned.1.call-done = f32[768,768]{1,0:T(8,128)} async-done(((f32[24,768]{1,0:T(8,128)}), f32[768,768]{1,0:T(8,128)}) %all-gather.8.cloned.1.call-update) | async-done | bytes 2359312 | tf_op jit(solution)/shard_map/while/body/eval_jaxpr/all_gather | solution.py:52
  294.7 3.7 fusion.52
  298.4 3.5 fusion.53
  302.0 56.3 %all-gather.8.cloned.1.call-done = f32[768,768]{1,0:T(8,128)} async-done(((f32[24,768]{1,0:T(8,128)}), f32[768,768]{1,0:T(8,128)}) %all-gather.8.cloned.1.call-update) | async-done | bytes 2359312 | tf_op jit(solution)/shard_map/while/body/eval_jaxpr/all_gather | solution.py:52
  359.4 4.1 fusion.21
  363.6 4.4 fusion.19
  367.9 9.3 %while.44 = (s32[]{:T(128)}, f32[256,16,12]{0,2,1:T(8,128)S(1)}, f32[256,16]{0,1:T(8,128)S(1)}, bf16[768,1024]{1,0:T(8,128)(2,1)S(1)}, bf16[192,768]{1,0:T(8,128...) while((s32[]{:T(128)}, f32[256,16,12]{0,2,1:T(8,128)S(1)}, ...), condition=%wide.region_8.0_spmd.clone, body=%wide.region_6.0_spmd.clone.sunk | while | flops 212013056 | bytes 2457766 | solution.py:85
  368.4 2.8 fusion.61
  373.0 2.8 fusion.61
  378.9 59.0 %reduce-scatter.12.cloned.1.call-done = f32[32,16]{1,0:T(8,128)} async-done(((f32[256,16]{1,0:T(8,128)}), f32[32,16]{1,0:T(8,128)}) %reduce-scatter.12.cloned.1.call-update) | async-done | bytes 2064
  438.8 63.2 %reduce-scatter.10.cloned.1.call-done = f32[32,192]{1,0:T(8,128)} async-done(((f32[256,192]{1,0:T(8,128)}), f32[32,192]{1,0:T(8,128)}) %reduce-scatter.10.cloned.1.call-update) | async-done | bytes 24592
  (63 shorter events, 16.3 us)
Async XLA Ops:
  7.2 24.8 %all-gather.4.cloned.1.call-start = ((), (), s32[]{:S(2)}) async-start(), calls=%async_computation.3 | async-start | bytes 1966080 | tf_op jit(solution)/shard_map/all_gather | solution.py:22
  7.9 93.9 %reduce-scatter.8.cloned.1.call-start = ((), (), s32[]{:S(2)}) async-start(), calls=%async_computation.4 | async-start | bytes 663552 | tf_op jit(solution)/shard_map/reduce_scatter | solution.py:47
  32.7 2.1 copy-start
  36.1 2.1 copy-start
  38.7 0.8 copy-start.2
  39.6 122.0 %all-gather.6.cloned.1.call-start = ((), (), s32[]{:S(2)}) async-start(), calls=%async_computation.5 | async-start | bytes 2433024 | tf_op jit(solution)/shard_map/all_gather | solution.py:52
  161.5 3.7 copy-start.3
  165.2 1.6 copy-start.5
  167.5 63.6 %all-gather.8.cloned.1.call-start = ((), (), s32[]{:S(2)}) async-start(), calls=%async_computation.8 | async-start | bytes 2433024 | tf_op jit(solution)/shard_map/while/body/eval_jaxpr/all_gather | solution.py:52
  231.1 63.6 %all-gather.8.cloned.1.call-start = ((), (), s32[]{:S(2)}) async-start(), calls=%async_computation.8 | async-start | bytes 2433024 | tf_op jit(solution)/shard_map/while/body/eval_jaxpr/all_gather | solution.py:52
  294.7 63.6 %all-gather.8.cloned.1.call-start = ((), (), s32[]{:S(2)}) async-start(), calls=%async_computation.8 | async-start | bytes 2433024 | tf_op jit(solution)/shard_map/while/body/eval_jaxpr/all_gather | solution.py:52
  358.3 79.6 %reduce-scatter.12.cloned.1.call-start = ((), (), s32[]{:S(2)}) async-start(), calls=%async_computation.7 | async-start | bytes 147456
  363.6 4.4 copy-start.1
  363.6 4.4 copy-start.4
  378.0 123.9 %reduce-scatter.10.cloned.1.call-start = ((), (), s32[]{:S(2)}) async-start(), calls=%async_computation.6 | async-start | bytes 294912
Sparse Core Ops, SparseCore 0:
  9.6 22.3 all-gather.3
  39.7 62.0 reduce-scatter.7
  105.1 56.3 all-gather.5
  174.9 56.1 all-gather.7
  238.5 56.1 all-gather.7
  302.1 56.1 all-gather.7
  378.1 59.7 reduce-scatter.11
  441.6 60.2 reduce-scatter.9
where the time goes:
time: 511 us; the launch traced here: 510 us
  waiting for transfers between devices  437 us (86%)
  matrix products  41.4 us (8%)
  between operations  14.9 us (3%)
  local copies, waits for them, and re-layouts  8.57 us (2%)
  other arithmetic  8.11 us (2%)
    all_gather x4, waiting for transfers between devices, gather_spread(): return lax.all_gather(rows, ('dp', 'dim'), axis=0, tiled=True)  229 us
    unnamed x7, waiting for transfers between devices  123 us
    reduce_scatter x1, waiting for transfers between devices, per_device(): lax.psum_scatter(cross_part, 'dp', scatter_dimension=0, tiled=True)  62.2 us
    all_gather x1, waiting for transfers between devices, per_device(): gathered_rows = lax.all_gather(vectors, 'dim', axis=0, tiled=True)  23.1 us
    dot_general x4, matrix products, newton_update(): gram_rows = jnp.dot(rows, whole.T, precision=lax.Precision.HIGHEST)  15.3 us
    dot_general x4, matrix products, newton_update(): jnp.dot(gram_rows, whole, precision=lax.Precision.HIGHEST)  15 us
  transfers between devices with their start and end apart: 8, of which 8 were waited for; matrix products, arithmetic and copies ran while one was open for 1% of the time, Pallas kernels for 0%

commit v1 on v0

v1 whole, which is shorter than its diff:
```python
import functools

import jax
import jax.numpy as jnp
from jax import lax
from jax.experimental import pallas as pl
from jax.experimental.pallas import tpu as pltpu
from jax.sharding import PartitionSpec as P

NS_STEPS = 4
DIMS = 4
LANES = 128
VMEM_LIMIT = 56 * 1024 * 1024


def swap(value, mask):
    count = lax.axis_size("dp") * lax.axis_size("dim")
    return lax.ppermute(value, ("dp", "dim"), [(i, i ^ mask) for i in range(count)])


def place():
    dim = lax.axis_index("dim")
    dp = lax.axis_index("dp")
    return dim & 1, dim >> 1, dp & 3, dp >> 2


def split(value):
    high = value.astype(jnp.bfloat16)
    low = (value - high.astype(jnp.float32)).astype(jnp.bfloat16)
    return high, low


def dot_t(a, b):
    return lax.dot_general(a, b, (((1,), (1,)), ((), ())), preferred_element_type=jnp.float32)


def dot(a, b):
    return jnp.dot(a, b, preferred_element_type=jnp.float32)


def decode(codes_ref, book_ref, sub_width, write):
    sub_count, row_count = codes_ref.shape
    width = sub_count * sub_width
    sublane = lax.broadcasted_iota(jnp.int32, (8, row_count), 0)
    for first in range(0, width, 8):
        one, two = first // sub_width, (first + 7) // sub_width
        index = jnp.broadcast_to(codes_ref[one : one + 1, :], (8, row_count))
        if two != one:
            later = jnp.broadcast_to(codes_ref[two : two + 1, :], (8, row_count))
            index = jnp.where(sublane < two * sub_width - first, index, later)
        book = book_ref[first : first + 8, :].astype(jnp.float32)
        parts = []
        for start in range(0, row_count, LANES):
            at = index[:, start : start + LANES]
            inner = at & (LANES - 1)
            value = jnp.take_along_axis(book[:, :LANES], inner, axis=1, mode="promise_in_bounds")
            for level in range(LANES, book.shape[1], LANES):
                other = jnp.take_along_axis(
                    book[:, level : level + LANES], inner, axis=1, mode="promise_in_bounds"
                )
                value = jnp.where(at >= level, other, value)
            parts.append(value)
        write(first, jnp.concatenate(parts, axis=1))


def cross_kernel(sub_width, v0, v1, code0, code1, book0, book1, *rest):
    outs, (vectors, decoded32) = rest[:4], rest[4:]
    core, pair, quarter, _ = place()
    width = v0.shape[0]
    vectors[pl.ds(pl.multiple_of(core * width, 16), width), :] = v0[...]
    vectors[pl.ds(pl.multiple_of((1 - core) * width, 16), width), :] = v1[...]

    def writer(base):
        def write(row, rows):
            decoded32[pl.ds(pl.multiple_of(base + row, 8), 8), :] = rows

        return write

    decode(code0, book0, sub_width, writer(pair * width))
    decode(code1, book1, sub_width, writer((1 - pair) * width))
    thin = width // 2
    for k, out in enumerate(outs):
        rows = decoded32[pl.ds(pl.multiple_of((quarter ^ k) * thin, 8), thin), :]
        out[...] = dot_t(rows.astype(jnp.bfloat16), vectors[...])


def refit_kernel(sub_width, *refs):
    pieces, (v0, v1, v2, v3, codes) = refs[:16], refs[16:21]
    rotation_out, outs = refs[21], refs[22:26]
    current, high_ref, low_ref, vectors, rotated, total = refs[26:]
    core, pair, quarter, high_part = place()
    dp_count = lax.axis_size("dp")
    thin, half = pieces[0].shape
    width = 2 * thin
    own = (pair * 2 + core) * width

    for mask, piece in enumerate(pieces):
        c, p, q = core ^ (mask & 1), pair ^ (mask >> 1 & 1), quarter ^ (mask >> 2)
        row = ((q >> 1) * 2 + c) * width + (q & 1) * thin
        current[p, pl.ds(pl.multiple_of(row, 8), thin), :] = piece[...]
    for k, v in enumerate((v0, v1, v2, v3)):
        at = ((pair ^ (k >> 1)) * 2 + (core ^ (k & 1))) * width
        vectors[pl.ds(pl.multiple_of(at, 16), width), :] = v[...]

    magnitude = jnp.sqrt(jnp.sum(current[...] * current[...]))
    current[...] = current[...] / magnitude

    def put_split():
        for side in range(2):
            high, low = split(current[side])
            high_ref[:, side * half : (side + 1) * half] = high
            low_ref[:, side * half : (side + 1) * half] = low

    def cubic(high_rows, low_rows):
        gram = dot_t(high_rows, high_ref[...]) + (
            dot_t(high_rows, low_ref[...]) + dot_t(low_rows, high_ref[...])
        )
        high, low = split(gram)
        return dot(high, high_ref[...]) + (dot(high, low_ref[...]) + dot(low, high_ref[...]))

    def step(iteration, carry):
        put_split()
        update = cubic(high_ref[...], low_ref[...])
        for side in range(2):
            current[side] = 1.5 * current[side] - 0.5 * update[:, side * half : (side + 1) * half]
        return carry

    lax.fori_loop(0, NS_STEPS - 1, step, 0)
    put_split()
    rows = pl.ds(pl.multiple_of(own, 16), width)
    update = cubic(high_ref[rows, :], low_ref[rows, :])
    for side in range(2):
        rotation_out[:, side * half : (side + 1) * half] = (
            1.5 * current[side, rows, :] - 0.5 * update[:, side * half : (side + 1) * half]
        )

    sub_count, row_count = codes.shape
    rotated[:width, :] = dot(rotation_out[...].astype(jnp.bfloat16), vectors[...]).astype(jnp.bfloat16)
    rotated[width:, :] = jnp.ones((rotated.shape[0] - width, row_count), jnp.bfloat16)

    centroid_count = total.shape[0]
    row = lax.broadcasted_iota(jnp.int32, (centroid_count, row_count), 0)
    owner_rows = centroid_count // dp_count
    quarter_rows = centroid_count // 4
    position = row // quarter_rows
    inner = row % quarter_rows
    level = (((inner // owner_rows) ^ high_part) * 4 + (position ^ quarter)) * owner_rows + inner % owner_rows
    column = lax.broadcasted_iota(jnp.int32, total.shape, 1)
    subspace = jnp.where(column < width, column // sub_width, column - width)
    total[...] = jnp.zeros(total.shape, jnp.float32)
    for m in range(sub_count):
        onehot = (codes[m : m + 1, :] == level).astype(jnp.float32).astype(jnp.bfloat16)
        total[...] = jnp.where(subspace == m, dot_t(onehot, rotated[...]), total[...])
    for k, out in enumerate(outs):
        out[...] = total[k * quarter_rows : (k + 1) * quarter_rows, :]


def finish_kernel(sub_width, kept, received, out):
    total = kept[...] + received[...]
    width = out.shape[1]
    row = lax.broadcasted_iota(jnp.int32, (total.shape[1], width), 0)
    column = lax.broadcasted_iota(jnp.int32, (total.shape[1], width), 1)
    spread = (row == width + column // sub_width).astype(jnp.float32)
    counts = jnp.dot(total, spread, precision=lax.Precision.HIGHEST)
    out[...] = total[:, :width] / jnp.maximum(counts, 1.0)


def call(kernel, outs, scratch, *args):
    return pl.pallas_call(
        kernel,
        out_shape=[jax.ShapeDtypeStruct(s, jnp.float32) for s in outs],
        in_specs=[pl.BlockSpec(memory_space=pltpu.VMEM)] * len(args),
        out_specs=[pl.BlockSpec(memory_space=pltpu.VMEM)] * len(outs),
        scratch_shapes=scratch,
        compiler_params=pltpu.CompilerParams(vmem_limit_bytes=VMEM_LIMIT),
    )(*args)


def per_device(vectors, codes, codebook):
    width, row_count = vectors.shape
    sub_count = codes.shape[0]
    sub_width = width // sub_count
    centroid_count = codebook.shape[0]
    dp_count = lax.axis_size("dp")
    total_width = width * DIMS
    half, thin = 2 * width, width // 2
    high_masks = [4 << bit for bit in range(2, dp_count.bit_length() - 1)]

    book = codebook.T
    book_other, codes_other = swap(book, 2), swap(codes, 2)
    vectors_core = swap(vectors, 1)
    parts = call(
        functools.partial(cross_kernel, sub_width),
        [(thin, half)] * 4,
        [pltpu.VMEM((half, row_count), jnp.bfloat16), pltpu.VMEM((half, row_count), jnp.float32)],
        vectors, vectors_core, codes, codes_other, book, book_other,
    )
    held, vectors_late = lax.optimization_barrier((parts, vectors))
    vectors_pair = swap(vectors_late, 2)
    vectors_last = swap(vectors_pair, 1)

    piece = held[0] + swap(held[1], 4) + swap(held[2], 8) + swap(held[3], 12)
    for mask in high_masks:
        piece = piece + swap(piece, mask)
    pieces = [piece if mask == 0 else swap(piece, mask) for mask in range(0, 16, 2)]
    both = []
    for own in pieces:
        both += [own, swap(own, 1)]

    columns = width + sub_count
    columns += -columns % LANES
    rotation, *sums = call(
        functools.partial(refit_kernel, sub_width),
        [(width, total_width)] + [(centroid_count // 4, columns)] * 4,
        [
            pltpu.VMEM((2, total_width, half), jnp.float32),
            pltpu.VMEM((total_width, total_width), jnp.bfloat16),
            pltpu.VMEM((total_width, total_width), jnp.bfloat16),
            pltpu.VMEM((total_width, row_count), jnp.bfloat16),
            pltpu.VMEM((columns, row_count), jnp.bfloat16),
            pltpu.VMEM((centroid_count, columns), jnp.float32),
        ],
        *both, vectors, vectors_core, vectors_pair, vectors_last, codes,
    )
    held = sums[0] + swap(sums[1], 4) + swap(sums[2], 8) + swap(sums[3], 12)
    received = jnp.zeros_like(held)
    for step, mask in enumerate(reversed(high_masks)):
        if step:
            held = held + received
        middle = held.shape[0] // 2
        held, received = held[:middle], swap(held[middle:], mask)
    (new_codebook,) = call(
        functools.partial(finish_kernel, sub_width),
        [(centroid_count // dp_count, width)],
        [],
        held, received,
    )
    return rotation, new_codebook


def solution(mesh):
    placed = (P("dim", "dp"), P("dim", "dp"), P(None, "dim"))
    return jax.shard_map(
        per_device,
        mesh=mesh,
        in_specs=placed,
        out_specs=(P("dim", None), P("dp", "dim")),
        check_vma=False,
    )
```

time: 511 us -> 114 us (0.22)
  waiting for transfers between devices: 437 us -> 32.5 us
  Pallas kernels: 0 us -> 47.9 us
  matrix products: 41.4 us -> 0 us
  starting transfers between devices: 0.17 us -> 27.2 us
  between operations: 14.9 us -> 0.82 us
  other arithmetic: 8.11 us -> 1.82 us
    all_gather x5 -> x0, waiting for transfers between devices: 252 us -> none  [the longest x4 229 us: gather_spread(): return lax.all_gather(rows, ('dp', 'dim'), axis=0, tiled=True)]
    unnamed x7 -> x0, waiting for transfers between devices: 123 us -> none
    reduce_scatter x1 -> x0, waiting for transfers between devices: 62.2 us -> none  [per_device(): lax.psum_scatter(cross_part, 'dp', scatter_dimension=0, tiled=True)]
    pallas_call x0 -> x3, Pallas kernels: none -> 47.9 us  [call(): pl.pallas_call(kernel, out_shape=[jax.ShapeDtypeStruct(s, jnp.float32) fo...]
    dot_general x16 -> x0, matrix products: 41.4 us -> none  [the longest x4 15.3 us: newton_update(): gram_rows = jnp.dot(rows, whole.T, precision=lax.Precision.HIGHEST)]
    ppermute x0 -> x28, waiting for transfers between devices: none -> 32.5 us  [swap(): lax.ppermute(value, ('dp', 'dim'), [(i, i ^ mask) for i in range(count)])]
    ppermute x0 -> x28, starting transfers between devices: none -> 27.2 us  [swap(): lax.ppermute(value, ('dp', 'dim'), [(i, i ^ mask) for i in range(count)])]
    reduce_sum x3 -> x0, other arithmetic: 5.85 us -> none  [the longest x1 3.02 us: per_device(): magnitude = jnp.sqrt(jnp.sum(gathered * gathered))]
  transfers between devices with their start and end apart: 8 -> 28, of which waited for: 8 -> 19; matrix products, arithmetic and copies ran while one was open for 1% -> 1% of each run, Pallas kernels for 0% -> 0%
where the time goes in v1:
time: 114 us
  Pallas kernels  47.9 us (42%)
  waiting for transfers between devices  32.5 us (29%)
  starting transfers between devices  27.2 us (24%)
  local copies, waits for them, and re-layouts  3.94 us (3%)
  other arithmetic  1.82 us (2%)
    pallas_call x3, Pallas kernels, call(): pl.pallas_call(kernel, out_shape=[jax.ShapeDtypeStruct(s, jnp.float32) fo...  47.9 us
    ppermute x28, waiting for transfers between devices, swap(): lax.ppermute(value, ('dp', 'dim'), [(i, i ^ mask) for i in range(count)])  32.5 us
    ppermute x28, starting transfers between devices, swap(): lax.ppermute(value, ('dp', 'dim'), [(i, i ^ mask) for i in range(count)])  27.2 us
    unnamed x46, local copies, waits for them, and re-layouts  3.33 us
  transfers between devices with their start and end apart: 28, of which 19 were waited for; matrix products, arithmetic and copies ran while one was open for 1% of the time, Pallas kernels for 0%

profile of v1, /device:TPU:0, one launch (start us, length us, event | category | flops | bytes accessed | tf_op | source)
XLA Modules:
  0.0 114.2 jit_solution(3644132894882753208)
XLA Ops:
  1.1 2.6 %collective-permute-start.2 = (bf16[192,256]{1,0:T(8,128)(2,1)}, bf16[192,256]{1,0:T(8,128)(2,1)S(1)}, u32[]{:S(2)}, u32[]{:S(2)}) collective-permute-start(bf16[192,256]{1,0:T(8,128)(2,1)} %bitcast.1), channel_id=1, source_target_pairs={{0,2},{1,3},{2,0},{3,1},{4,6},{5,7},{6,4},{7,5},{8,10},{9,11},{10,... | collective-permute-start | bytes 294920 | tf_op jit(solution)/shard_map/ppermute | solution.py:18
  3.8 4.9 %collective-permute-done.1.code1 = s32[16,1024]{1,0:T(8,128)S(1)} collective-permute-done((s32[16,1024]{1,0:T(8,128)}, s32[16,1024]{1,0:T(8,128)S(1)}, u32[]{:S(2)}, u32[]{:S(2)}) %collective-permute-start.1) | collective-permute-done | bytes 65568 | tf_op jit(solution)/shard_map/ppermute | solution.py:18
  10.2 3.9 %shard_map.50 = (f32[96,384]{1,0:T(8,128)}, f32[96,384]{1,0:T(8,128)}, f32[96,384]{1,0:T(8,128)}, f32[96,384]{1,0:T(8,128)}) custom-call(bf16[192,1024]{1,0:T(8,128)(2,1)} %refs_16_.1, bf16[192,1024]{1,0:T(8,128)(2,1)} %copy-done.1, s32[16,1024]{1,0:T(8,128)} %refs_20_.1, s32[16,1024]{1,0:T(8,128)} %copy-done.21, bf16[192,256]{1,0:T(8,128)(2,1)} %bitcast.2, ...), custom_call_target="tpu_custom_call" | custom-call | tf_op jit(solution)/shard_map/pallas_call | solution.py:169
  14.1 1.7 %collective-permute-start.3 = (f32[96,384]{1,0:T(8,128)}, f32[96,384]{1,0:T(8,128)S(1)}, u32[]{:S(2)}, u32[]{:S(2)}) collective-permute-start(f32[96,384]{1,0:T(8,128)} %get-tuple-element.21), channel_id=1, source_target_pairs={{0,4},{1,5},{2,6},{3,7},{4,0},{5,1},{6,2},{7,3},{8,12},{9,13},{10,... | collective-permute-start | bytes 442376 | tf_op jit(solution)/shard_map/ppermute | solution.py:18
  15.8 1.6 %collective-permute-start.4 = (f32[96,384]{1,0:T(8,128)}, f32[96,384]{1,0:T(8,128)S(1)}, u32[]{:S(2)}, u32[]{:S(2)}) collective-permute-start(f32[96,384]{1,0:T(8,128)} %get-tuple-element.22), channel_id=1, source_target_pairs={{0,8},{1,9},{2,10},{3,11},{4,12},{5,13},{6,14},{7,15},{8,0},{9,1},... | collective-permute-start | bytes 442376 | tf_op jit(solution)/shard_map/ppermute | solution.py:18
  17.6 1.8 %collective-permute-start.22 = (bf16[192,1024]{1,0:T(8,128)(2,1)S(1)}, bf16[192,1024]{1,0:T(8,128)(2,1)S(1)}, u32[]{:S(2)}, u32[]{:S(2)}) collective-permute-start(bf16[192,1024]{1,0:T(8,128)(2,1)S(1)} %copy-done), channel_id=1, source_target_pairs={{0,2},{1,3},{2,0},{3,1},{4,6},{5,7},{6,4},{7,5},{8,10},{9,11},{10,... | collective-permute-start | bytes 1179656 | tf_op jit(solution)/shard_map/ppermute | solution.py:18
  20.0 2.8 %collective-permute-done.4 = f32[96,384]{1,0:T(8,128)S(1)} collective-permute-done((f32[96,384]{1,0:T(8,128)}, f32[96,384]{1,0:T(8,128)S(1)}, u32[]{:S(2)}, u32[]{:S(2)}) %collective-permute-start.4) | collective-permute-done | bytes 147488 | tf_op jit(solution)/shard_map/ppermute | solution.py:18
  22.8 1.5 %collective-permute-done.5 = f32[96,384]{1,0:T(8,128)S(1)} collective-permute-done((f32[96,384]{1,0:T(8,128)}, f32[96,384]{1,0:T(8,128)S(1)}, u32[]{:S(2)}, u32[]{:S(2)}) %collective-permute-start.5) | collective-permute-done | bytes 147488 | tf_op jit(solution)/shard_map/ppermute | solution.py:18
  25.2 2.7 %collective-permute-start.6 = (f32[96,384]{1,0:T(8,128)S(1)}, f32[96,384]{1,0:T(8,128)S(1)}, u32[]{:S(2)}, u32[]{:S(2)}) collective-permute-start(f32[96,384]{1,0:T(8,128)S(1)} %add_add_fusion), channel_id=1, source_target_pairs={{0,16},{1,17},{2,18},{3,19},{4,20},{5,21},{6,22},{7,23},{8,24},{9,... | collective-permute-start | bytes 442376 | tf_op jit(solution)/shard_map/ppermute | solution.py:18
  27.9 6.3 %collective-permute-done.6 = f32[96,384]{1,0:T(8,128)S(1)} collective-permute-done((f32[96,384]{1,0:T(8,128)S(1)}, f32[96,384]{1,0:T(8,128)S(1)}, u32[]{:S(2)}, u32[]{:S(2)}) %collective-permute-start.6) | collective-permute-done | bytes 147488 | tf_op jit(solution)/shard_map/ppermute | solution.py:18
  34.3 1.7 %collective-permute-start.20 = (f32[96,384]{1,0:T(8,128)S(1)}, f32[96,384]{1,0:T(8,128)S(1)}, u32[]{:S(2)}, u32[]{:S(2)}) collective-permute-start(f32[96,384]{1,0:T(8,128)S(1)} %add.24.refs_0_), channel_id=1, source_target_pairs={{0,14},{1,15},{2,12},{3,13},{4,10},{5,11},{6,8},{7,9},{8,6},{9,7},... | collective-permute-start | bytes 442376 | tf_op jit(solution)/shard_map/ppermute | solution.py:18
  36.0 2.2 %collective-permute-start.18 = (f32[96,384]{1,0:T(8,128)S(1)}, f32[96,384]{1,0:T(8,128)S(1)}, u32[]{:S(2)}, u32[]{:S(2)}) collective-permute-start(f32[96,384]{1,0:T(8,128)S(1)} %add.24.refs_0_), channel_id=1, source_target_pairs={{0,12},{1,13},{2,14},{3,15},{4,8},{5,9},{6,10},{7,11},{8,4},{9,5},... | collective-permute-start | bytes 442376 | tf_op jit(solution)/shard_map/ppermute | solution.py:18
  38.3 1.9 %collective-permute-start.14 = (f32[96,384]{1,0:T(8,128)S(1)}, f32[96,384]{1,0:T(8,128)S(1)}, u32[]{:S(2)}, u32[]{:S(2)}) collective-permute-start(f32[96,384]{1,0:T(8,128)S(1)} %add.24.refs_0_), channel_id=1, source_target_pairs={{0,8},{1,9},{2,10},{3,11},{4,12},{5,13},{6,14},{7,15},{8,0},{9,1},... | collective-permute-start | bytes 442376 | tf_op jit(solution)/shard_map/ppermute | solution.py:18
  40.2 1.6 %collective-permute-start.12 = (f32[96,384]{1,0:T(8,128)S(1)}, f32[96,384]{1,0:T(8,128)S(1)}, u32[]{:S(2)}, u32[]{:S(2)}) collective-permute-start(f32[96,384]{1,0:T(8,128)S(1)} %add.24.refs_0_), channel_id=1, source_target_pairs={{0,6},{1,7},{2,4},{3,5},{4,2},{5,3},{6,0},{7,1},{8,14},{9,15},{10,... | collective-permute-start | bytes 442376 | tf_op jit(solution)/shard_map/ppermute | solution.py:18
  43.2 2.9 %collective-permute-done.18.refs_12_ = f32[96,384]{1,0:T(8,128)S(1)} collective-permute-done((f32[96,384]{1,0:T(8,128)S(1)}, f32[96,384]{1,0:T(8,128)S(1)}, u32[]{:S(2)}, u32[]{:S(2)}) %collective-permute-start.18) | collective-permute-done | bytes 147488 | tf_op jit(solution)/shard_map/ppermute | solution.py:18
  46.6 2.0 %collective-permute-done.14.refs_8_ = f32[96,384]{1,0:T(8,128)S(1)} collective-permute-done((f32[96,384]{1,0:T(8,128)S(1)}, f32[96,384]{1,0:T(8,128)S(1)}, u32[]{:S(2)}, u32[]{:S(2)}) %collective-permute-start.14) | collective-permute-done | bytes 147488 | tf_op jit(solution)/shard_map/ppermute | solution.py:18
  49.2 2.6 %collective-permute-done.10.refs_4_ = f32[96,384]{1,0:T(8,128)S(1)} collective-permute-done((f32[96,384]{1,0:T(8,128)S(1)}, f32[96,384]{1,0:T(8,128)S(1)}, u32[]{:S(2)}, u32[]{:S(2)}) %collective-permute-start.10) | collective-permute-done | bytes 147488 | tf_op jit(solution)/shard_map/ppermute | solution.py:18
  56.1 42.3 %shard_map.51 = (f32[192,768]{1,0:T(8,128)}, f32[64,256]{1,0:T(8,128)}, f32[64,256]{1,0:T(8,128)}, f32[64,256]{1,0:T(8,128)}, f32[64,256]{1,0:T(8,128)}) custom-call(f32[96,384]{1,0:T(8,128)} %copy-done.2, f32[96,384]{1,0:T(8,128)} %copy-done.12, f32[96,384]{1,0:T(8,128)} %copy-done.11, f32[96,384]{1,0:T(8,128)} %copy-done.19, f32[96,384]{1,0:T(8,128)} %copy-done.10, ...), custom_call_target="tpu_custom_call" | custom-call | tf_op jit(solution)/shard_map/pallas_call | solution.py:169
  100.2 1.8 %collective-permute-start.26 = (f32[64,256]{1,0:T(8,128)}, f32[64,256]{1,0:T(8,128)S(1)}, u32[]{:S(2)}, u32[]{:S(2)}) collective-permute-start(f32[64,256]{1,0:T(8,128)} %get-tuple-element.29), channel_id=1, source_target_pairs={{0,12},{1,13},{2,14},{3,15},{4,8},{5,9},{6,10},{7,11},{8,4},{9,5},... | collective-permute-start | bytes 196616 | tf_op jit(solution)/shard_map/ppermute | solution.py:18
  103.1 1.4 %collective-permute-done.25 = f32[64,256]{1,0:T(8,128)S(1)} collective-permute-done((f32[64,256]{1,0:T(8,128)}, f32[64,256]{1,0:T(8,128)S(1)}, u32[]{:S(2)}, u32[]{:S(2)}) %collective-permute-start.25) | collective-permute-done | bytes 65568 | tf_op jit(solution)/shard_map/ppermute | solution.py:18
  104.5 1.2 %collective-permute-done.26 = f32[64,256]{1,0:T(8,128)S(1)} collective-permute-done((f32[64,256]{1,0:T(8,128)}, f32[64,256]{1,0:T(8,128)S(1)}, u32[]{:S(2)}, u32[]{:S(2)}) %collective-permute-start.26) | collective-permute-done | bytes 65568 | tf_op jit(solution)/shard_map/ppermute | solution.py:18
  107.1 2.4 %collective-permute-start.27 = (f32[32,256]{1,0:T(8,128)S(1)}, f32[32,256]{1,0:T(8,128)S(1)}, u32[]{:S(2)}, u32[]{:S(2)}) collective-permute-start(f32[32,256]{1,0:T(8,128)S(1)} %get-tuple-element.30), channel_id=1, source_target_pairs={{0,16},{1,17},{2,18},{3,19},{4,20},{5,21},{6,22},{7,23},{8,24},{9,... | collective-permute-start | bytes 98312 | tf_op jit(solution)/shard_map/ppermute | solution.py:18
  109.6 2.4 %collective-permute-done.27.received = f32[32,256]{1,0:T(8,128)S(1)} collective-permute-done((f32[32,256]{1,0:T(8,128)S(1)}, f32[32,256]{1,0:T(8,128)S(1)}, u32[]{:S(2)}, u32[]{:S(2)}) %collective-permute-start.27) | collective-permute-done | bytes 32800 | tf_op jit(solution)/shard_map/ppermute | solution.py:18
  112.5 1.7 %shard_map.52 = f32[32,192]{1,0:T(8,128)} custom-call(f32[32,256]{1,0:T(8,128)} %get-tuple-element.31.kept, f32[32,256]{1,0:T(8,128)} %copy-done.22), custom_call_target="tpu_custom_call" | custom-call | tf_op jit(solution)/shard_map/pallas_call | solution.py:169
  (85 shorter events, 15.3 us)
Async XLA Ops:
  0.6 8.1 %collective-permute-start = (bf16[192,1024]{1,0:T(8,128)(2,1)}, bf16[192,1024]{1,0:T(8,128)(2,1)S(1)}, u32[]{:S(2)}, u32[]{:S(2)}) collective-permute-start(bf16[192,1024]{1,0:T(8,128)(2,1)} %refs_16_.1), channel_id=1, source_target_pairs={{0,1},{1,0},{2,3},{3,2},{4,5},{5,4},{6,7},{7,6},{8,9},{9,8},{10,11... | collective-permute-start | bytes 1179656 | tf_op jit(solution)/shard_map/ppermute | solution.py:18
  1.1 7.6 %collective-permute-start.2 = (bf16[192,256]{1,0:T(8,128)(2,1)}, bf16[192,256]{1,0:T(8,128)(2,1)S(1)}, u32[]{:S(2)}, u32[]{:S(2)}) collective-permute-start(bf16[192,256]{1,0:T(8,128)(2,1)} %bitcast.1), channel_id=1, source_target_pairs={{0,2},{1,3},{2,0},{3,1},{4,6},{5,7},{6,4},{7,5},{8,10},{9,11},{10,... | collective-permute-start | bytes 294920 | tf_op jit(solution)/shard_map/ppermute | solution.py:18
  3.8 5.0 %collective-permute-start.1 = (s32[16,1024]{1,0:T(8,128)}, s32[16,1024]{1,0:T(8,128)S(1)}, u32[]{:S(2)}, u32[]{:S(2)}) collective-permute-start(s32[16,1024]{1,0:T(8,128)} %refs_20_.1), channel_id=1, source_target_pairs={{0,2},{1,3},{2,0},{3,1},{4,6},{5,7},{6,4},{7,5},{8,10},{9,11},{10,... | collective-permute-start | bytes 196616 | tf_op jit(solution)/shard_map/ppermute | solution.py:18
  14.1 5.9 %collective-permute-start.3 = (f32[96,384]{1,0:T(8,128)}, f32[96,384]{1,0:T(8,128)S(1)}, u32[]{:S(2)}, u32[]{:S(2)}) collective-permute-start(f32[96,384]{1,0:T(8,128)} %get-tuple-element.21), channel_id=1, source_target_pairs={{0,4},{1,5},{2,6},{3,7},{4,0},{5,1},{6,2},{7,3},{8,12},{9,13},{10,... | collective-permute-start | bytes 442376 | tf_op jit(solution)/shard_map/ppermute | solution.py:18
  15.8 7.0 %collective-permute-start.4 = (f32[96,384]{1,0:T(8,128)}, f32[96,384]{1,0:T(8,128)S(1)}, u32[]{:S(2)}, u32[]{:S(2)}) collective-permute-start(f32[96,384]{1,0:T(8,128)} %get-tuple-element.22), channel_id=1, source_target_pairs={{0,8},{1,9},{2,10},{3,11},{4,12},{5,13},{6,14},{7,15},{8,0},{9,1},... | collective-permute-start | bytes 442376 | tf_op jit(solution)/shard_map/ppermute | solution.py:18
  17.4 6.9 %collective-permute-start.5 = (f32[96,384]{1,0:T(8,128)}, f32[96,384]{1,0:T(8,128)S(1)}, u32[]{:S(2)}, u32[]{:S(2)}) collective-permute-start(f32[96,384]{1,0:T(8,128)} %get-tuple-element.23), channel_id=1, source_target_pairs={{0,12},{1,13},{2,14},{3,15},{4,8},{5,9},{6,10},{7,11},{8,4},{9,5},... | collective-permute-start | bytes 442376 | tf_op jit(solution)/shard_map/ppermute | solution.py:18
  17.6 22.6 %collective-permute-start.22 = (bf16[192,1024]{1,0:T(8,128)(2,1)S(1)}, bf16[192,1024]{1,0:T(8,128)(2,1)S(1)}, u32[]{:S(2)}, u32[]{:S(2)}) collective-permute-start(bf16[192,1024]{1,0:T(8,128)(2,1)S(1)} %copy-done), channel_id=1, source_target_pairs={{0,2},{1,3},{2,0},{3,1},{4,6},{5,7},{6,4},{7,5},{8,10},{9,11},{10,... | collective-permute-start | bytes 1179656 | tf_op jit(solution)/shard_map/ppermute | solution.py:18
  25.2 9.0 %collective-permute-start.6 = (f32[96,384]{1,0:T(8,128)S(1)}, f32[96,384]{1,0:T(8,128)S(1)}, u32[]{:S(2)}, u32[]{:S(2)}) collective-permute-start(f32[96,384]{1,0:T(8,128)S(1)} %add_add_fusion), channel_id=1, source_target_pairs={{0,16},{1,17},{2,18},{3,19},{4,20},{5,21},{6,22},{7,23},{8,24},{9,... | collective-permute-start | bytes 442376 | tf_op jit(solution)/shard_map/ppermute | solution.py:18
  34.3 8.7 %collective-permute-start.20 = (f32[96,384]{1,0:T(8,128)S(1)}, f32[96,384]{1,0:T(8,128)S(1)}, u32[]{:S(2)}, u32[]{:S(2)}) collective-permute-start(f32[96,384]{1,0:T(8,128)S(1)} %add.24.refs_0_), channel_id=1, source_target_pairs={{0,14},{1,15},{2,12},{3,13},{4,10},{5,11},{6,8},{7,9},{8,6},{9,7},... | collective-permute-start | bytes 442376 | tf_op jit(solution)/shard_map/ppermute | solution.py:18
  36.0 10.1 %collective-permute-start.18 = (f32[96,384]{1,0:T(8,128)S(1)}, f32[96,384]{1,0:T(8,128)S(1)}, u32[]{:S(2)}, u32[]{:S(2)}) collective-permute-start(f32[96,384]{1,0:T(8,128)S(1)} %add.24.refs_0_), channel_id=1, source_target_pairs={{0,12},{1,13},{2,14},{3,15},{4,8},{5,9},{6,10},{7,11},{8,4},{9,5},... | collective-permute-start | bytes 442376 | tf_op jit(solution)/shard_map/ppermute | solution.py:18
  38.3 8.4 %collective-permute-start.16 = (f32[96,384]{1,0:T(8,128)S(1)}, f32[96,384]{1,0:T(8,128)S(1)}, u32[]{:S(2)}, u32[]{:S(2)}) collective-permute-start(f32[96,384]{1,0:T(8,128)S(1)} %add.24.refs_0_), channel_id=1, source_target_pairs={{0,10},{1,11},{2,8},{3,9},{4,14},{5,15},{6,12},{7,13},{8,2},{9,3},... | collective-permute-start | bytes 442376 | tf_op jit(solution)/shard_map/ppermute | solution.py:18
  38.3 10.4 %collective-permute-start.14 = (f32[96,384]{1,0:T(8,128)S(1)}, f32[96,384]{1,0:T(8,128)S(1)}, u32[]{:S(2)}, u32[]{:S(2)}) collective-permute-start(f32[96,384]{1,0:T(8,128)S(1)} %add.24.refs_0_), channel_id=1, source_target_pairs={{0,8},{1,9},{2,10},{3,11},{4,12},{5,13},{6,14},{7,15},{8,0},{9,1},... | collective-permute-start | bytes 442376 | tf_op jit(solution)/shard_map/ppermute | solution.py:18
  40.2 8.6 %collective-permute-start.12 = (f32[96,384]{1,0:T(8,128)S(1)}, f32[96,384]{1,0:T(8,128)S(1)}, u32[]{:S(2)}, u32[]{:S(2)}) collective-permute-start(f32[96,384]{1,0:T(8,128)S(1)} %add.24.refs_0_), channel_id=1, source_target_pairs={{0,6},{1,7},{2,4},{3,5},{4,2},{5,3},{6,0},{7,1},{8,14},{9,15},{10,... | collective-permute-start | bytes 442376 | tf_op jit(solution)/shard_map/ppermute | solution.py:18
  43.0 8.8 %collective-permute-start.10 = (f32[96,384]{1,0:T(8,128)S(1)}, f32[96,384]{1,0:T(8,128)S(1)}, u32[]{:S(2)}, u32[]{:S(2)}) collective-permute-start(f32[96,384]{1,0:T(8,128)S(1)} %add.24.refs_0_), channel_id=1, source_target_pairs={{0,4},{1,5},{2,6},{3,7},{4,0},{5,1},{6,2},{7,3},{8,12},{9,13},{10,... | collective-permute-start | bytes 442376 | tf_op jit(solution)/shard_map/ppermute | solution.py:18
  46.1 5.6 %collective-permute-start.8 = (f32[96,384]{1,0:T(8,128)S(1)}, f32[96,384]{1,0:T(8,128)S(1)}, u32[]{:S(2)}, u32[]{:S(2)}) collective-permute-start(f32[96,384]{1,0:T(8,128)S(1)} %add.24.refs_0_), channel_id=1, source_target_pairs={{0,2},{1,3},{2,0},{3,1},{4,6},{5,7},{6,4},{7,5},{8,10},{9,11},{10,... | collective-permute-start | bytes 442376 | tf_op jit(solution)/shard_map/ppermute | solution.py:18
  46.6 8.1 %collective-permute-start.23 = (bf16[192,1024]{1,0:T(8,128)(2,1)S(1)}, bf16[192,1024]{1,0:T(8,128)(2,1)S(1)}, u32[]{:S(2)}, u32[]{:S(2)}) collective-permute-start(bf16[192,1024]{1,0:T(8,128)(2,1)S(1)} %collective-permute-done.22.refs_18_), channel_id=1, source_target_pairs={{0,1},{1,0},{2,3},{3,2},{4,5},{5,4},{6,7},{7,6},{8,9},{9,8},{10,11... | collective-permute-start | bytes 1179656 | tf_op jit(solution)/shard_map/ppermute | solution.py:18
  48.6 3.7 %collective-permute-start.7 = (f32[96,384]{1,0:T(8,128)S(1)}, f32[96,384]{1,0:T(8,128)S(1)}, u32[]{:S(2)}, u32[]{:S(2)}) collective-permute-start(f32[96,384]{1,0:T(8,128)S(1)} %add.24.refs_0_), channel_id=1, source_target_pairs={{0,1},{1,0},{2,3},{3,2},{4,5},{5,4},{6,7},{7,6},{8,9},{9,8},{10,11... | collective-permute-start | bytes 442376 | tf_op jit(solution)/shard_map/ppermute | solution.py:18
  48.8 3.6 %collective-permute-start.21 = (f32[96,384]{1,0:T(8,128)S(1)}, f32[96,384]{1,0:T(8,128)S(1)}, u32[]{:S(2)}, u32[]{:S(2)}) collective-permute-start(f32[96,384]{1,0:T(8,128)S(1)} %collective-permute-done.20.refs_14_), channel_id=1, source_target_pairs={{0,1},{1,0},{2,3},{3,2},{4,5},{5,4},{6,7},{7,6},{8,9},{9,8},{10,11... | collective-permute-start | bytes 442376 | tf_op jit(solution)/shard_map/ppermute | solution.py:18
  51.8 1.6 %collective-permute-start.17 = (f32[96,384]{1,0:T(8,128)S(1)}, f32[96,384]{1,0:T(8,128)S(1)}, u32[]{:S(2)}, u32[]{:S(2)}) collective-permute-start(f32[96,384]{1,0:T(8,128)S(1)} %collective-permute-done.16.refs_10_), channel_id=1, source_target_pairs={{0,1},{1,0},{2,3},{3,2},{4,5},{5,4},{6,7},{7,6},{8,9},{9,8},{10,11... | collective-permute-start | bytes 442376 | tf_op jit(solution)/shard_map/ppermute | solution.py:18
  52.4 1.5 %collective-permute-start.13 = (f32[96,384]{1,0:T(8,128)S(1)}, f32[96,384]{1,0:T(8,128)S(1)}, u32[]{:S(2)}, u32[]{:S(2)}) collective-permute-start(f32[96,384]{1,0:T(8,128)S(1)} %collective-permute-done.12.refs_6_), channel_id=1, source_target_pairs={{0,1},{1,0},{2,3},{3,2},{4,5},{5,4},{6,7},{7,6},{8,9},{9,8},{10,11... | collective-permute-start | bytes 442376 | tf_op jit(solution)/shard_map/ppermute | solution.py:18
  98.5 4.6 %collective-permute-start.24 = (f32[64,256]{1,0:T(8,128)}, f32[64,256]{1,0:T(8,128)S(1)}, u32[]{:S(2)}, u32[]{:S(2)}) collective-permute-start(f32[64,256]{1,0:T(8,128)} %get-tuple-element.27), channel_id=1, source_target_pairs={{0,4},{1,5},{2,6},{3,7},{4,0},{5,1},{6,2},{7,3},{8,12},{9,13},{10,... | collective-permute-start | bytes 196616 | tf_op jit(solution)/shard_map/ppermute | solution.py:18
  99.6 4.8 %collective-permute-start.25 = (f32[64,256]{1,0:T(8,128)}, f32[64,256]{1,0:T(8,128)S(1)}, u32[]{:S(2)}, u32[]{:S(2)}) collective-permute-start(f32[64,256]{1,0:T(8,128)} %get-tuple-element.28), channel_id=1, source_target_pairs={{0,8},{1,9},{2,10},{3,11},{4,12},{5,13},{6,14},{7,15},{8,0},{9,1},... | collective-permute-start | bytes 196616 | tf_op jit(solution)/shard_map/ppermute | solution.py:18
  100.2 5.4 %collective-permute-start.26 = (f32[64,256]{1,0:T(8,128)}, f32[64,256]{1,0:T(8,128)S(1)}, u32[]{:S(2)}, u32[]{:S(2)}) collective-permute-start(f32[64,256]{1,0:T(8,128)} %get-tuple-element.29), channel_id=1, source_target_pairs={{0,12},{1,13},{2,14},{3,15},{4,8},{5,9},{6,10},{7,11},{8,4},{9,5},... | collective-permute-start | bytes 196616 | tf_op jit(solution)/shard_map/ppermute | solution.py:18
  107.1 4.8 %collective-permute-start.27 = (f32[32,256]{1,0:T(8,128)S(1)}, f32[32,256]{1,0:T(8,128)S(1)}, u32[]{:S(2)}, u32[]{:S(2)}) collective-permute-start(f32[32,256]{1,0:T(8,128)S(1)} %get-tuple-element.30), channel_id=1, source_target_pairs={{0,16},{1,17},{2,18},{3,19},{4,20},{5,21},{6,22},{7,23},{8,24},{9,... | collective-permute-start | bytes 98312 | tf_op jit(solution)/shard_map/ppermute | solution.py:18
  (27 other events, 118.8 us)

commit v2 on v1

v2 whole, which is shorter than its diff:
```python
import functools

import jax
import jax.numpy as jnp
from jax import lax
from jax.experimental import pallas as pl
from jax.experimental.pallas import tpu as pltpu
from jax.sharding import PartitionSpec as P

NS_STEPS = 4
DIMS = 4
LANES = 128
VMEM_LIMIT = 56 * 1024 * 1024


def swap(value, mask):
    count = lax.axis_size("dp") * lax.axis_size("dim")
    return lax.ppermute(value, ("dp", "dim"), [(i, i ^ mask) for i in range(count)])


def place():
    dim = lax.axis_index("dim")
    dp = lax.axis_index("dp")
    return dim & 1, dim >> 1, dp & 3, dp >> 2


def split(value):
    high = value.astype(jnp.bfloat16)
    low = (value - high.astype(jnp.float32)).astype(jnp.bfloat16)
    return high, low


def dot_t(a, b):
    return lax.dot_general(a, b, (((1,), (1,)), ((), ())), preferred_element_type=jnp.float32)


def dot(a, b):
    return jnp.dot(a, b, preferred_element_type=jnp.float32)


def decode(codes_ref, book_ref, sub_width, write):
    sub_count, row_count = codes_ref.shape
    width = sub_count * sub_width
    sublane = lax.broadcasted_iota(jnp.int32, (8, row_count), 0)
    for first in range(0, width, 8):
        one, two = first // sub_width, (first + 7) // sub_width
        index = jnp.broadcast_to(codes_ref[one : one + 1, :], (8, row_count))
        if two != one:
            later = jnp.broadcast_to(codes_ref[two : two + 1, :], (8, row_count))
            index = jnp.where(sublane < two * sub_width - first, index, later)
        book = book_ref[first : first + 8, :].astype(jnp.float32)
        parts = []
        for start in range(0, row_count, LANES):
            at = index[:, start : start + LANES]
            inner = at & (LANES - 1)
            value = jnp.take_along_axis(book[:, :LANES], inner, axis=1, mode="promise_in_bounds")
            for level in range(LANES, book.shape[1], LANES):
                other = jnp.take_along_axis(
                    book[:, level : level + LANES], inner, axis=1, mode="promise_in_bounds"
                )
                value = jnp.where(at >= level, other, value)
            parts.append(value)
        write(first, jnp.concatenate(parts, axis=1))


def decoded_rows(codes, book, sub_width, rows):
    def write(row, value):
        rows[row : row + 8, :] = value

    decode(codes, book, sub_width, write)
    return rows[...].astype(jnp.bfloat16)


def own_cross_kernel(sub_width, v0, v1, codes, book, cross, vectors, rows):
    core, _, _, _ = place()
    width = v0.shape[0]
    for k, v in enumerate((v0, v1)):
        vectors[pl.ds(pl.multiple_of((core ^ k) * width, 16), width), :] = v[...]
    cross[...] = dot_t(decoded_rows(codes, book, sub_width, rows), vectors[...])


def other_cross_kernel(sub_width, vectors, own, codes, book, *rest):
    outs, (both, rows) = rest[:4], rest[4:]
    _, pair, quarter, _ = place()
    width = own.shape[0]
    thin = width // 2
    both[pl.ds(pl.multiple_of(pair * width, 8), width), :] = own[...]
    other = dot_t(decoded_rows(codes, book, sub_width, rows), vectors[...])
    both[pl.ds(pl.multiple_of((1 - pair) * width, 8), width), :] = other
    for k, out in enumerate(outs):
        out[...] = both[pl.ds(pl.multiple_of((quarter ^ k) * thin, 8), thin), :]


def gram_blocks(size, high, low, whole, write):
    count = high.shape[0] // size
    for i in range(count):
        a = pl.ds(i * size, size)
        for j in range(i, count):
            b = pl.ds(j * size, size)
            block = dot_t(high[a, :], high[b, :])
            if whole:
                block = block + (dot_t(high[a, :], low[b, :]) + dot_t(low[a, :], high[b, :]))
            block = block.astype(jnp.bfloat16)
            write(i, j, block)
            if i != j:
                write(j, i, block.T)


def refit_kernel(sub_width, *refs):
    pieces, sources, codes = refs[:16], refs[16:20], refs[20]
    rotation_out, outs = refs[21], refs[22:26]
    current, halves, gram, vectors, rotated, total, arrived = refs[26:]
    core, pair, quarter, high_part = place()
    dp_count = lax.axis_size("dp")
    thin, half = pieces[0].shape
    width, size = 2 * thin, current.shape[0]
    block = 2 * LANES
    own = (pair * 2 + core) * width

    copies = []
    for mask, piece in enumerate(pieces):
        c, p, q = core ^ (mask & 1), pair ^ (mask >> 1 & 1), quarter ^ (mask >> 2)
        row = ((q >> 1) * 2 + c) * width + (q & 1) * thin
        rows, columns = pl.ds(pl.multiple_of(row, 8), thin), pl.ds(pl.multiple_of(p * half, LANES), half)
        copies.append(pltpu.make_async_copy(piece, current.at[rows, columns], arrived.at[mask]))
    for k, source in enumerate(sources):
        at = ((pair ^ (k >> 1)) * 2 + (core ^ (k & 1))) * width
        rows = pl.ds(pl.multiple_of(at, 16), width)
        copies.append(pltpu.make_async_copy(source, vectors.at[rows, :], arrived.at[16 + k]))
    for copy in copies:
        copy.start()
    for copy in copies[:16]:
        copy.wait()
    squares = jnp.zeros((8, size), jnp.float32)
    for row in range(0, size, 8):
        value = current[row : row + 8, :]
        squares = squares + value * value
    magnitude = jnp.sqrt(jnp.sum(squares))
    for row in range(0, size, block):
        value = current[row : row + block, :] / magnitude
        current[row : row + block, :] = value
        halves[0, 0, row : row + block, :], halves[0, 1, row : row + block, :] = split(value)

    def step(iteration):
        now, later = iteration % 2, (iteration + 1) % 2
        high, low = halves.at[now, 0], halves.at[now, 1]

        def write(i, j, value):
            gram[pl.ds(i * block, block), pl.ds(j * block, block)] = value

        gram_blocks(block, high, low, iteration == 0, write)
        for row in range(0, size, block):
            rows = pl.ds(row, block)
            update = dot(gram[rows, :], high[...]) + dot(gram[rows, :], low[...])
            value = 1.5 * current[rows, :] - 0.5 * update
            current[rows, :] = value
            halves[later, 0, rows, :], halves[later, 1, rows, :] = split(value)

    for iteration in range(NS_STEPS - 1):
        step(iteration)
    last = (NS_STEPS - 1) % 2
    high, low = halves.at[last, 0], halves.at[last, 1]
    rows = pl.ds(pl.multiple_of(own, 16), width)
    own_gram = dot_t(high[rows, :], high[...]) + (
        dot_t(high[rows, :], low[...]) + dot_t(low[rows, :], high[...])
    )
    own_high, own_low = split(own_gram)
    update = dot(own_high, high[...]) + (dot(own_high, low[...]) + dot(own_low, high[...]))
    rotation = 1.5 * current[rows, :] - 0.5 * update
    rotation_out[...] = rotation

    for copy in copies[16:]:
        copy.wait()
    sub_count, row_count = codes.shape
    rotated[:width, :] = dot(rotation.astype(jnp.bfloat16), vectors[...]).astype(jnp.bfloat16)
    rotated[width:, :] = jnp.ones((rotated.shape[0] - width, row_count), jnp.bfloat16)

    centroid_count, columns = total.shape
    owner_rows = centroid_count // dp_count
    quarter_rows = centroid_count // 4
    row = lax.broadcasted_iota(jnp.int32, (centroid_count, LANES), 0)
    position = row // quarter_rows
    inner = row % quarter_rows
    level = (((inner // owner_rows) ^ high_part) * 4 + (position ^ quarter)) * owner_rows + inner % owner_rows
    level = jnp.concatenate([level] * (row_count // LANES), axis=1)
    column = lax.broadcasted_iota(jnp.int32, (8, columns), 1)
    subspace = jnp.where(column < width, column // sub_width, column - width)
    subspace = jnp.broadcast_to(subspace[:1], total.shape)
    for m in range(sub_count):
        onehot = (codes[m : m + 1, :] == level).astype(jnp.float32).astype(jnp.bfloat16)
        sums = dot_t(onehot, rotated[...])
        total[...] = jnp.where(subspace == m, sums, total[...] if m else 0.0)
    for k, out in enumerate(outs):
        out[...] = total[k * quarter_rows : (k + 1) * quarter_rows, :]


def finish_kernel(sub_width, kept, received, out):
    total = kept[...] + received[...]
    width = out.shape[1]
    row = lax.broadcasted_iota(jnp.int32, (total.shape[1], width), 0)
    column = lax.broadcasted_iota(jnp.int32, (total.shape[1], width), 1)
    spread = (row == width + column // sub_width).astype(jnp.float32)
    counts = jnp.dot(total, spread, precision=lax.Precision.HIGHEST)
    out[...] = total[:, :width] / jnp.maximum(counts, 1.0)


def floats(*shape):
    return jax.ShapeDtypeStruct(shape, jnp.float32)


def call(kernel, outs, scratch, far, *args):
    spaces = [pltpu.HBM] * far + [pltpu.VMEM] * (len(args) - far)
    return pl.pallas_call(
        kernel,
        out_shape=outs,
        in_specs=[pl.BlockSpec(memory_space=space) for space in spaces],
        out_specs=[pl.BlockSpec(memory_space=pltpu.VMEM)] * len(outs),
        scratch_shapes=scratch,
        compiler_params=pltpu.CompilerParams(vmem_limit_bytes=VMEM_LIMIT),
    )(*args)


def per_device(vectors, codes, codebook):
    width, row_count = vectors.shape
    sub_count = codes.shape[0]
    sub_width = width // sub_count
    centroid_count = codebook.shape[0]
    dp_count = lax.axis_size("dp")
    total_width = width * DIMS
    half, thin = 2 * width, width // 2
    high_masks = [4 << bit for bit in range(2, dp_count.bit_length() - 1)]

    book = codebook.T
    book_other, codes_other = swap(book, 2), swap(codes, 2)
    vectors_core = swap(vectors, 1)
    own_cross, own_vectors = call(
        functools.partial(own_cross_kernel, sub_width),
        [floats(width, half), jax.ShapeDtypeStruct((half, row_count), jnp.bfloat16)],
        [pltpu.VMEM((width, row_count), jnp.float32)],
        0,
        vectors, vectors_core, codes, book,
    )
    parts = call(
        functools.partial(other_cross_kernel, sub_width),
        [floats(thin, half)] * 4,
        [pltpu.VMEM((half, half), jnp.float32), pltpu.VMEM((width, row_count), jnp.float32)],
        0,
        own_vectors, own_cross, codes_other, book_other,
    )
    held, vectors_late = lax.optimization_barrier((parts, vectors))
    vectors_pair = swap(vectors_late, 2)
    vectors_last = swap(vectors_pair, 1)

    piece = held[0] + swap(held[1], 4) + swap(held[2], 8) + swap(held[3], 12)
    for mask in high_masks:
        piece = piece + swap(piece, mask)
    pieces = [piece if mask == 0 else swap(piece, mask) for mask in range(0, 16, 2)]
    both = []
    for own in pieces:
        both += [own, swap(own, 1)]

    columns = width + sub_count
    columns += -columns % LANES
    rotation, *sums = call(
        functools.partial(refit_kernel, sub_width),
        [floats(width, total_width)] + [floats(centroid_count // 4, columns)] * 4,
        [
            pltpu.VMEM((total_width, total_width), jnp.float32),
            pltpu.VMEM((2, 2, total_width, total_width), jnp.bfloat16),
            pltpu.VMEM((total_width, total_width), jnp.bfloat16),
            pltpu.VMEM((total_width, row_count), jnp.bfloat16),
            pltpu.VMEM((columns, row_count), jnp.bfloat16),
            pltpu.VMEM((centroid_count, columns), jnp.float32),
            pltpu.SemaphoreType.DMA((20,)),
        ],
        20,
        *both, vectors, vectors_core, vectors_pair, vectors_last, codes,
    )
    held = sums[0] + swap(sums[1], 4) + swap(sums[2], 8) + swap(sums[3], 12)
    received = jnp.zeros_like(held)
    for step, mask in enumerate(reversed(high_masks)):
        if step:
            held = held + received
        middle = held.shape[0] // 2
        held, received = held[:middle], swap(held[middle:], mask)
    (new_codebook,) = call(
        functools.partial(finish_kernel, sub_width),
        [floats(centroid_count // dp_count, width)],
        [],
        0,
        held, received,
    )
    return rotation, new_codebook


def solution(mesh):
    placed = (P("dim", "dp"), P("dim", "dp"), P(None, "dim"))
    return jax.shard_map(
        per_device,
        mesh=mesh,
        in_specs=placed,
        out_specs=(P("dim", None), P("dp", "dim")),
        check_vma=False,
    )
```

time: 114 us -> 88.5 us (0.78)
  Pallas kernels: 47.9 us -> 25.4 us
  waiting for transfers between devices: 32.5 us -> 29 us
    pallas_call x3 -> x4, Pallas kernels: 47.9 us -> 25.4 us  [call(): pl.pallas_call(kernel, out_shape=outs, in_specs=[pl.BlockSpec(memory_spac...]
    ppermute x28, waiting for transfers between devices: 32.5 us -> 29 us  [swap(): lax.ppermute(value, ('dp', 'dim'), [(i, i ^ mask) for i in range(count)])]
  transfers between devices with their start and end apart: 28 -> 28, of which waited for: 19 -> 19; matrix products, arithmetic and copies ran while one was open for 1% -> 1% of each run, Pallas kernels for 0% -> 3%
where the time goes in v2:
time: 88.5 us; the launch traced here: 88.2 us
  waiting for transfers between devices  29 us (33%)
  starting transfers between devices  27.2 us (31%)
  Pallas kernels  25.4 us (29%)
  local copies, waits for them, and re-layouts  4 us (5%)
  other arithmetic  1.82 us (2%)
    ppermute x28, waiting for transfers between devices, swap(): lax.ppermute(value, ('dp', 'dim'), [(i, i ^ mask) for i in range(count)])  29 us
    ppermute x28, starting transfers between devices, swap(): lax.ppermute(value, ('dp', 'dim'), [(i, i ^ mask) for i in range(count)])  27.2 us
    pallas_call x4, Pallas kernels, call(): pl.pallas_call(kernel, out_shape=outs, in_specs=[pl.BlockSpec(memory_spac...  25.4 us
    unnamed x46, local copies, waits for them, and re-layouts  3.38 us
  transfers between devices with their start and end apart: 28, of which 19 were waited for; matrix products, arithmetic and copies ran while one was open for 1% of the time, Pallas kernels for 3%

profile of v2, /device:TPU:0, one launch (start us, length us, event | category | flops | bytes accessed | tf_op | source)
XLA Modules:
  0.0 88.2 jit_solution(13879456197879215399)
XLA Ops:
  1.1 2.6 %collective-permute-start.2 = (bf16[192,256]{1,0:T(8,128)(2,1)}, bf16[192,256]{1,0:T(8,128)(2,1)S(1)}, u32[]{:S(2)}, u32[]{:S(2)}) collective-permute-start(bf16[192,256]{1,0:T(8,128)(2,1)} %bitcast.1), channel_id=1, source_target_pairs={{0,2},{1,3},{2,0},{3,1},{4,6},{5,7},{6,4},{7,5},{8,10},{9,11},{10,... | collective-permute-start | bytes 294920 | tf_op jit(solution)/shard_map/ppermute | solution.py:18
  4.6 2.7 %shard_map.50 = (f32[192,384]{1,0:T(8,128)}, bf16[384,1024]{1,0:T(8,128)(2,1)}) custom-call(bf16[192,1024]{1,0:T(8,128)(2,1)} %refs_16_.1, bf16[192,1024]{1,0:T(8,128)(2,1)} %copy-done.1, s32[16,1024]{1,0:T(8,128)} %refs_20_.1, bf16[192,256]{1,0:T(8,128)(2,1)} %bitcast.2), custom_call_target="tpu_custom_call" | custom-call | tf_op jit(solution)/shard_map/pallas_call | solution.py:213
  7.3 1.5 %collective-permute-done.1.codes = s32[16,1024]{1,0:T(8,128)S(1)} collective-permute-done((s32[16,1024]{1,0:T(8,128)}, s32[16,1024]{1,0:T(8,128)S(1)}, u32[]{:S(2)}, u32[]{:S(2)}) %collective-permute-start.1) | collective-permute-done | bytes 65568 | tf_op jit(solution)/shard_map/ppermute | solution.py:18
  9.4 2.9 %shard_map.51 = (f32[96,384]{1,0:T(8,128)}, f32[96,384]{1,0:T(8,128)}, f32[96,384]{1,0:T(8,128)}, f32[96,384]{1,0:T(8,128)}) custom-call(bf16[384,1024]{1,0:T(8,128)(2,1)} %get-tuple-element.18.vectors, f32[192,384]{1,0:T(8,128)} %get-tuple-element.19.own, s32[16,1024]{1,0:T(8,128)} %copy-done.21, bf16[192,256]{1,0:T(8,128)(2,1)} %copy-done.20), custom_call_target="tpu_custom_call" | custom-call | tf_op jit(solution)/shard_map/pallas_call | solution.py:213
  12.4 1.7 %collective-permute-start.3 = (f32[96,384]{1,0:T(8,128)}, f32[96,384]{1,0:T(8,128)S(1)}, u32[]{:S(2)}, u32[]{:S(2)}) collective-permute-start(f32[96,384]{1,0:T(8,128)} %get-tuple-element.25), channel_id=1, source_target_pairs={{0,4},{1,5},{2,6},{3,7},{4,0},{5,1},{6,2},{7,3},{8,12},{9,13},{10,... | collective-permute-start | bytes 442376 | tf_op jit(solution)/shard_map/ppermute | solution.py:18
  14.1 1.6 %collective-permute-start.4 = (f32[96,384]{1,0:T(8,128)}, f32[96,384]{1,0:T(8,128)S(1)}, u32[]{:S(2)}, u32[]{:S(2)}) collective-permute-start(f32[96,384]{1,0:T(8,128)} %get-tuple-element.26), channel_id=1, source_target_pairs={{0,8},{1,9},{2,10},{3,11},{4,12},{5,13},{6,14},{7,15},{8,0},{9,1},... | collective-permute-start | bytes 442376 | tf_op jit(solution)/shard_map/ppermute | solution.py:18
  15.9 1.8 %collective-permute-start.22 = (bf16[192,1024]{1,0:T(8,128)(2,1)S(1)}, bf16[192,1024]{1,0:T(8,128)(2,1)S(1)}, u32[]{:S(2)}, u32[]{:S(2)}) collective-permute-start(bf16[192,1024]{1,0:T(8,128)(2,1)S(1)} %copy-done), channel_id=1, source_target_pairs={{0,2},{1,3},{2,0},{3,1},{4,6},{5,7},{6,4},{7,5},{8,10},{9,11},{10,... | collective-permute-start | bytes 1179656 | tf_op jit(solution)/shard_map/ppermute | solution.py:18
  18.2 2.8 %collective-permute-done.4 = f32[96,384]{1,0:T(8,128)S(1)} collective-permute-done((f32[96,384]{1,0:T(8,128)}, f32[96,384]{1,0:T(8,128)S(1)}, u32[]{:S(2)}, u32[]{:S(2)}) %collective-permute-start.4) | collective-permute-done | bytes 147488 | tf_op jit(solution)/shard_map/ppermute | solution.py:18
  21.0 1.5 %collective-permute-done.5 = f32[96,384]{1,0:T(8,128)S(1)} collective-permute-done((f32[96,384]{1,0:T(8,128)}, f32[96,384]{1,0:T(8,128)S(1)}, u32[]{:S(2)}, u32[]{:S(2)}) %collective-permute-start.5) | collective-permute-done | bytes 147488 | tf_op jit(solution)/shard_map/ppermute | solution.py:18
  23.5 2.7 %collective-permute-start.6 = (f32[96,384]{1,0:T(8,128)S(1)}, f32[96,384]{1,0:T(8,128)S(1)}, u32[]{:S(2)}, u32[]{:S(2)}) collective-permute-start(f32[96,384]{1,0:T(8,128)S(1)} %add_add_fusion), channel_id=1, source_target_pairs={{0,16},{1,17},{2,18},{3,19},{4,20},{5,21},{6,22},{7,23},{8,24},{9,... | collective-permute-start | bytes 442376 | tf_op jit(solution)/shard_map/ppermute | solution.py:18
  26.2 6.3 %collective-permute-done.6 = f32[96,384]{1,0:T(8,128)S(1)} collective-permute-done((f32[96,384]{1,0:T(8,128)S(1)}, f32[96,384]{1,0:T(8,128)S(1)}, u32[]{:S(2)}, u32[]{:S(2)}) %collective-permute-start.6) | collective-permute-done | bytes 147488 | tf_op jit(solution)/shard_map/ppermute | solution.py:18
  32.5 1.7 %collective-permute-start.20 = (f32[96,384]{1,0:T(8,128)S(1)}, f32[96,384]{1,0:T(8,128)S(1)}, u32[]{:S(2)}, u32[]{:S(2)}) collective-permute-start(f32[96,384]{1,0:T(8,128)S(1)} %add.24.refs_0_), channel_id=1, source_target_pairs={{0,14},{1,15},{2,12},{3,13},{4,10},{5,11},{6,8},{7,9},{8,6},{9,7},... | collective-permute-start | bytes 442376 | tf_op jit(solution)/shard_map/ppermute | solution.py:18
  34.2 2.3 %collective-permute-start.18 = (f32[96,384]{1,0:T(8,128)S(1)}, f32[96,384]{1,0:T(8,128)S(1)}, u32[]{:S(2)}, u32[]{:S(2)}) collective-permute-start(f32[96,384]{1,0:T(8,128)S(1)} %add.24.refs_0_), channel_id=1, source_target_pairs={{0,12},{1,13},{2,14},{3,15},{4,8},{5,9},{6,10},{7,11},{8,4},{9,5},... | collective-permute-start | bytes 442376 | tf_op jit(solution)/shard_map/ppermute | solution.py:18
  36.5 1.9 %collective-permute-start.14 = (f32[96,384]{1,0:T(8,128)S(1)}, f32[96,384]{1,0:T(8,128)S(1)}, u32[]{:S(2)}, u32[]{:S(2)}) collective-permute-start(f32[96,384]{1,0:T(8,128)S(1)} %add.24.refs_0_), channel_id=1, source_target_pairs={{0,8},{1,9},{2,10},{3,11},{4,12},{5,13},{6,14},{7,15},{8,0},{9,1},... | collective-permute-start | bytes 442376 | tf_op jit(solution)/shard_map/ppermute | solution.py:18
  38.4 1.5 %collective-permute-start.12 = (f32[96,384]{1,0:T(8,128)S(1)}, f32[96,384]{1,0:T(8,128)S(1)}, u32[]{:S(2)}, u32[]{:S(2)}) collective-permute-start(f32[96,384]{1,0:T(8,128)S(1)} %add.24.refs_0_), channel_id=1, source_target_pairs={{0,6},{1,7},{2,4},{3,5},{4,2},{5,3},{6,0},{7,1},{8,14},{9,15},{10,... | collective-permute-start | bytes 442376 | tf_op jit(solution)/shard_map/ppermute | solution.py:18
  41.5 2.9 %collective-permute-done.18.refs_12_ = f32[96,384]{1,0:T(8,128)S(1)} collective-permute-done((f32[96,384]{1,0:T(8,128)S(1)}, f32[96,384]{1,0:T(8,128)S(1)}, u32[]{:S(2)}, u32[]{:S(2)}) %collective-permute-start.18) | collective-permute-done | bytes 147488 | tf_op jit(solution)/shard_map/ppermute | solution.py:18
  44.8 2.0 %collective-permute-done.14.refs_8_ = f32[96,384]{1,0:T(8,128)S(1)} collective-permute-done((f32[96,384]{1,0:T(8,128)S(1)}, f32[96,384]{1,0:T(8,128)S(1)}, u32[]{:S(2)}, u32[]{:S(2)}) %collective-permute-start.14) | collective-permute-done | bytes 147488 | tf_op jit(solution)/shard_map/ppermute | solution.py:18
  47.4 2.6 %collective-permute-done.10.refs_4_ = f32[96,384]{1,0:T(8,128)S(1)} collective-permute-done((f32[96,384]{1,0:T(8,128)S(1)}, f32[96,384]{1,0:T(8,128)S(1)}, u32[]{:S(2)}, u32[]{:S(2)}) %collective-permute-start.10) | collective-permute-done | bytes 147488 | tf_op jit(solution)/shard_map/ppermute | solution.py:18
  54.3 18.1 %shard_map.52 = (f32[192,768]{1,0:T(8,128)}, f32[64,256]{1,0:T(8,128)}, f32[64,256]{1,0:T(8,128)}, f32[64,256]{1,0:T(8,128)}, f32[64,256]{1,0:T(8,128)}) custom-call(f32[96,384]{1,0:T(8,128)} %copy-done.2, f32[96,384]{1,0:T(8,128)} %copy-done.12, f32[96,384]{1,0:T(8,128)} %copy-done.11, f32[96,384]{1,0:T(8,128)} %copy-done.19, f32[96,384]{1,0:T(8,128)} %copy-done.10, ...), custom_call_target="tpu_custom_call" | custom-call | tf_op jit(solution)/shard_map/pallas_call | solution.py:213
  74.2 1.8 %collective-permute-start.26 = (f32[64,256]{1,0:T(8,128)}, f32[64,256]{1,0:T(8,128)S(1)}, u32[]{:S(2)}, u32[]{:S(2)}) collective-permute-start(f32[64,256]{1,0:T(8,128)} %get-tuple-element.33), channel_id=1, source_target_pairs={{0,12},{1,13},{2,14},{3,15},{4,8},{5,9},{6,10},{7,11},{8,4},{9,5},... | collective-permute-start | bytes 196616 | tf_op jit(solution)/shard_map/ppermute | solution.py:18
  77.0 1.4 %collective-permute-done.25 = f32[64,256]{1,0:T(8,128)S(1)} collective-permute-done((f32[64,256]{1,0:T(8,128)}, f32[64,256]{1,0:T(8,128)S(1)}, u32[]{:S(2)}, u32[]{:S(2)}) %collective-permute-start.25) | collective-permute-done | bytes 65568 | tf_op jit(solution)/shard_map/ppermute | solution.py:18
  81.1 2.4 %collective-permute-start.27 = (f32[32,256]{1,0:T(8,128)S(1)}, f32[32,256]{1,0:T(8,128)S(1)}, u32[]{:S(2)}, u32[]{:S(2)}) collective-permute-start(f32[32,256]{1,0:T(8,128)S(1)} %get-tuple-element.34), channel_id=1, source_target_pairs={{0,16},{1,17},{2,18},{3,19},{4,20},{5,21},{6,22},{7,23},{8,24},{9,... | collective-permute-start | bytes 98312 | tf_op jit(solution)/shard_map/ppermute | solution.py:18
  83.5 2.4 %collective-permute-done.27.received = f32[32,256]{1,0:T(8,128)S(1)} collective-permute-done((f32[32,256]{1,0:T(8,128)S(1)}, f32[32,256]{1,0:T(8,128)S(1)}, u32[]{:S(2)}, u32[]{:S(2)}) %collective-permute-start.27) | collective-permute-done | bytes 32800 | tf_op jit(solution)/shard_map/ppermute | solution.py:18
  86.5 1.6 %shard_map.53 = f32[32,192]{1,0:T(8,128)} custom-call(f32[32,256]{1,0:T(8,128)} %get-tuple-element.35.kept, f32[32,256]{1,0:T(8,128)} %copy-done.22), custom_call_target="tpu_custom_call" | custom-call | tf_op jit(solution)/shard_map/pallas_call | solution.py:213
  (86 shorter events, 16.5 us)
Async XLA Ops:
  0.6 3.2 %collective-permute-start = (bf16[192,1024]{1,0:T(8,128)(2,1)}, bf16[192,1024]{1,0:T(8,128)(2,1)S(1)}, u32[]{:S(2)}, u32[]{:S(2)}) collective-permute-start(bf16[192,1024]{1,0:T(8,128)(2,1)} %refs_16_.1), channel_id=1, source_target_pairs={{0,1},{1,0},{2,3},{3,2},{4,5},{5,4},{6,7},{7,6},{8,9},{9,8},{10,11... | collective-permute-start | bytes 1179656 | tf_op jit(solution)/shard_map/ppermute | solution.py:18
  1.1 7.6 %collective-permute-start.2 = (bf16[192,256]{1,0:T(8,128)(2,1)}, bf16[192,256]{1,0:T(8,128)(2,1)S(1)}, u32[]{:S(2)}, u32[]{:S(2)}) collective-permute-start(bf16[192,256]{1,0:T(8,128)(2,1)} %bitcast.1), channel_id=1, source_target_pairs={{0,2},{1,3},{2,0},{3,1},{4,6},{5,7},{6,4},{7,5},{8,10},{9,11},{10,... | collective-permute-start | bytes 294920 | tf_op jit(solution)/shard_map/ppermute | solution.py:18
  3.7 5.0 %collective-permute-start.1 = (s32[16,1024]{1,0:T(8,128)}, s32[16,1024]{1,0:T(8,128)S(1)}, u32[]{:S(2)}, u32[]{:S(2)}) collective-permute-start(s32[16,1024]{1,0:T(8,128)} %refs_20_.1), channel_id=1, source_target_pairs={{0,2},{1,3},{2,0},{3,1},{4,6},{5,7},{6,4},{7,5},{8,10},{9,11},{10,... | collective-permute-start | bytes 196616 | tf_op jit(solution)/shard_map/ppermute | solution.py:18
  12.4 5.8 %collective-permute-start.3 = (f32[96,384]{1,0:T(8,128)}, f32[96,384]{1,0:T(8,128)S(1)}, u32[]{:S(2)}, u32[]{:S(2)}) collective-permute-start(f32[96,384]{1,0:T(8,128)} %get-tuple-element.25), channel_id=1, source_target_pairs={{0,4},{1,5},{2,6},{3,7},{4,0},{5,1},{6,2},{7,3},{8,12},{9,13},{10,... | collective-permute-start | bytes 442376 | tf_op jit(solution)/shard_map/ppermute | solution.py:18
  14.1 6.9 %collective-permute-start.4 = (f32[96,384]{1,0:T(8,128)}, f32[96,384]{1,0:T(8,128)S(1)}, u32[]{:S(2)}, u32[]{:S(2)}) collective-permute-start(f32[96,384]{1,0:T(8,128)} %get-tuple-element.26), channel_id=1, source_target_pairs={{0,8},{1,9},{2,10},{3,11},{4,12},{5,13},{6,14},{7,15},{8,0},{9,1},... | collective-permute-start | bytes 442376 | tf_op jit(solution)/shard_map/ppermute | solution.py:18
  15.7 6.8 %collective-permute-start.5 = (f32[96,384]{1,0:T(8,128)}, f32[96,384]{1,0:T(8,128)S(1)}, u32[]{:S(2)}, u32[]{:S(2)}) collective-permute-start(f32[96,384]{1,0:T(8,128)} %get-tuple-element.27), channel_id=1, source_target_pairs={{0,12},{1,13},{2,14},{3,15},{4,8},{5,9},{6,10},{7,11},{8,4},{9,5},... | collective-permute-start | bytes 442376 | tf_op jit(solution)/shard_map/ppermute | solution.py:18
  15.9 22.6 %collective-permute-start.22 = (bf16[192,1024]{1,0:T(8,128)(2,1)S(1)}, bf16[192,1024]{1,0:T(8,128)(2,1)S(1)}, u32[]{:S(2)}, u32[]{:S(2)}) collective-permute-start(bf16[192,1024]{1,0:T(8,128)(2,1)S(1)} %copy-done), channel_id=1, source_target_pairs={{0,2},{1,3},{2,0},{3,1},{4,6},{5,7},{6,4},{7,5},{8,10},{9,11},{10,... | collective-permute-start | bytes 1179656 | tf_op jit(solution)/shard_map/ppermute | solution.py:18
  23.5 9.0 %collective-permute-start.6 = (f32[96,384]{1,0:T(8,128)S(1)}, f32[96,384]{1,0:T(8,128)S(1)}, u32[]{:S(2)}, u32[]{:S(2)}) collective-permute-start(f32[96,384]{1,0:T(8,128)S(1)} %add_add_fusion), channel_id=1, source_target_pairs={{0,16},{1,17},{2,18},{3,19},{4,20},{5,21},{6,22},{7,23},{8,24},{9,... | collective-permute-start | bytes 442376 | tf_op jit(solution)/shard_map/ppermute | solution.py:18
  32.5 8.7 %collective-permute-start.20 = (f32[96,384]{1,0:T(8,128)S(1)}, f32[96,384]{1,0:T(8,128)S(1)}, u32[]{:S(2)}, u32[]{:S(2)}) collective-permute-start(f32[96,384]{1,0:T(8,128)S(1)} %add.24.refs_0_), channel_id=1, source_target_pairs={{0,14},{1,15},{2,12},{3,13},{4,10},{5,11},{6,8},{7,9},{8,6},{9,7},... | collective-permute-start | bytes 442376 | tf_op jit(solution)/shard_map/ppermute | solution.py:18
  34.2 10.2 %collective-permute-start.18 = (f32[96,384]{1,0:T(8,128)S(1)}, f32[96,384]{1,0:T(8,128)S(1)}, u32[]{:S(2)}, u32[]{:S(2)}) collective-permute-start(f32[96,384]{1,0:T(8,128)S(1)} %add.24.refs_0_), channel_id=1, source_target_pairs={{0,12},{1,13},{2,14},{3,15},{4,8},{5,9},{6,10},{7,11},{8,4},{9,5},... | collective-permute-start | bytes 442376 | tf_op jit(solution)/shard_map/ppermute | solution.py:18
  36.5 8.3 %collective-permute-start.16 = (f32[96,384]{1,0:T(8,128)S(1)}, f32[96,384]{1,0:T(8,128)S(1)}, u32[]{:S(2)}, u32[]{:S(2)}) collective-permute-start(f32[96,384]{1,0:T(8,128)S(1)} %add.24.refs_0_), channel_id=1, source_target_pairs={{0,10},{1,11},{2,8},{3,9},{4,14},{5,15},{6,12},{7,13},{8,2},{9,3},... | collective-permute-start | bytes 442376 | tf_op jit(solution)/shard_map/ppermute | solution.py:18
  36.5 10.4 %collective-permute-start.14 = (f32[96,384]{1,0:T(8,128)S(1)}, f32[96,384]{1,0:T(8,128)S(1)}, u32[]{:S(2)}, u32[]{:S(2)}) collective-permute-start(f32[96,384]{1,0:T(8,128)S(1)} %add.24.refs_0_), channel_id=1, source_target_pairs={{0,8},{1,9},{2,10},{3,11},{4,12},{5,13},{6,14},{7,15},{8,0},{9,1},... | collective-permute-start | bytes 442376 | tf_op jit(solution)/shard_map/ppermute | solution.py:18
  38.4 8.6 %collective-permute-start.12 = (f32[96,384]{1,0:T(8,128)S(1)}, f32[96,384]{1,0:T(8,128)S(1)}, u32[]{:S(2)}, u32[]{:S(2)}) collective-permute-start(f32[96,384]{1,0:T(8,128)S(1)} %add.24.refs_0_), channel_id=1, source_target_pairs={{0,6},{1,7},{2,4},{3,5},{4,2},{5,3},{6,0},{7,1},{8,14},{9,15},{10,... | collective-permute-start | bytes 442376 | tf_op jit(solution)/shard_map/ppermute | solution.py:18
  41.2 8.8 %collective-permute-start.10 = (f32[96,384]{1,0:T(8,128)S(1)}, f32[96,384]{1,0:T(8,128)S(1)}, u32[]{:S(2)}, u32[]{:S(2)}) collective-permute-start(f32[96,384]{1,0:T(8,128)S(1)} %add.24.refs_0_), channel_id=1, source_target_pairs={{0,4},{1,5},{2,6},{3,7},{4,0},{5,1},{6,2},{7,3},{8,12},{9,13},{10,... | collective-permute-start | bytes 442376 | tf_op jit(solution)/shard_map/ppermute | solution.py:18
  44.4 5.6 %collective-permute-start.8 = (f32[96,384]{1,0:T(8,128)S(1)}, f32[96,384]{1,0:T(8,128)S(1)}, u32[]{:S(2)}, u32[]{:S(2)}) collective-permute-start(f32[96,384]{1,0:T(8,128)S(1)} %add.24.refs_0_), channel_id=1, source_target_pairs={{0,2},{1,3},{2,0},{3,1},{4,6},{5,7},{6,4},{7,5},{8,10},{9,11},{10,... | collective-permute-start | bytes 442376 | tf_op jit(solution)/shard_map/ppermute | solution.py:18
  44.8 8.1 %collective-permute-start.23 = (bf16[192,1024]{1,0:T(8,128)(2,1)S(1)}, bf16[192,1024]{1,0:T(8,128)(2,1)S(1)}, u32[]{:S(2)}, u32[]{:S(2)}) collective-permute-start(bf16[192,1024]{1,0:T(8,128)(2,1)S(1)} %collective-permute-done.22.refs_18_), channel_id=1, source_target_pairs={{0,1},{1,0},{2,3},{3,2},{4,5},{5,4},{6,7},{7,6},{8,9},{9,8},{10,11... | collective-permute-start | bytes 1179656 | tf_op jit(solution)/shard_map/ppermute | solution.py:18
  46.9 3.6 %collective-permute-start.7 = (f32[96,384]{1,0:T(8,128)S(1)}, f32[96,384]{1,0:T(8,128)S(1)}, u32[]{:S(2)}, u32[]{:S(2)}) collective-permute-start(f32[96,384]{1,0:T(8,128)S(1)} %add.24.refs_0_), channel_id=1, source_target_pairs={{0,1},{1,0},{2,3},{3,2},{4,5},{5,4},{6,7},{7,6},{8,9},{9,8},{10,11... | collective-permute-start | bytes 442376 | tf_op jit(solution)/shard_map/ppermute | solution.py:18
  47.0 3.5 %collective-permute-start.21 = (f32[96,384]{1,0:T(8,128)S(1)}, f32[96,384]{1,0:T(8,128)S(1)}, u32[]{:S(2)}, u32[]{:S(2)}) collective-permute-start(f32[96,384]{1,0:T(8,128)S(1)} %collective-permute-done.20.refs_14_), channel_id=1, source_target_pairs={{0,1},{1,0},{2,3},{3,2},{4,5},{5,4},{6,7},{7,6},{8,9},{9,8},{10,11... | collective-permute-start | bytes 442376 | tf_op jit(solution)/shard_map/ppermute | solution.py:18
  50.0 1.6 %collective-permute-start.17 = (f32[96,384]{1,0:T(8,128)S(1)}, f32[96,384]{1,0:T(8,128)S(1)}, u32[]{:S(2)}, u32[]{:S(2)}) collective-permute-start(f32[96,384]{1,0:T(8,128)S(1)} %collective-permute-done.16.refs_10_), channel_id=1, source_target_pairs={{0,1},{1,0},{2,3},{3,2},{4,5},{5,4},{6,7},{7,6},{8,9},{9,8},{10,11... | collective-permute-start | bytes 442376 | tf_op jit(solution)/shard_map/ppermute | solution.py:18
  50.6 1.5 %collective-permute-start.13 = (f32[96,384]{1,0:T(8,128)S(1)}, f32[96,384]{1,0:T(8,128)S(1)}, u32[]{:S(2)}, u32[]{:S(2)}) collective-permute-start(f32[96,384]{1,0:T(8,128)S(1)} %collective-permute-done.12.refs_6_), channel_id=1, source_target_pairs={{0,1},{1,0},{2,3},{3,2},{4,5},{5,4},{6,7},{7,6},{8,9},{9,8},{10,11... | collective-permute-start | bytes 442376 | tf_op jit(solution)/shard_map/ppermute | solution.py:18
  72.4 4.6 %collective-permute-start.24 = (f32[64,256]{1,0:T(8,128)}, f32[64,256]{1,0:T(8,128)S(1)}, u32[]{:S(2)}, u32[]{:S(2)}) collective-permute-start(f32[64,256]{1,0:T(8,128)} %get-tuple-element.31), channel_id=1, source_target_pairs={{0,4},{1,5},{2,6},{3,7},{4,0},{5,1},{6,2},{7,3},{8,12},{9,13},{10,... | collective-permute-start | bytes 196616 | tf_op jit(solution)/shard_map/ppermute | solution.py:18
  73.6 4.8 %collective-permute-start.25 = (f32[64,256]{1,0:T(8,128)}, f32[64,256]{1,0:T(8,128)S(1)}, u32[]{:S(2)}, u32[]{:S(2)}) collective-permute-start(f32[64,256]{1,0:T(8,128)} %get-tuple-element.32), channel_id=1, source_target_pairs={{0,8},{1,9},{2,10},{3,11},{4,12},{5,13},{6,14},{7,15},{8,0},{9,1},... | collective-permute-start | bytes 196616 | tf_op jit(solution)/shard_map/ppermute | solution.py:18
  74.2 5.4 %collective-permute-start.26 = (f32[64,256]{1,0:T(8,128)}, f32[64,256]{1,0:T(8,128)S(1)}, u32[]{:S(2)}, u32[]{:S(2)}) collective-permute-start(f32[64,256]{1,0:T(8,128)} %get-tuple-element.33), channel_id=1, source_target_pairs={{0,12},{1,13},{2,14},{3,15},{4,8},{5,9},{6,10},{7,11},{8,4},{9,5},... | collective-permute-start | bytes 196616 | tf_op jit(solution)/shard_map/ppermute | solution.py:18
  81.1 4.8 %collective-permute-start.27 = (f32[32,256]{1,0:T(8,128)S(1)}, f32[32,256]{1,0:T(8,128)S(1)}, u32[]{:S(2)}, u32[]{:S(2)}) collective-permute-start(f32[32,256]{1,0:T(8,128)S(1)} %get-tuple-element.34), channel_id=1, source_target_pairs={{0,16},{1,17},{2,18},{3,19},{4,20},{5,21},{6,22},{7,23},{8,24},{9,... | collective-permute-start | bytes 98312 | tf_op jit(solution)/shard_map/ppermute | solution.py:18
  (27 other events, 108.5 us)

commit v3 on v2

--- a/solution.py
+++ b/solution.py
@@ -107,7 +107,7 @@
 
 
 def refit_kernel(sub_width, *refs):
-    pieces, sources, codes = refs[:16], refs[16:20], refs[20]
+    pieces, codes, sources = refs[:16], refs[16], refs[17:21]
     rotation_out, outs = refs[21], refs[22:26]
     current, halves, gram, vectors, rotated, total, arrived = refs[26:]
     core, pair, quarter, high_part = place()
@@ -118,19 +118,16 @@
     own = (pair * 2 + core) * width
 
     copies = []
+    for k, source in enumerate(sources):
+        at = ((pair ^ (k >> 1)) * 2 + (core ^ (k & 1))) * width
+        rows = pl.ds(pl.multiple_of(at, 16), width)
+        copies.append(pltpu.make_async_copy(source, vectors.at[rows, :], arrived.at[k]))
+        copies[k].start()
     for mask, piece in enumerate(pieces):
         c, p, q = core ^ (mask & 1), pair ^ (mask >> 1 & 1), quarter ^ (mask >> 2)
         row = ((q >> 1) * 2 + c) * width + (q & 1) * thin
         rows, columns = pl.ds(pl.multiple_of(row, 8), thin), pl.ds(pl.multiple_of(p * half, LANES), half)
-        copies.append(pltpu.make_async_copy(piece, current.at[rows, columns], arrived.at[mask]))
-    for k, source in enumerate(sources):
-        at = ((pair ^ (k >> 1)) * 2 + (core ^ (k & 1))) * width
-        rows = pl.ds(pl.multiple_of(at, 16), width)
-        copies.append(pltpu.make_async_copy(source, vectors.at[rows, :], arrived.at[16 + k]))
-    for copy in copies:
-        copy.start()
-    for copy in copies[:16]:
-        copy.wait()
+        current[rows, columns] = piece[...]
     squares = jnp.zeros((8, size), jnp.float32)
     for row in range(0, size, 8):
         value = current[row : row + 8, :]
@@ -169,7 +166,7 @@
     rotation = 1.5 * current[rows, :] - 0.5 * update
     rotation_out[...] = rotation
 
-    for copy in copies[16:]:
+    for copy in copies:
         copy.wait()
     sub_count, row_count = codes.shape
     rotated[:width, :] = dot(rotation.astype(jnp.bfloat16), vectors[...]).astype(jnp.bfloat16)
@@ -208,8 +205,12 @@
     return jax.ShapeDtypeStruct(shape, jnp.float32)
 
 
+def near(value):
+    return pltpu.with_memory_space_constraint(value, pltpu.VMEM)
+
+
 def call(kernel, outs, scratch, far, *args):
-    spaces = [pltpu.HBM] * far + [pltpu.VMEM] * (len(args) - far)
+    spaces = [pltpu.VMEM] * (len(args) - far) + [pl.ANY] * far
     return pl.pallas_call(
         kernel,
         out_shape=outs,
@@ -235,17 +236,17 @@
     vectors_core = swap(vectors, 1)
     own_cross, own_vectors = call(
         functools.partial(own_cross_kernel, sub_width),
-        [floats(width, half), jax.ShapeDtypeStruct((half, row_count), jnp.bfloat16)],
+        [pltpu.VMEM((width, half), jnp.float32), pltpu.VMEM((half, row_count), jnp.bfloat16)],
         [pltpu.VMEM((width, row_count), jnp.float32)],
         0,
-        vectors, vectors_core, codes, book,
+        vectors, near(vectors_core), codes, book,
     )
     parts = call(
         functools.partial(other_cross_kernel, sub_width),
-        [floats(thin, half)] * 4,
+        [pltpu.VMEM((thin, half), jnp.float32)] * 4,
         [pltpu.VMEM((half, half), jnp.float32), pltpu.VMEM((width, row_count), jnp.float32)],
         0,
-        own_vectors, own_cross, codes_other, book_other,
+        near(own_vectors), near(own_cross), near(codes_other), near(book_other),
     )
     held, vectors_late = lax.optimization_barrier((parts, vectors))
     vectors_pair = swap(vectors_late, 2)
@@ -263,7 +264,7 @@
     columns += -columns % LANES
     rotation, *sums = call(
         functools.partial(refit_kernel, sub_width),
-        [floats(width, total_width)] + [floats(centroid_count // 4, columns)] * 4,
+        [floats(width, total_width)] + [pltpu.VMEM((centroid_count // 4, columns), jnp.float32)] * 4,
         [
             pltpu.VMEM((total_width, total_width), jnp.float32),
             pltpu.VMEM((2, 2, total_width, total_width), jnp.bfloat16),
@@ -271,10 +272,10 @@
             pltpu.VMEM((total_width, row_count), jnp.bfloat16),
             pltpu.VMEM((columns, row_count), jnp.bfloat16),
             pltpu.VMEM((centroid_count, columns), jnp.float32),
-            pltpu.SemaphoreType.DMA((20,)),
+            pltpu.SemaphoreType.DMA((4,)),
         ],
-        20,
-        *both, vectors, vectors_core, vectors_pair, vectors_last, codes,
+        4,
+        *map(near, both), codes, vectors, near(vectors_core), near(vectors_pair), near(vectors_last),
     )
     held = sums[0] + swap(sums[1], 4) + swap(sums[2], 8) + swap(sums[3], 12)
     received = jnp.zeros_like(held)
@@ -288,7 +289,7 @@
         [floats(centroid_count // dp_count, width)],
         [],
         0,
-        held, received,
+        near(held), near(received),
     )
     return rotation, new_codebook
 

time: 88.5 us -> 78.3 us (0.88)
  Pallas kernels: 25.4 us -> 19.9 us
  local copies, waits for them, and re-layouts: 4 us -> 0.01 us
  other arithmetic: 1.82 us -> 0.06 us
  waiting for transfers between devices: 29 us -> 30.2 us
    pallas_call x4, Pallas kernels: 25.4 us -> 19.9 us  [call(): pl.pallas_call(kernel, out_shape=outs, in_specs=[pl.BlockSpec(memory_spac...]
    unnamed x46 -> x2, local copies, waits for them, and re-layouts: 3.38 us -> 0.01 us
    ppermute x28, waiting for transfers between devices: 29 us -> 30.2 us  [swap(): lax.ppermute(value, ('dp', 'dim'), [(i, i ^ mask) for i in range(count)])]
    add x1, other arithmetic: 0.94 us -> 0.03 us  [per_device(): piece = held[0] + swap(held[1], 4) + swap(held[2], 8) + swap(held[3], 12)]
  transfers between devices with their start and end apart: 28 -> 28, of which waited for: 19 -> 19; matrix products, arithmetic and copies ran while one was open for 1% -> 0% of each run, Pallas kernels for 3% -> 2%
where the time goes in v3:
time: 78.3 us; the launch traced here: 78.2 us
  waiting for transfers between devices  30.2 us (39%)
  starting transfers between devices  27.3 us (35%)
  Pallas kernels  19.9 us (25%)
    ppermute x28, waiting for transfers between devices, swap(): lax.ppermute(value, ('dp', 'dim'), [(i, i ^ mask) for i in range(count)])  30.2 us
    ppermute x28, starting transfers between devices, swap(): lax.ppermute(value, ('dp', 'dim'), [(i, i ^ mask) for i in range(count)])  27.3 us
    pallas_call x4, Pallas kernels, call(): pl.pallas_call(kernel, out_shape=outs, in_specs=[pl.BlockSpec(memory_spac...  19.9 us
  transfers between devices with their start and end apart: 28, of which 19 were waited for; matrix products, arithmetic and copies ran while one was open for 0% of the time, Pallas kernels for 2%

profile of v3, /device:TPU:0, one launch (start us, length us, event | category | flops | bytes accessed | tf_op | source)
XLA Modules:
  0.0 78.2 jit_solution(9388037631054695323)
XLA Ops:
  1.1 2.6 %collective-permute-start.2 = (bf16[192,256]{1,0:T(8,128)(2,1)}, bf16[192,256]{1,0:T(8,128)(2,1)S(1)}, u32[]{:S(2)}, u32[]{:S(2)}) collective-permute-start(bf16[192,256]{1,0:T(8,128)(2,1)} %bitcast.1), channel_id=1, source_target_pairs={{0,2},{1,3},{2,0},{3,1},{4,6},{5,7},{6,4},{7,5},{8,10},{9,11},{10,... | collective-permute-start | bytes 294920 | tf_op jit(solution)/shard_map/ppermute | solution.py:18
  3.8 1.9 %shard_map.50 = (f32[192,384]{1,0:T(8,128)S(1)}, bf16[384,1024]{1,0:T(8,128)(2,1)S(1)}) custom-call(bf16[192,1024]{1,0:T(8,128)(2,1)} %refs_17_.1, bf16[192,1024]{1,0:T(8,128)(2,1)S(1)} %collective-permute-done.v1.refs_18_, s32[16,1024]{1,0:T(8,128)} %refs_16_.1, bf16[192,256]{1,0:T(8,128)(2,1)} %bitcast.2), custom_call_target="tpu_custom_call" | custom-call | tf_op jit(solution)/shard_map/pallas_call | solution.py:214
  5.7 3.0 %collective-permute-done.1.codes = s32[16,1024]{1,0:T(8,128)S(1)} collective-permute-done((s32[16,1024]{1,0:T(8,128)}, s32[16,1024]{1,0:T(8,128)S(1)}, u32[]{:S(2)}, u32[]{:S(2)}) %collective-permute-start.1) | collective-permute-done | bytes 65568 | tf_op jit(solution)/shard_map/ppermute | solution.py:18
  9.6 1.8 %collective-permute-start.3 = (f32[96,384]{1,0:T(8,128)S(1)}, f32[96,384]{1,0:T(8,128)S(1)}, u32[]{:S(2)}, u32[]{:S(2)}) collective-permute-start(f32[96,384]{1,0:T(8,128)S(1)} %get-tuple-element.25), channel_id=1, source_target_pairs={{0,4},{1,5},{2,6},{3,7},{4,0},{5,1},{6,2},{7,3},{8,12},{9,13},{10,... | collective-permute-start | bytes 442376 | tf_op jit(solution)/shard_map/ppermute | solution.py:18
  11.4 1.6 %collective-permute-start.4 = (f32[96,384]{1,0:T(8,128)S(1)}, f32[96,384]{1,0:T(8,128)S(1)}, u32[]{:S(2)}, u32[]{:S(2)}) collective-permute-start(f32[96,384]{1,0:T(8,128)S(1)} %get-tuple-element.26), channel_id=1, source_target_pairs={{0,8},{1,9},{2,10},{3,11},{4,12},{5,13},{6,14},{7,15},{8,0},{9,1},... | collective-permute-start | bytes 442376 | tf_op jit(solution)/shard_map/ppermute | solution.py:18
  13.2 1.8 %collective-permute-start.22 = (bf16[192,1024]{1,0:T(8,128)(2,1)S(1)}, bf16[192,1024]{1,0:T(8,128)(2,1)S(1)}, u32[]{:S(2)}, u32[]{:S(2)}) collective-permute-start(bf16[192,1024]{1,0:T(8,128)(2,1)S(1)} %copy-done), channel_id=1, source_target_pairs={{0,2},{1,3},{2,0},{3,1},{4,6},{5,7},{6,4},{7,5},{8,10},{9,11},{10,... | collective-permute-start | bytes 1179656 | tf_op jit(solution)/shard_map/ppermute | solution.py:18
  15.3 2.8 %collective-permute-done.4 = f32[96,384]{1,0:T(8,128)S(1)} collective-permute-done((f32[96,384]{1,0:T(8,128)S(1)}, f32[96,384]{1,0:T(8,128)S(1)}, u32[]{:S(2)}, u32[]{:S(2)}) %collective-permute-start.4) | collective-permute-done | bytes 147488 | tf_op jit(solution)/shard_map/ppermute | solution.py:18
  18.1 1.5 %collective-permute-done.5 = f32[96,384]{1,0:T(8,128)S(1)} collective-permute-done((f32[96,384]{1,0:T(8,128)S(1)}, f32[96,384]{1,0:T(8,128)S(1)}, u32[]{:S(2)}, u32[]{:S(2)}) %collective-permute-start.5) | collective-permute-done | bytes 147488 | tf_op jit(solution)/shard_map/ppermute | solution.py:18
  19.6 2.7 %collective-permute-start.6 = (f32[96,384]{1,0:T(8,128)S(1)}, f32[96,384]{1,0:T(8,128)S(1)}, u32[]{:S(2)}, u32[]{:S(2)}) collective-permute-start(f32[96,384]{1,0:T(8,128)S(1)} %add_add_fusion), channel_id=1, source_target_pairs={{0,16},{1,17},{2,18},{3,19},{4,20},{5,21},{6,22},{7,23},{8,24},{9,... | collective-permute-start | bytes 442376 | tf_op jit(solution)/shard_map/ppermute | solution.py:18
  22.4 6.3 %collective-permute-done.6 = f32[96,384]{1,0:T(8,128)S(1)} collective-permute-done((f32[96,384]{1,0:T(8,128)S(1)}, f32[96,384]{1,0:T(8,128)S(1)}, u32[]{:S(2)}, u32[]{:S(2)}) %collective-permute-start.6) | collective-permute-done | bytes 147488 | tf_op jit(solution)/shard_map/ppermute | solution.py:18
  28.7 1.7 %collective-permute-start.20 = (f32[96,384]{1,0:T(8,128)S(1)}, f32[96,384]{1,0:T(8,128)S(1)}, u32[]{:S(2)}, u32[]{:S(2)}) collective-permute-start(f32[96,384]{1,0:T(8,128)S(1)} %add.24.refs_0_), channel_id=1, source_target_pairs={{0,14},{1,15},{2,12},{3,13},{4,10},{5,11},{6,8},{7,9},{8,6},{9,7},... | collective-permute-start | bytes 442376 | tf_op jit(solution)/shard_map/ppermute | solution.py:18
  30.4 2.3 %collective-permute-start.18 = (f32[96,384]{1,0:T(8,128)S(1)}, f32[96,384]{1,0:T(8,128)S(1)}, u32[]{:S(2)}, u32[]{:S(2)}) collective-permute-start(f32[96,384]{1,0:T(8,128)S(1)} %add.24.refs_0_), channel_id=1, source_target_pairs={{0,12},{1,13},{2,14},{3,15},{4,8},{5,9},{6,10},{7,11},{8,4},{9,5},... | collective-permute-start | bytes 442376 | tf_op jit(solution)/shard_map/ppermute | solution.py:18
  32.7 1.9 %collective-permute-start.14 = (f32[96,384]{1,0:T(8,128)S(1)}, f32[96,384]{1,0:T(8,128)S(1)}, u32[]{:S(2)}, u32[]{:S(2)}) collective-permute-start(f32[96,384]{1,0:T(8,128)S(1)} %add.24.refs_0_), channel_id=1, source_target_pairs={{0,8},{1,9},{2,10},{3,11},{4,12},{5,13},{6,14},{7,15},{8,0},{9,1},... | collective-permute-start | bytes 442376 | tf_op jit(solution)/shard_map/ppermute | solution.py:18
  34.6 1.5 %collective-permute-start.12 = (f32[96,384]{1,0:T(8,128)S(1)}, f32[96,384]{1,0:T(8,128)S(1)}, u32[]{:S(2)}, u32[]{:S(2)}) collective-permute-start(f32[96,384]{1,0:T(8,128)S(1)} %add.24.refs_0_), channel_id=1, source_target_pairs={{0,6},{1,7},{2,4},{3,5},{4,2},{5,3},{6,0},{7,1},{8,14},{9,15},{10,... | collective-permute-start | bytes 442376 | tf_op jit(solution)/shard_map/ppermute | solution.py:18
  36.1 1.2 %collective-permute-done.20.refs_14_ = f32[96,384]{1,0:T(8,128)S(1)} collective-permute-done((f32[96,384]{1,0:T(8,128)S(1)}, f32[96,384]{1,0:T(8,128)S(1)}, u32[]{:S(2)}, u32[]{:S(2)}) %collective-permute-start.20) | collective-permute-done | bytes 147488 | tf_op jit(solution)/shard_map/ppermute | solution.py:18
  37.6 2.9 %collective-permute-done.18.refs_12_ = f32[96,384]{1,0:T(8,128)S(1)} collective-permute-done((f32[96,384]{1,0:T(8,128)S(1)}, f32[96,384]{1,0:T(8,128)S(1)}, u32[]{:S(2)}, u32[]{:S(2)}) %collective-permute-start.18) | collective-permute-done | bytes 147488 | tf_op jit(solution)/shard_map/ppermute | solution.py:18
  41.0 2.0 %collective-permute-done.14.refs_8_ = f32[96,384]{1,0:T(8,128)S(1)} collective-permute-done((f32[96,384]{1,0:T(8,128)S(1)}, f32[96,384]{1,0:T(8,128)S(1)}, u32[]{:S(2)}, u32[]{:S(2)}) %collective-permute-start.14) | collective-permute-done | bytes 147488 | tf_op jit(solution)/shard_map/ppermute | solution.py:18
  43.5 2.6 %collective-permute-done.10.refs_4_ = f32[96,384]{1,0:T(8,128)S(1)} collective-permute-done((f32[96,384]{1,0:T(8,128)S(1)}, f32[96,384]{1,0:T(8,128)S(1)}, u32[]{:S(2)}, u32[]{:S(2)}) %collective-permute-start.10) | collective-permute-done | bytes 147488 | tf_op jit(solution)/shard_map/ppermute | solution.py:18
  49.0 16.3 %shard_map.52 = (f32[192,768]{1,0:T(8,128)}, f32[64,256]{1,0:T(8,128)S(1)}, f32[64,256]{1,0:T(8,128)S(1)}, f32[64,256]{1,0:T(8,128)S(1)}, f32[64,256]{1,0:T(8,128)S(1)}) custom-call(f32[96,384]{1,0:T(8,128)S(1)} %add.24.refs_0_, f32[96,384]{1,0:T(8,128)S(1)} %collective-permute-done.7.refs_1_, f32[96,384]{1,0:T(8,128)S(1)} %collective-permute-done.8.refs_2_, ...), custom_call_target="tpu_custom_call" | custom-call | tf_op jit(solution)/shard_map/pallas_call | solution.py:214
  65.4 1.2 %collective-permute-start.24 = (f32[64,256]{1,0:T(8,128)S(1)}, f32[64,256]{1,0:T(8,128)S(1)}, u32[]{:S(2)}, u32[]{:S(2)}) collective-permute-start(f32[64,256]{1,0:T(8,128)S(1)} %get-tuple-element.31), channel_id=1, source_target_pairs={{0,4},{1,5},{2,6},{3,7},{4,0},{5,1},{6,2},{7,3},{8,12},{9,13},{10,... | collective-permute-start | bytes 196616 | tf_op jit(solution)/shard_map/ppermute | solution.py:18
  67.2 1.8 %collective-permute-start.26 = (f32[64,256]{1,0:T(8,128)S(1)}, f32[64,256]{1,0:T(8,128)S(1)}, u32[]{:S(2)}, u32[]{:S(2)}) collective-permute-start(f32[64,256]{1,0:T(8,128)S(1)} %get-tuple-element.33), channel_id=1, source_target_pairs={{0,12},{1,13},{2,14},{3,15},{4,8},{5,9},{6,10},{7,11},{8,4},{9,5},... | collective-permute-start | bytes 196616 | tf_op jit(solution)/shard_map/ppermute | solution.py:18
  69.7 1.5 %collective-permute-done.25 = f32[64,256]{1,0:T(8,128)S(1)} collective-permute-done((f32[64,256]{1,0:T(8,128)S(1)}, f32[64,256]{1,0:T(8,128)S(1)}, u32[]{:S(2)}, u32[]{:S(2)}) %collective-permute-start.25) | collective-permute-done | bytes 65568 | tf_op jit(solution)/shard_map/ppermute | solution.py:18
  72.4 2.5 %collective-permute-start.27 = (f32[32,256]{1,0:T(8,128)S(1)}, f32[32,256]{1,0:T(8,128)S(1)}, u32[]{:S(2)}, u32[]{:S(2)}) collective-permute-start(f32[32,256]{1,0:T(8,128)S(1)} %get-tuple-element.34), channel_id=1, source_target_pairs={{0,16},{1,17},{2,18},{3,19},{4,20},{5,21},{6,22},{7,23},{8,24},{9,... | collective-permute-start | bytes 98312 | tf_op jit(solution)/shard_map/ppermute | solution.py:18
  74.9 2.4 %collective-permute-done.27.received = f32[32,256]{1,0:T(8,128)S(1)} collective-permute-done((f32[32,256]{1,0:T(8,128)S(1)}, f32[32,256]{1,0:T(8,128)S(1)}, u32[]{:S(2)}, u32[]{:S(2)}) %collective-permute-start.27) | collective-permute-done | bytes 32800 | tf_op jit(solution)/shard_map/ppermute | solution.py:18
  (42 shorter events, 9.7 us)
Async XLA Ops:
  0.6 3.2 %collective-permute-start = (bf16[192,1024]{1,0:T(8,128)(2,1)}, bf16[192,1024]{1,0:T(8,128)(2,1)S(1)}, u32[]{:S(2)}, u32[]{:S(2)}) collective-permute-start(bf16[192,1024]{1,0:T(8,128)(2,1)} %refs_17_.1), channel_id=1, source_target_pairs={{0,1},{1,0},{2,3},{3,2},{4,5},{5,4},{6,7},{7,6},{8,9},{9,8},{10,11... | collective-permute-start | bytes 1179656 | tf_op jit(solution)/shard_map/ppermute | solution.py:18
  1.1 7.6 %collective-permute-start.2 = (bf16[192,256]{1,0:T(8,128)(2,1)}, bf16[192,256]{1,0:T(8,128)(2,1)S(1)}, u32[]{:S(2)}, u32[]{:S(2)}) collective-permute-start(bf16[192,256]{1,0:T(8,128)(2,1)} %bitcast.1), channel_id=1, source_target_pairs={{0,2},{1,3},{2,0},{3,1},{4,6},{5,7},{6,4},{7,5},{8,10},{9,11},{10,... | collective-permute-start | bytes 294920 | tf_op jit(solution)/shard_map/ppermute | solution.py:18
  3.7 5.0 %collective-permute-start.1 = (s32[16,1024]{1,0:T(8,128)}, s32[16,1024]{1,0:T(8,128)S(1)}, u32[]{:S(2)}, u32[]{:S(2)}) collective-permute-start(s32[16,1024]{1,0:T(8,128)} %refs_16_.1), channel_id=1, source_target_pairs={{0,2},{1,3},{2,0},{3,1},{4,6},{5,7},{6,4},{7,5},{8,10},{9,11},{10,... | collective-permute-start | bytes 196616 | tf_op jit(solution)/shard_map/ppermute | solution.py:18
  9.6 5.7 %collective-permute-start.3 = (f32[96,384]{1,0:T(8,128)S(1)}, f32[96,384]{1,0:T(8,128)S(1)}, u32[]{:S(2)}, u32[]{:S(2)}) collective-permute-start(f32[96,384]{1,0:T(8,128)S(1)} %get-tuple-element.25), channel_id=1, source_target_pairs={{0,4},{1,5},{2,6},{3,7},{4,0},{5,1},{6,2},{7,3},{8,12},{9,13},{10,... | collective-permute-start | bytes 442376 | tf_op jit(solution)/shard_map/ppermute | solution.py:18
  11.4 6.7 %collective-permute-start.4 = (f32[96,384]{1,0:T(8,128)S(1)}, f32[96,384]{1,0:T(8,128)S(1)}, u32[]{:S(2)}, u32[]{:S(2)}) collective-permute-start(f32[96,384]{1,0:T(8,128)S(1)} %get-tuple-element.26), channel_id=1, source_target_pairs={{0,8},{1,9},{2,10},{3,11},{4,12},{5,13},{6,14},{7,15},{8,0},{9,1},... | collective-permute-start | bytes 442376 | tf_op jit(solution)/shard_map/ppermute | solution.py:18
  13.0 6.6 %collective-permute-start.5 = (f32[96,384]{1,0:T(8,128)S(1)}, f32[96,384]{1,0:T(8,128)S(1)}, u32[]{:S(2)}, u32[]{:S(2)}) collective-permute-start(f32[96,384]{1,0:T(8,128)S(1)} %get-tuple-element.27), channel_id=1, source_target_pairs={{0,12},{1,13},{2,14},{3,15},{4,8},{5,9},{6,10},{7,11},{8,4},{9,5},... | collective-permute-start | bytes 442376 | tf_op jit(solution)/shard_map/ppermute | solution.py:18
  13.2 21.4 %collective-permute-start.22 = (bf16[192,1024]{1,0:T(8,128)(2,1)S(1)}, bf16[192,1024]{1,0:T(8,128)(2,1)S(1)}, u32[]{:S(2)}, u32[]{:S(2)}) collective-permute-start(bf16[192,1024]{1,0:T(8,128)(2,1)S(1)} %copy-done), channel_id=1, source_target_pairs={{0,2},{1,3},{2,0},{3,1},{4,6},{5,7},{6,4},{7,5},{8,10},{9,11},{10,... | collective-permute-start | bytes 1179656 | tf_op jit(solution)/shard_map/ppermute | solution.py:18
  19.6 9.0 %collective-permute-start.6 = (f32[96,384]{1,0:T(8,128)S(1)}, f32[96,384]{1,0:T(8,128)S(1)}, u32[]{:S(2)}, u32[]{:S(2)}) collective-permute-start(f32[96,384]{1,0:T(8,128)S(1)} %add_add_fusion), channel_id=1, source_target_pairs={{0,16},{1,17},{2,18},{3,19},{4,20},{5,21},{6,22},{7,23},{8,24},{9,... | collective-permute-start | bytes 442376 | tf_op jit(solution)/shard_map/ppermute | solution.py:18
  28.7 8.7 %collective-permute-start.20 = (f32[96,384]{1,0:T(8,128)S(1)}, f32[96,384]{1,0:T(8,128)S(1)}, u32[]{:S(2)}, u32[]{:S(2)}) collective-permute-start(f32[96,384]{1,0:T(8,128)S(1)} %add.24.refs_0_), channel_id=1, source_target_pairs={{0,14},{1,15},{2,12},{3,13},{4,10},{5,11},{6,8},{7,9},{8,6},{9,7},... | collective-permute-start | bytes 442376 | tf_op jit(solution)/shard_map/ppermute | solution.py:18
  30.4 10.2 %collective-permute-start.18 = (f32[96,384]{1,0:T(8,128)S(1)}, f32[96,384]{1,0:T(8,128)S(1)}, u32[]{:S(2)}, u32[]{:S(2)}) collective-permute-start(f32[96,384]{1,0:T(8,128)S(1)} %add.24.refs_0_), channel_id=1, source_target_pairs={{0,12},{1,13},{2,14},{3,15},{4,8},{5,9},{6,10},{7,11},{8,4},{9,5},... | collective-permute-start | bytes 442376 | tf_op jit(solution)/shard_map/ppermute | solution.py:18
  32.7 8.3 %collective-permute-start.16 = (f32[96,384]{1,0:T(8,128)S(1)}, f32[96,384]{1,0:T(8,128)S(1)}, u32[]{:S(2)}, u32[]{:S(2)}) collective-permute-start(f32[96,384]{1,0:T(8,128)S(1)} %add.24.refs_0_), channel_id=1, source_target_pairs={{0,10},{1,11},{2,8},{3,9},{4,14},{5,15},{6,12},{7,13},{8,2},{9,3},... | collective-permute-start | bytes 442376 | tf_op jit(solution)/shard_map/ppermute | solution.py:18
  32.7 10.3 %collective-permute-start.14 = (f32[96,384]{1,0:T(8,128)S(1)}, f32[96,384]{1,0:T(8,128)S(1)}, u32[]{:S(2)}, u32[]{:S(2)}) collective-permute-start(f32[96,384]{1,0:T(8,128)S(1)} %add.24.refs_0_), channel_id=1, source_target_pairs={{0,8},{1,9},{2,10},{3,11},{4,12},{5,13},{6,14},{7,15},{8,0},{9,1},... | collective-permute-start | bytes 442376 | tf_op jit(solution)/shard_map/ppermute | solution.py:18
  34.6 8.6 %collective-permute-start.12 = (f32[96,384]{1,0:T(8,128)S(1)}, f32[96,384]{1,0:T(8,128)S(1)}, u32[]{:S(2)}, u32[]{:S(2)}) collective-permute-start(f32[96,384]{1,0:T(8,128)S(1)} %add.24.refs_0_), channel_id=1, source_target_pairs={{0,6},{1,7},{2,4},{3,5},{4,2},{5,3},{6,0},{7,1},{8,14},{9,15},{10,... | collective-permute-start | bytes 442376 | tf_op jit(solution)/shard_map/ppermute | solution.py:18
  37.3 8.7 %collective-permute-start.10 = (f32[96,384]{1,0:T(8,128)S(1)}, f32[96,384]{1,0:T(8,128)S(1)}, u32[]{:S(2)}, u32[]{:S(2)}) collective-permute-start(f32[96,384]{1,0:T(8,128)S(1)} %add.24.refs_0_), channel_id=1, source_target_pairs={{0,4},{1,5},{2,6},{3,7},{4,0},{5,1},{6,2},{7,3},{8,12},{9,13},{10,... | collective-permute-start | bytes 442376 | tf_op jit(solution)/shard_map/ppermute | solution.py:18
  40.6 5.5 %collective-permute-start.8 = (f32[96,384]{1,0:T(8,128)S(1)}, f32[96,384]{1,0:T(8,128)S(1)}, u32[]{:S(2)}, u32[]{:S(2)}) collective-permute-start(f32[96,384]{1,0:T(8,128)S(1)} %add.24.refs_0_), channel_id=1, source_target_pairs={{0,2},{1,3},{2,0},{3,1},{4,6},{5,7},{6,4},{7,5},{8,10},{9,11},{10,... | collective-permute-start | bytes 442376 | tf_op jit(solution)/shard_map/ppermute | solution.py:18
  41.0 8.0 %collective-permute-start.23 = (bf16[192,1024]{1,0:T(8,128)(2,1)S(1)}, bf16[192,1024]{1,0:T(8,128)(2,1)S(1)}, u32[]{:S(2)}, u32[]{:S(2)}) collective-permute-start(bf16[192,1024]{1,0:T(8,128)(2,1)S(1)} %collective-permute-done.22.refs_19_), channel_id=1, source_target_pairs={{0,1},{1,0},{2,3},{3,2},{4,5},{5,4},{6,7},{7,6},{8,9},{9,8},{10,11... | collective-permute-start | bytes 1179656 | tf_op jit(solution)/shard_map/ppermute | solution.py:18
  43.0 3.6 %collective-permute-start.7 = (f32[96,384]{1,0:T(8,128)S(1)}, f32[96,384]{1,0:T(8,128)S(1)}, u32[]{:S(2)}, u32[]{:S(2)}) collective-permute-start(f32[96,384]{1,0:T(8,128)S(1)} %add.24.refs_0_), channel_id=1, source_target_pairs={{0,1},{1,0},{2,3},{3,2},{4,5},{5,4},{6,7},{7,6},{8,9},{9,8},{10,11... | collective-permute-start | bytes 442376 | tf_op jit(solution)/shard_map/ppermute | solution.py:18
  43.2 3.5 %collective-permute-start.21 = (f32[96,384]{1,0:T(8,128)S(1)}, f32[96,384]{1,0:T(8,128)S(1)}, u32[]{:S(2)}, u32[]{:S(2)}) collective-permute-start(f32[96,384]{1,0:T(8,128)S(1)} %collective-permute-done.20.refs_14_), channel_id=1, source_target_pairs={{0,1},{1,0},{2,3},{3,2},{4,5},{5,4},{6,7},{7,6},{8,9},{9,8},{10,11... | collective-permute-start | bytes 442376 | tf_op jit(solution)/shard_map/ppermute | solution.py:18
  46.1 1.6 %collective-permute-start.17 = (f32[96,384]{1,0:T(8,128)S(1)}, f32[96,384]{1,0:T(8,128)S(1)}, u32[]{:S(2)}, u32[]{:S(2)}) collective-permute-start(f32[96,384]{1,0:T(8,128)S(1)} %collective-permute-done.16.refs_10_), channel_id=1, source_target_pairs={{0,1},{1,0},{2,3},{3,2},{4,5},{5,4},{6,7},{7,6},{8,9},{9,8},{10,11... | collective-permute-start | bytes 442376 | tf_op jit(solution)/shard_map/ppermute | solution.py:18
  46.7 1.5 %collective-permute-start.13 = (f32[96,384]{1,0:T(8,128)S(1)}, f32[96,384]{1,0:T(8,128)S(1)}, u32[]{:S(2)}, u32[]{:S(2)}) collective-permute-start(f32[96,384]{1,0:T(8,128)S(1)} %collective-permute-done.12.refs_6_), channel_id=1, source_target_pairs={{0,1},{1,0},{2,3},{3,2},{4,5},{5,4},{6,7},{7,6},{8,9},{9,8},{10,11... | collective-permute-start | bytes 442376 | tf_op jit(solution)/shard_map/ppermute | solution.py:18
  65.4 4.3 %collective-permute-start.24 = (f32[64,256]{1,0:T(8,128)S(1)}, f32[64,256]{1,0:T(8,128)S(1)}, u32[]{:S(2)}, u32[]{:S(2)}) collective-permute-start(f32[64,256]{1,0:T(8,128)S(1)} %get-tuple-element.31), channel_id=1, source_target_pairs={{0,4},{1,5},{2,6},{3,7},{4,0},{5,1},{6,2},{7,3},{8,12},{9,13},{10,... | collective-permute-start | bytes 196616 | tf_op jit(solution)/shard_map/ppermute | solution.py:18
  66.6 4.6 %collective-permute-start.25 = (f32[64,256]{1,0:T(8,128)S(1)}, f32[64,256]{1,0:T(8,128)S(1)}, u32[]{:S(2)}, u32[]{:S(2)}) collective-permute-start(f32[64,256]{1,0:T(8,128)S(1)} %get-tuple-element.32), channel_id=1, source_target_pairs={{0,8},{1,9},{2,10},{3,11},{4,12},{5,13},{6,14},{7,15},{8,0},{9,1},... | collective-permute-start | bytes 196616 | tf_op jit(solution)/shard_map/ppermute | solution.py:18
  67.2 5.2 %collective-permute-start.26 = (f32[64,256]{1,0:T(8,128)S(1)}, f32[64,256]{1,0:T(8,128)S(1)}, u32[]{:S(2)}, u32[]{:S(2)}) collective-permute-start(f32[64,256]{1,0:T(8,128)S(1)} %get-tuple-element.33), channel_id=1, source_target_pairs={{0,12},{1,13},{2,14},{3,15},{4,8},{5,9},{6,10},{7,11},{8,4},{9,5},... | collective-permute-start | bytes 196616 | tf_op jit(solution)/shard_map/ppermute | solution.py:18
  72.4 4.9 %collective-permute-start.27 = (f32[32,256]{1,0:T(8,128)S(1)}, f32[32,256]{1,0:T(8,128)S(1)}, u32[]{:S(2)}, u32[]{:S(2)}) collective-permute-start(f32[32,256]{1,0:T(8,128)S(1)} %get-tuple-element.34), channel_id=1, source_target_pairs={{0,16},{1,17},{2,18},{3,19},{4,20},{5,21},{6,22},{7,23},{8,24},{9,... | collective-permute-start | bytes 98312 | tf_op jit(solution)/shard_map/ppermute | solution.py:18
  (5 other events, 9.9 us)

commit v4 on v3

--- a/solution.py
+++ b/solution.py
@@ -10,12 +10,21 @@
 NS_STEPS = 4
 DIMS = 4
 LANES = 128
+TAIL = 16
+TINY = 1e-30
+ROUNDS = ((4, 8), (2, 12), (10, 6))
+LAST = 14
 VMEM_LIMIT = 56 * 1024 * 1024
 
 
 def swap(value, mask):
     count = lax.axis_size("dp") * lax.axis_size("dim")
     return lax.ppermute(value, ("dp", "dim"), [(i, i ^ mask) for i in range(count)])
+
+
+def swap_by_core(value, one, two):
+    count = lax.axis_size("dp") * lax.axis_size("dim")
+    return lax.ppermute(value, ("dp", "dim"), [(i, i ^ (two if i & 1 else one)) for i in range(count)])
 
 
 def place():
@@ -91,6 +100,30 @@
         out[...] = both[pl.ds(pl.multiple_of((quarter ^ k) * thin, 8), thin), :]
 
 
+def code_kernel(kept, received, kept_other, received_other, both, mine):
+    core, _, _, _ = place()
+    count = kept.shape[0]
+    for k, (one, two) in enumerate(((kept, received), (kept_other, received_other))):
+        total = one[...] + two[...]
+        top = jnp.maximum(jnp.max(jnp.abs(total), axis=0, keepdims=True), TINY)
+        exponent = jnp.ceil(jnp.log2(top))
+        scaled = jnp.round(total * jnp.exp2(15.0 - exponent))
+        coded = jnp.clip(scaled, -32767.0, 32767.0).astype(jnp.int32).astype(jnp.int16)
+        tail = jnp.broadcast_to(exponent, (TAIL, total.shape[1])).astype(jnp.int32).astype(jnp.int16)
+        first = pl.multiple_of((core ^ k) * (count + TAIL), TAIL)
+        both[pl.ds(first, count), :] = coded
+        both[pl.ds(pl.multiple_of(first + count, TAIL), TAIL), :] = tail
+        if k == 0:
+            mine[:count, :] = coded
+            mine[count:, :] = tail
+
+
+def decoded_piece(ref, first, count):
+    exponent = ref[first + count : first + count + TAIL, :].astype(jnp.int32).astype(jnp.float32)[:1]
+    coded = ref[first : first + count, :].astype(jnp.int32).astype(jnp.float32)
+    return coded * jnp.exp2(exponent - 15.0)
+
+
 def gram_blocks(size, high, low, whole, write):
     count = high.shape[0] // size
     for i in range(count):
@@ -107,12 +140,12 @@
 
 
 def refit_kernel(sub_width, *refs):
-    pieces, codes, sources = refs[:16], refs[16], refs[17:21]
-    rotation_out, outs = refs[21], refs[22:26]
-    current, halves, gram, vectors, rotated, total, arrived = refs[26:]
+    pairs, singles, codes, sources = refs[:7], refs[7:9], refs[9], refs[10:14]
+    rotation_out, outs = refs[14], refs[15:19]
+    current, halves, gram, vectors, rotated, total, arrived = refs[19:]
     core, pair, quarter, high_part = place()
     dp_count = lax.axis_size("dp")
-    thin, half = pieces[0].shape
+    thin, half = singles[0].shape[0] - TAIL, singles[0].shape[1]
     width, size = 2 * thin, current.shape[0]
     block = 2 * LANES
     own = (pair * 2 + core) * width
@@ -123,11 +156,19 @@
         rows = pl.ds(pl.multiple_of(at, 16), width)
         copies.append(pltpu.make_async_copy(source, vectors.at[rows, :], arrived.at[k]))
         copies[k].start()
-    for mask, piece in enumerate(pieces):
-        c, p, q = core ^ (mask & 1), pair ^ (mask >> 1 & 1), quarter ^ (mask >> 2)
+
+    def place_piece(mask, c, ref, first):
+        p, q = pair ^ (mask >> 1 & 1), quarter ^ (mask >> 2)
         row = ((q >> 1) * 2 + c) * width + (q & 1) * thin
         rows, columns = pl.ds(pl.multiple_of(row, 8), thin), pl.ds(pl.multiple_of(p * half, LANES), half)
-        current[rows, columns] = piece[...]
+        current[rows, columns] = decoded_piece(ref, first, thin)
+
+    masks = [0] + [jnp.where(core == c, one, two) for c in (0, 1) for one, two in ROUNDS]
+    for mask, ref in zip(masks, pairs):
+        for c in (0, 1):
+            place_piece(mask, c, ref, c * (thin + TAIL))
+    for k, ref in enumerate(singles):
+        place_piece(LAST, core ^ k, ref, 0)
     squares = jnp.zeros((8, size), jnp.float32)
     for row in range(0, size, 8):
         value = current[row : row + 8, :]
@@ -253,12 +294,19 @@
     vectors_last = swap(vectors_pair, 1)
 
     piece = held[0] + swap(held[1], 4) + swap(held[2], 8) + swap(held[3], 12)
-    for mask in high_masks:
+    for mask in high_masks[:-1]:
         piece = piece + swap(piece, mask)
-    pieces = [piece if mask == 0 else swap(piece, mask) for mask in range(0, 16, 2)]
-    both = []
-    for own in pieces:
-        both += [own, swap(own, 1)]
+    received = swap(piece, high_masks[-1])
+    own_pair, own_piece = call(
+        code_kernel,
+        [pltpu.VMEM((2 * (thin + TAIL), half), jnp.int16), pltpu.VMEM((thin + TAIL, half), jnp.int16)],
+        [],
+        0,
+        *map(near, (piece, received, swap(piece, 1), swap(received, 1))),
+    )
+    pairs = [swap_by_core(own_pair, one, two) for one, two in ROUNDS]
+    last = swap(own_piece, LAST)
+    gathered = [own_pair, *pairs, *(swap(pair, 1) for pair in pairs), last, swap(last, 1)]
 
     columns = width + sub_count
     columns += -columns % LANES
@@ -275,7 +323,7 @@
             pltpu.SemaphoreType.DMA((4,)),
         ],
         4,
-        *map(near, both), codes, vectors, near(vectors_core), near(vectors_pair), near(vectors_last),
+        *map(near, gathered), codes, vectors, near(vectors_core), near(vectors_pair), near(vectors_last),
     )
     held = sums[0] + swap(sums[1], 4) + swap(sums[2], 8) + swap(sums[3], 12)
     received = jnp.zeros_like(held)

time: 78.3 us -> 72.4 us (0.925)
  waiting for transfers between devices: 30.2 us -> 25.8 us
  starting transfers between devices: 27.3 us -> 25.6 us
    ppermute x28 -> x20, waiting for transfers between devices: 30.2 us -> 21.6 us  [swap(): lax.ppermute(value, ('dp', 'dim'), [(i, i ^ mask) for i in range(count)])]
    ppermute x28 -> x20, starting transfers between devices: 27.3 us -> 22.8 us  [swap(): lax.ppermute(value, ('dp', 'dim'), [(i, i ^ mask) for i in range(count)])]
    ppermute x0 -> x3, waiting for transfers between devices: none -> 4.23 us  [swap_by_core(): lax.ppermute(value, ('dp', 'dim'), [(i, i ^ (two if i & 1 else one)) for...]
    ppermute x0 -> x3, starting transfers between devices: none -> 2.76 us  [swap_by_core(): lax.ppermute(value, ('dp', 'dim'), [(i, i ^ (two if i & 1 else one)) for...]
    pallas_call x4 -> x5, Pallas kernels: 19.9 us -> 20.1 us  [call(): pl.pallas_call(kernel, out_shape=outs, in_specs=[pl.BlockSpec(memory_spac...]
  transfers between devices with their start and end apart: 28 -> 23, of which waited for: 19 -> 14; matrix products, arithmetic and copies ran while one was open for 0% -> 0% of each run, Pallas kernels for 2% -> 3%
where the time goes in v4:
time: 72.4 us; the launch traced here: 72.3 us
  waiting for transfers between devices  25.8 us (36%)
  starting transfers between devices  25.6 us (35%)
  Pallas kernels  20.1 us (28%)
    ppermute x20, starting transfers between devices, swap(): lax.ppermute(value, ('dp', 'dim'), [(i, i ^ mask) for i in range(count)])  22.8 us
    ppermute x20, waiting for transfers between devices, swap(): lax.ppermute(value, ('dp', 'dim'), [(i, i ^ mask) for i in range(count)])  21.6 us
    pallas_call x5, Pallas kernels, call(): pl.pallas_call(kernel, out_shape=outs, in_specs=[pl.BlockSpec(memory_spac...  20.1 us
    ppermute x3, waiting for transfers between devices, swap_by_core(): lax.ppermute(value, ('dp', 'dim'), [(i, i ^ (two if i & 1 else one)) for...  4.23 us
    ppermute x3, starting transfers between devices, swap_by_core(): lax.ppermute(value, ('dp', 'dim'), [(i, i ^ (two if i & 1 else one)) for...  2.76 us
  transfers between devices with their start and end apart: 23, of which 14 were waited for; matrix products, arithmetic and copies ran while one was open for 0% of the time, Pallas kernels for 3%

profile of v4, /device:TPU:0, one launch (start us, length us, event | category | flops | bytes accessed | tf_op | source)
XLA Modules:
  0.0 72.3 jit_solution(14133544750863235610)
XLA Ops:
  1.1 2.6 %collective-permute-start.2 = (bf16[192,256]{1,0:T(8,128)(2,1)}, bf16[192,256]{1,0:T(8,128)(2,1)S(1)}, u32[]{:S(2)}, u32[]{:S(2)}) collective-permute-start(bf16[192,256]{1,0:T(8,128)(2,1)} %bitcast.1), channel_id=1, source_target_pairs={{0,2},{1,3},{2,0},{3,1},{4,6},{5,7},{6,4},{7,5},{8,10},{9,11},{10,... | collective-permute-start | bytes 294920 | tf_op jit(solution)/shard_map/ppermute | solution.py:22
  3.8 1.9 %shard_map.50 = (f32[192,384]{1,0:T(8,128)S(1)}, bf16[384,1024]{1,0:T(8,128)(2,1)S(1)}) custom-call(bf16[192,1024]{1,0:T(8,128)(2,1)} %refs_10_.1, bf16[192,1024]{1,0:T(8,128)(2,1)S(1)} %collective-permute-done.v1.refs_11_, s32[16,1024]{1,0:T(8,128)} %refs_9_.1, bf16[192,256]{1,0:T(8,128)(2,1)} %bitcast.2), custom_call_target="tpu_custom_call" | custom-call | tf_op jit(solution)/shard_map/pallas_call | solution.py:255
  5.7 3.0 %collective-permute-done.1.codes = s32[16,1024]{1,0:T(8,128)S(1)} collective-permute-done((s32[16,1024]{1,0:T(8,128)}, s32[16,1024]{1,0:T(8,128)S(1)}, u32[]{:S(2)}, u32[]{:S(2)}) %collective-permute-start.1) | collective-permute-done | bytes 65568 | tf_op jit(solution)/shard_map/ppermute | solution.py:22
  9.6 1.8 %collective-permute-start.3 = (f32[96,384]{1,0:T(8,128)S(1)}, f32[96,384]{1,0:T(8,128)S(1)}, u32[]{:S(2)}, u32[]{:S(2)}) collective-permute-start(f32[96,384]{1,0:T(8,128)S(1)} %get-tuple-element.27), channel_id=1, source_target_pairs={{0,4},{1,5},{2,6},{3,7},{4,0},{5,1},{6,2},{7,3},{8,12},{9,13},{10,... | collective-permute-start | bytes 442376 | tf_op jit(solution)/shard_map/ppermute | solution.py:22
  11.4 1.6 %collective-permute-start.4 = (f32[96,384]{1,0:T(8,128)S(1)}, f32[96,384]{1,0:T(8,128)S(1)}, u32[]{:S(2)}, u32[]{:S(2)}) collective-permute-start(f32[96,384]{1,0:T(8,128)S(1)} %get-tuple-element.28), channel_id=1, source_target_pairs={{0,8},{1,9},{2,10},{3,11},{4,12},{5,13},{6,14},{7,15},{8,0},{9,1},... | collective-permute-start | bytes 442376 | tf_op jit(solution)/shard_map/ppermute | solution.py:22
  13.2 1.8 %collective-permute-start.17 = (bf16[192,1024]{1,0:T(8,128)(2,1)S(1)}, bf16[192,1024]{1,0:T(8,128)(2,1)S(1)}, u32[]{:S(2)}, u32[]{:S(2)}) collective-permute-start(bf16[192,1024]{1,0:T(8,128)(2,1)S(1)} %copy-done), channel_id=1, source_target_pairs={{0,2},{1,3},{2,0},{3,1},{4,6},{5,7},{6,4},{7,5},{8,10},{9,11},{10,... | collective-permute-start | bytes 1179656 | tf_op jit(solution)/shard_map/ppermute | solution.py:22
  15.3 2.8 %collective-permute-done.4 = f32[96,384]{1,0:T(8,128)S(1)} collective-permute-done((f32[96,384]{1,0:T(8,128)S(1)}, f32[96,384]{1,0:T(8,128)S(1)}, u32[]{:S(2)}, u32[]{:S(2)}) %collective-permute-start.4) | collective-permute-done | bytes 147488 | tf_op jit(solution)/shard_map/ppermute | solution.py:22
  18.1 1.5 %collective-permute-done.5 = f32[96,384]{1,0:T(8,128)S(1)} collective-permute-done((f32[96,384]{1,0:T(8,128)S(1)}, f32[96,384]{1,0:T(8,128)S(1)}, u32[]{:S(2)}, u32[]{:S(2)}) %collective-permute-start.5) | collective-permute-done | bytes 147488 | tf_op jit(solution)/shard_map/ppermute | solution.py:22
  19.7 2.7 %collective-permute-start.6 = (f32[96,384]{1,0:T(8,128)S(1)}, f32[96,384]{1,0:T(8,128)S(1)}, u32[]{:S(2)}, u32[]{:S(2)}) collective-permute-start(f32[96,384]{1,0:T(8,128)S(1)} %add_add_fusion.kept), channel_id=1, source_target_pairs={{0,16},{1,17},{2,18},{3,19},{4,20},{5,21},{6,22},{7,23},{8,24},{9,... | collective-permute-start | bytes 442376 | tf_op jit(solution)/shard_map/ppermute | solution.py:22
  22.4 6.3 %collective-permute-done.6.received = f32[96,384]{1,0:T(8,128)S(1)} collective-permute-done((f32[96,384]{1,0:T(8,128)S(1)}, f32[96,384]{1,0:T(8,128)S(1)}, u32[]{:S(2)}, u32[]{:S(2)}) %collective-permute-start.6) | collective-permute-done | bytes 147488 | tf_op jit(solution)/shard_map/ppermute | solution.py:22
  30.1 0.9 %collective-permute-start.11 = (s16[224,384]{1,0:T(8,128)(2,1)S(1)}, s16[224,384]{1,0:T(8,128)(2,1)S(1)}, u32[]{:S(2)}, u32[]{:S(2)}) collective-permute-start(s16[224,384]{1,0:T(8,128)(2,1)S(1)} %get-tuple-element.30.refs_0_), channel_id=1, source_target_pairs={{0,10},{1,7},{2,8},{3,5},{4,14},{5,3},{6,12},{7,1},{8,2},{9,15},{1... | collective-permute-start | bytes 516104 | tf_op jit(solution)/shard_map/ppermute | solution.py:27
  31.8 1.1 %collective-permute-start.9 = (s16[224,384]{1,0:T(8,128)(2,1)S(1)}, s16[224,384]{1,0:T(8,128)(2,1)S(1)}, u32[]{:S(2)}, u32[]{:S(2)}) collective-permute-start(s16[224,384]{1,0:T(8,128)(2,1)S(1)} %get-tuple-element.30.refs_0_), channel_id=1, source_target_pairs={{0,4},{1,9},{2,6},{3,11},{4,0},{5,13},{6,2},{7,15},{8,12},{9,1},{1... | collective-permute-start | bytes 516104 | tf_op jit(solution)/shard_map/ppermute | solution.py:27
  32.9 3.2 %collective-permute-start.15 = (s16[112,384]{1,0:T(8,128)(2,1)S(1)}, s16[112,384]{1,0:T(8,128)(2,1)S(1)}, u32[]{:S(2)}, u32[]{:S(2)}) collective-permute-start(s16[112,384]{1,0:T(8,128)(2,1)S(1)} %get-tuple-element.31), channel_id=1, source_target_pairs={{0,14},{1,15},{2,12},{3,13},{4,10},{5,11},{6,8},{7,9},{8,6},{9,7},... | collective-permute-start | bytes 258056 | tf_op jit(solution)/shard_map/ppermute | solution.py:22
  36.1 2.0 %collective-permute-done.11.refs_3_ = s16[224,384]{1,0:T(8,128)(2,1)S(1)} collective-permute-done((s16[224,384]{1,0:T(8,128)(2,1)S(1)}, s16[224,384]{1,0:T(8,128)(2,1)S(1)}, u32[]{:S(2)}, u32[]{:S(2)}) %collective-permute-start.11) | collective-permute-done | bytes 172064 | tf_op jit(solution)/shard_map/ppermute | solution.py:27
  38.1 2.2 %collective-permute-done.10.refs_2_ = s16[224,384]{1,0:T(8,128)(2,1)S(1)} collective-permute-done((s16[224,384]{1,0:T(8,128)(2,1)S(1)}, s16[224,384]{1,0:T(8,128)(2,1)S(1)}, u32[]{:S(2)}, u32[]{:S(2)}) %collective-permute-start.10) | collective-permute-done | bytes 172064 | tf_op jit(solution)/shard_map/ppermute | solution.py:27
  41.9 0.9 %collective-permute-done.16.refs_8_ = s16[112,384]{1,0:T(8,128)(2,1)S(1)} collective-permute-done((s16[112,384]{1,0:T(8,128)(2,1)S(1)}, s16[112,384]{1,0:T(8,128)(2,1)S(1)}, u32[]{:S(2)}, u32[]{:S(2)}) %collective-permute-start.16) | collective-permute-done | bytes 86048 | tf_op jit(solution)/shard_map/ppermute | solution.py:22
  42.8 16.4 %shard_map.53 = (f32[192,768]{1,0:T(8,128)}, f32[64,256]{1,0:T(8,128)S(1)}, f32[64,256]{1,0:T(8,128)S(1)}, f32[64,256]{1,0:T(8,128)S(1)}, f32[64,256]{1,0:T(8,128)S(1)}) custom-call(s16[224,384]{1,0:T(8,128)(2,1)S(1)} %get-tuple-element.30.refs_0_, s16[224,384]{1,0:T(8,128)(2,1)S(1)} %collective-permute-done.9.refs_1_, ...), custom_call_target="tpu_custom_call" | custom-call | tf_op jit(solution)/shard_map/pallas_call | solution.py:255
  59.3 1.5 %collective-permute-start.19 = (f32[64,256]{1,0:T(8,128)S(1)}, f32[64,256]{1,0:T(8,128)S(1)}, u32[]{:S(2)}, u32[]{:S(2)}) collective-permute-start(f32[64,256]{1,0:T(8,128)S(1)} %get-tuple-element.35), channel_id=1, source_target_pairs={{0,4},{1,5},{2,6},{3,7},{4,0},{5,1},{6,2},{7,3},{8,12},{9,13},{10,... | collective-permute-start | bytes 196616 | tf_op jit(solution)/shard_map/ppermute | solution.py:22
  60.9 1.9 %collective-permute-start.21 = (f32[64,256]{1,0:T(8,128)S(1)}, f32[64,256]{1,0:T(8,128)S(1)}, u32[]{:S(2)}, u32[]{:S(2)}) collective-permute-start(f32[64,256]{1,0:T(8,128)S(1)} %get-tuple-element.37), channel_id=1, source_target_pairs={{0,12},{1,13},{2,14},{3,15},{4,8},{5,9},{6,10},{7,11},{8,4},{9,5},... | collective-permute-start | bytes 196616 | tf_op jit(solution)/shard_map/ppermute | solution.py:22
  63.7 1.9 %collective-permute-done.20 = f32[64,256]{1,0:T(8,128)S(1)} collective-permute-done((f32[64,256]{1,0:T(8,128)S(1)}, f32[64,256]{1,0:T(8,128)S(1)}, u32[]{:S(2)}, u32[]{:S(2)}) %collective-permute-start.20) | collective-permute-done | bytes 65568 | tf_op jit(solution)/shard_map/ppermute | solution.py:22
  65.6 0.9 %collective-permute-done.21 = f32[64,256]{1,0:T(8,128)S(1)} collective-permute-done((f32[64,256]{1,0:T(8,128)S(1)}, f32[64,256]{1,0:T(8,128)S(1)}, u32[]{:S(2)}, u32[]{:S(2)}) %collective-permute-start.21) | collective-permute-done | bytes 65568 | tf_op jit(solution)/shard_map/ppermute | solution.py:22
  66.5 2.8 %collective-permute-start.22 = (f32[32,256]{1,0:T(8,128)S(1)}, f32[32,256]{1,0:T(8,128)S(1)}, u32[]{:S(2)}, u32[]{:S(2)}) collective-permute-start(f32[32,256]{1,0:T(8,128)S(1)} %get-tuple-element.38), channel_id=1, source_target_pairs={{0,16},{1,17},{2,18},{3,19},{4,20},{5,21},{6,22},{7,23},{8,24},{9,... | collective-permute-start | bytes 98312 | tf_op jit(solution)/shard_map/ppermute | solution.py:22
  69.3 2.1 %collective-permute-done.22.received = f32[32,256]{1,0:T(8,128)S(1)} collective-permute-done((f32[32,256]{1,0:T(8,128)S(1)}, f32[32,256]{1,0:T(8,128)S(1)}, u32[]{:S(2)}, u32[]{:S(2)}) %collective-permute-start.22) | collective-permute-done | bytes 32800 | tf_op jit(solution)/shard_map/ppermute | solution.py:22
  71.4 0.9 %shard_map.54 = f32[32,192]{1,0:T(8,128)} custom-call(f32[32,256]{1,0:T(8,128)S(1)} %get-tuple-element.39.kept, f32[32,256]{1,0:T(8,128)S(1)} %collective-permute-done.22.received), custom_call_target="tpu_custom_call" | custom-call | tf_op jit(solution)/shard_map/pallas_call | solution.py:255
  (32 shorter events, 6.8 us)
Async XLA Ops:
  0.6 3.2 %collective-permute-start = (bf16[192,1024]{1,0:T(8,128)(2,1)}, bf16[192,1024]{1,0:T(8,128)(2,1)S(1)}, u32[]{:S(2)}, u32[]{:S(2)}) collective-permute-start(bf16[192,1024]{1,0:T(8,128)(2,1)} %refs_10_.1), channel_id=1, source_target_pairs={{0,1},{1,0},{2,3},{3,2},{4,5},{5,4},{6,7},{7,6},{8,9},{9,8},{10,11... | collective-permute-start | bytes 1179656 | tf_op jit(solution)/shard_map/ppermute | solution.py:22
  1.1 7.6 %collective-permute-start.2 = (bf16[192,256]{1,0:T(8,128)(2,1)}, bf16[192,256]{1,0:T(8,128)(2,1)S(1)}, u32[]{:S(2)}, u32[]{:S(2)}) collective-permute-start(bf16[192,256]{1,0:T(8,128)(2,1)} %bitcast.1), channel_id=1, source_target_pairs={{0,2},{1,3},{2,0},{3,1},{4,6},{5,7},{6,4},{7,5},{8,10},{9,11},{10,... | collective-permute-start | bytes 294920 | tf_op jit(solution)/shard_map/ppermute | solution.py:22
  3.7 5.0 %collective-permute-start.1 = (s32[16,1024]{1,0:T(8,128)}, s32[16,1024]{1,0:T(8,128)S(1)}, u32[]{:S(2)}, u32[]{:S(2)}) collective-permute-start(s32[16,1024]{1,0:T(8,128)} %refs_9_.1), channel_id=1, source_target_pairs={{0,2},{1,3},{2,0},{3,1},{4,6},{5,7},{6,4},{7,5},{8,10},{9,11},{10,... | collective-permute-start | bytes 196616 | tf_op jit(solution)/shard_map/ppermute | solution.py:22
  8.7 4.4 %copy-start = (bf16[192,1024]{1,0:T(8,128)(2,1)S(1)}, bf16[192,1024]{1,0:T(8,128)(2,1)}, u32[]{:S(2)}) copy-start(bf16[192,1024]{1,0:T(8,128)(2,1)} %refs_10_.1) | copy-start | bytes 1179652
  9.6 5.7 %collective-permute-start.3 = (f32[96,384]{1,0:T(8,128)S(1)}, f32[96,384]{1,0:T(8,128)S(1)}, u32[]{:S(2)}, u32[]{:S(2)}) collective-permute-start(f32[96,384]{1,0:T(8,128)S(1)} %get-tuple-element.27), channel_id=1, source_target_pairs={{0,4},{1,5},{2,6},{3,7},{4,0},{5,1},{6,2},{7,3},{8,12},{9,13},{10,... | collective-permute-start | bytes 442376 | tf_op jit(solution)/shard_map/ppermute | solution.py:22
  11.4 6.7 %collective-permute-start.4 = (f32[96,384]{1,0:T(8,128)S(1)}, f32[96,384]{1,0:T(8,128)S(1)}, u32[]{:S(2)}, u32[]{:S(2)}) collective-permute-start(f32[96,384]{1,0:T(8,128)S(1)} %get-tuple-element.28), channel_id=1, source_target_pairs={{0,8},{1,9},{2,10},{3,11},{4,12},{5,13},{6,14},{7,15},{8,0},{9,1},... | collective-permute-start | bytes 442376 | tf_op jit(solution)/shard_map/ppermute | solution.py:22
  13.0 6.6 %collective-permute-start.5 = (f32[96,384]{1,0:T(8,128)S(1)}, f32[96,384]{1,0:T(8,128)S(1)}, u32[]{:S(2)}, u32[]{:S(2)}) collective-permute-start(f32[96,384]{1,0:T(8,128)S(1)} %get-tuple-element.29), channel_id=1, source_target_pairs={{0,12},{1,13},{2,14},{3,15},{4,8},{5,9},{6,10},{7,11},{8,4},{9,5},... | collective-permute-start | bytes 442376 | tf_op jit(solution)/shard_map/ppermute | solution.py:22
  13.2 15.5 %collective-permute-start.17 = (bf16[192,1024]{1,0:T(8,128)(2,1)S(1)}, bf16[192,1024]{1,0:T(8,128)(2,1)S(1)}, u32[]{:S(2)}, u32[]{:S(2)}) collective-permute-start(bf16[192,1024]{1,0:T(8,128)(2,1)S(1)} %copy-done), channel_id=1, source_target_pairs={{0,2},{1,3},{2,0},{3,1},{4,6},{5,7},{6,4},{7,5},{8,10},{9,11},{10,... | collective-permute-start | bytes 1179656 | tf_op jit(solution)/shard_map/ppermute | solution.py:22
  19.7 9.0 %collective-permute-start.6 = (f32[96,384]{1,0:T(8,128)S(1)}, f32[96,384]{1,0:T(8,128)S(1)}, u32[]{:S(2)}, u32[]{:S(2)}) collective-permute-start(f32[96,384]{1,0:T(8,128)S(1)} %add_add_fusion.kept), channel_id=1, source_target_pairs={{0,16},{1,17},{2,18},{3,19},{4,20},{5,21},{6,22},{7,23},{8,24},{9,... | collective-permute-start | bytes 442376 | tf_op jit(solution)/shard_map/ppermute | solution.py:22
  22.4 6.8 %collective-permute-start.7 = (f32[96,384]{1,0:T(8,128)S(1)}, f32[96,384]{1,0:T(8,128)S(1)}, u32[]{:S(2)}, u32[]{:S(2)}) collective-permute-start(f32[96,384]{1,0:T(8,128)S(1)} %add_add_fusion.kept), channel_id=1, source_target_pairs={{0,1},{1,0},{2,3},{3,2},{4,5},{5,4},{6,7},{7,6},{8,9},{9,8},{10,11... | collective-permute-start | bytes 442376 | tf_op jit(solution)/shard_map/ppermute | solution.py:22
  28.7 1.4 %collective-permute-start.8 = (f32[96,384]{1,0:T(8,128)S(1)}, f32[96,384]{1,0:T(8,128)S(1)}, u32[]{:S(2)}, u32[]{:S(2)}) collective-permute-start(f32[96,384]{1,0:T(8,128)S(1)} %collective-permute-done.6.received), channel_id=1, source_target_pairs={{0,1},{1,0},{2,3},{3,2},{4,5},{5,4},{6,7},{7,6},{8,9},{9,8},{10,11... | collective-permute-start | bytes 442376 | tf_op jit(solution)/shard_map/ppermute | solution.py:22
  28.7 14.1 %collective-permute-start.18 = (bf16[192,1024]{1,0:T(8,128)(2,1)S(1)}, bf16[192,1024]{1,0:T(8,128)(2,1)S(1)}, u32[]{:S(2)}, u32[]{:S(2)}) collective-permute-start(bf16[192,1024]{1,0:T(8,128)(2,1)S(1)} %collective-permute-done.17.refs_12_), channel_id=1, source_target_pairs={{0,1},{1,0},{2,3},{3,2},{4,5},{5,4},{6,7},{7,6},{8,9},{9,8},{10,11... | collective-permute-start | bytes 1179656 | tf_op jit(solution)/shard_map/ppermute | solution.py:22
  30.1 7.9 %collective-permute-start.11 = (s16[224,384]{1,0:T(8,128)(2,1)S(1)}, s16[224,384]{1,0:T(8,128)(2,1)S(1)}, u32[]{:S(2)}, u32[]{:S(2)}) collective-permute-start(s16[224,384]{1,0:T(8,128)(2,1)S(1)} %get-tuple-element.30.refs_0_), channel_id=1, source_target_pairs={{0,10},{1,7},{2,8},{3,5},{4,14},{5,3},{6,12},{7,1},{8,2},{9,15},{1... | collective-permute-start | bytes 516104 | tf_op jit(solution)/shard_map/ppermute | solution.py:27
  31.0 9.3 %collective-permute-start.10 = (s16[224,384]{1,0:T(8,128)(2,1)S(1)}, s16[224,384]{1,0:T(8,128)(2,1)S(1)}, u32[]{:S(2)}, u32[]{:S(2)}) collective-permute-start(s16[224,384]{1,0:T(8,128)(2,1)S(1)} %get-tuple-element.30.refs_0_), channel_id=1, source_target_pairs={{0,2},{1,13},{2,0},{3,15},{4,6},{5,9},{6,4},{7,11},{8,10},{9,5},{1... | collective-permute-start | bytes 516104 | tf_op jit(solution)/shard_map/ppermute | solution.py:27
  31.8 8.5 %collective-permute-start.9 = (s16[224,384]{1,0:T(8,128)(2,1)S(1)}, s16[224,384]{1,0:T(8,128)(2,1)S(1)}, u32[]{:S(2)}, u32[]{:S(2)}) collective-permute-start(s16[224,384]{1,0:T(8,128)(2,1)S(1)} %get-tuple-element.30.refs_0_), channel_id=1, source_target_pairs={{0,4},{1,9},{2,6},{3,11},{4,0},{5,13},{6,2},{7,15},{8,12},{9,1},{1... | collective-permute-start | bytes 516104 | tf_op jit(solution)/shard_map/ppermute | solution.py:27
  32.9 8.1 %collective-permute-start.15 = (s16[112,384]{1,0:T(8,128)(2,1)S(1)}, s16[112,384]{1,0:T(8,128)(2,1)S(1)}, u32[]{:S(2)}, u32[]{:S(2)}) collective-permute-start(s16[112,384]{1,0:T(8,128)(2,1)S(1)} %get-tuple-element.31), channel_id=1, source_target_pairs={{0,14},{1,15},{2,12},{3,13},{4,10},{5,11},{6,8},{7,9},{8,6},{9,7},... | collective-permute-start | bytes 258056 | tf_op jit(solution)/shard_map/ppermute | solution.py:22
  38.1 4.7 %collective-permute-start.14 = (s16[224,384]{1,0:T(8,128)(2,1)S(1)}, s16[224,384]{1,0:T(8,128)(2,1)S(1)}, u32[]{:S(2)}, u32[]{:S(2)}) collective-permute-start(s16[224,384]{1,0:T(8,128)(2,1)S(1)} %collective-permute-done.11.refs_3_), channel_id=1, source_target_pairs={{0,1},{1,0},{2,3},{3,2},{4,5},{5,4},{6,7},{7,6},{8,9},{9,8},{10,11... | collective-permute-start | bytes 516104 | tf_op jit(solution)/shard_map/ppermute | solution.py:22
  40.3 2.5 %collective-permute-start.13 = (s16[224,384]{1,0:T(8,128)(2,1)S(1)}, s16[224,384]{1,0:T(8,128)(2,1)S(1)}, u32[]{:S(2)}, u32[]{:S(2)}) collective-permute-start(s16[224,384]{1,0:T(8,128)(2,1)S(1)} %collective-permute-done.10.refs_2_), channel_id=1, source_target_pairs={{0,1},{1,0},{2,3},{3,2},{4,5},{5,4},{6,7},{7,6},{8,9},{9,8},{10,11... | collective-permute-start | bytes 516104 | tf_op jit(solution)/shard_map/ppermute | solution.py:22
  40.4 2.4 %collective-permute-start.12 = (s16[224,384]{1,0:T(8,128)(2,1)S(1)}, s16[224,384]{1,0:T(8,128)(2,1)S(1)}, u32[]{:S(2)}, u32[]{:S(2)}) collective-permute-start(s16[224,384]{1,0:T(8,128)(2,1)S(1)} %collective-permute-done.9.refs_1_), channel_id=1, source_target_pairs={{0,1},{1,0},{2,3},{3,2},{4,5},{5,4},{6,7},{7,6},{8,9},{9,8},{10,11... | collective-permute-start | bytes 516104 | tf_op jit(solution)/shard_map/ppermute | solution.py:22
  41.0 1.8 %collective-permute-start.16 = (s16[112,384]{1,0:T(8,128)(2,1)S(1)}, s16[112,384]{1,0:T(8,128)(2,1)S(1)}, u32[]{:S(2)}, u32[]{:S(2)}) collective-permute-start(s16[112,384]{1,0:T(8,128)(2,1)S(1)} %collective-permute-done.15.refs_7_), channel_id=1, source_target_pairs={{0,1},{1,0},{2,3},{3,2},{4,5},{5,4},{6,7},{7,6},{8,9},{9,8},{10,11... | collective-permute-start | bytes 258056 | tf_op jit(solution)/shard_map/ppermute | solution.py:22
  59.3 4.4 %collective-permute-start.19 = (f32[64,256]{1,0:T(8,128)S(1)}, f32[64,256]{1,0:T(8,128)S(1)}, u32[]{:S(2)}, u32[]{:S(2)}) collective-permute-start(f32[64,256]{1,0:T(8,128)S(1)} %get-tuple-element.35), channel_id=1, source_target_pairs={{0,4},{1,5},{2,6},{3,7},{4,0},{5,1},{6,2},{7,3},{8,12},{9,13},{10,... | collective-permute-start | bytes 196616 | tf_op jit(solution)/shard_map/ppermute | solution.py:22
  60.8 4.8 %collective-permute-start.20 = (f32[64,256]{1,0:T(8,128)S(1)}, f32[64,256]{1,0:T(8,128)S(1)}, u32[]{:S(2)}, u32[]{:S(2)}) collective-permute-start(f32[64,256]{1,0:T(8,128)S(1)} %get-tuple-element.36), channel_id=1, source_target_pairs={{0,8},{1,9},{2,10},{3,11},{4,12},{5,13},{6,14},{7,15},{8,0},{9,1},... | collective-permute-start | bytes 196616 | tf_op jit(solution)/shard_map/ppermute | solution.py:22
  60.9 5.6 %collective-permute-start.21 = (f32[64,256]{1,0:T(8,128)S(1)}, f32[64,256]{1,0:T(8,128)S(1)}, u32[]{:S(2)}, u32[]{:S(2)}) collective-permute-start(f32[64,256]{1,0:T(8,128)S(1)} %get-tuple-element.37), channel_id=1, source_target_pairs={{0,12},{1,13},{2,14},{3,15},{4,8},{5,9},{6,10},{7,11},{8,4},{9,5},... | collective-permute-start | bytes 196616 | tf_op jit(solution)/shard_map/ppermute | solution.py:22
  66.5 4.9 %collective-permute-start.22 = (f32[32,256]{1,0:T(8,128)S(1)}, f32[32,256]{1,0:T(8,128)S(1)}, u32[]{:S(2)}, u32[]{:S(2)}) collective-permute-start(f32[32,256]{1,0:T(8,128)S(1)} %get-tuple-element.38), channel_id=1, source_target_pairs={{0,16},{1,17},{2,18},{3,19},{4,20},{5,21},{6,22},{7,23},{8,24},{9,... | collective-permute-start | bytes 98312 | tf_op jit(solution)/shard_map/ppermute | solution.py:22

commit v5 on v4

--- a/solution.py
+++ b/solution.py
@@ -49,13 +49,14 @@
 
 def decode(codes_ref, book_ref, sub_width, write):
     sub_count, row_count = codes_ref.shape
+    codes = codes_ref[...].astype(jnp.int32)
     width = sub_count * sub_width
     sublane = lax.broadcasted_iota(jnp.int32, (8, row_count), 0)
     for first in range(0, width, 8):
         one, two = first // sub_width, (first + 7) // sub_width
-        index = jnp.broadcast_to(codes_ref[one : one + 1, :], (8, row_count))
+        index = jnp.broadcast_to(codes[one : one + 1, :], (8, row_count))
         if two != one:
-            later = jnp.broadcast_to(codes_ref[two : two + 1, :], (8, row_count))
+            later = jnp.broadcast_to(codes[two : two + 1, :], (8, row_count))
             index = jnp.where(sublane < two * sub_width - first, index, later)
         book = book_ref[first : first + 8, :].astype(jnp.float32)
         parts = []
@@ -103,23 +104,25 @@
 def code_kernel(kept, received, kept_other, received_other, both, mine):
     core, _, _, _ = place()
     count = kept.shape[0]
+    exponents = []
     for k, (one, two) in enumerate(((kept, received), (kept_other, received_other))):
         total = one[...] + two[...]
         top = jnp.maximum(jnp.max(jnp.abs(total), axis=0, keepdims=True), TINY)
         exponent = jnp.ceil(jnp.log2(top))
         scaled = jnp.round(total * jnp.exp2(15.0 - exponent))
         coded = jnp.clip(scaled, -32767.0, 32767.0).astype(jnp.int32).astype(jnp.int16)
-        tail = jnp.broadcast_to(exponent, (TAIL, total.shape[1])).astype(jnp.int32).astype(jnp.int16)
-        first = pl.multiple_of((core ^ k) * (count + TAIL), TAIL)
-        both[pl.ds(first, count), :] = coded
-        both[pl.ds(pl.multiple_of(first + count, TAIL), TAIL), :] = tail
+        exponents.append(jnp.broadcast_to(exponent, (TAIL, total.shape[1])).astype(jnp.int32))
+        both[pl.ds(pl.multiple_of((core ^ k) * count, TAIL), count), :] = coded
         if k == 0:
             mine[:count, :] = coded
-            mine[count:, :] = tail
-
-
-def decoded_piece(ref, first, count):
-    exponent = ref[first + count : first + count + TAIL, :].astype(jnp.int32).astype(jnp.float32)[:1]
+    row = lax.broadcasted_iota(jnp.int32, exponents[0].shape, 0)
+    both[2 * count :, :] = jnp.where((row < TAIL // 2) == (core == 0), *exponents).astype(jnp.int16)
+    mine[count:, :] = exponents[0].astype(jnp.int16)
+
+
+def decoded_piece(ref, first, count, half):
+    tail = ref[ref.shape[0] - TAIL :, :].astype(jnp.int32).astype(jnp.float32)
+    exponent = tail[half * (TAIL // 2) : half * (TAIL // 2) + 1]
     coded = ref[first : first + count, :].astype(jnp.int32).astype(jnp.float32)
     return coded * jnp.exp2(exponent - 15.0)
 
@@ -157,16 +160,16 @@
         copies.append(pltpu.make_async_copy(source, vectors.at[rows, :], arrived.at[k]))
         copies[k].start()
 
-    def place_piece(mask, c, ref, first):
+    def place_piece(mask, c, ref, part):
         p, q = pair ^ (mask >> 1 & 1), quarter ^ (mask >> 2)
         row = ((q >> 1) * 2 + c) * width + (q & 1) * thin
         rows, columns = pl.ds(pl.multiple_of(row, 8), thin), pl.ds(pl.multiple_of(p * half, LANES), half)
-        current[rows, columns] = decoded_piece(ref, first, thin)
+        current[rows, columns] = decoded_piece(ref, part * thin, thin, part)
 
     masks = [0] + [jnp.where(core == c, one, two) for c in (0, 1) for one, two in ROUNDS]
     for mask, ref in zip(masks, pairs):
         for c in (0, 1):
-            place_piece(mask, c, ref, c * (thin + TAIL))
+            place_piece(mask, c, ref, c)
     for k, ref in enumerate(singles):
         place_piece(LAST, core ^ k, ref, 0)
     squares = jnp.zeros((8, size), jnp.float32)
@@ -199,11 +202,15 @@
     last = (NS_STEPS - 1) % 2
     high, low = halves.at[last, 0], halves.at[last, 1]
     rows = pl.ds(pl.multiple_of(own, 16), width)
-    own_gram = dot_t(high[rows, :], high[...]) + (
-        dot_t(high[rows, :], low[...]) + dot_t(low[rows, :], high[...])
-    )
-    own_high, own_low = split(own_gram)
-    update = dot(own_high, high[...]) + (dot(own_high, low[...]) + dot(own_low, high[...]))
+    stacked = halves.at[(NS_STEPS - 2) % 2, 0]
+
+    def thin_product(product, a_high, a_low):
+        stacked[:width, :], stacked[width : 2 * width, :] = a_high, a_low
+        with_high = product(stacked[: 2 * width, :], high[...])
+        return with_high[:width] + (with_high[width:] + product(stacked[:width, :], low[...]))
+
+    own_gram = thin_product(dot_t, high[rows, :], low[rows, :])
+    update = thin_product(dot, *split(own_gram))
     rotation = 1.5 * current[rows, :] - 0.5 * update
     rotation_out[...] = rotation
 
@@ -273,7 +280,7 @@
     high_masks = [4 << bit for bit in range(2, dp_count.bit_length() - 1)]
 
     book = codebook.T
-    book_other, codes_other = swap(book, 2), swap(codes, 2)
+    book_other, codes_other = swap(book, 2), swap(codes.astype(jnp.int16), 2)
     vectors_core = swap(vectors, 1)
     own_cross, own_vectors = call(
         functools.partial(own_cross_kernel, sub_width),
@@ -282,14 +289,14 @@
         0,
         vectors, near(vectors_core), codes, book,
     )
-    parts = call(
+    own_cross, vectors_late = lax.optimization_barrier((own_cross, vectors))
+    held = call(
         functools.partial(other_cross_kernel, sub_width),
         [pltpu.VMEM((thin, half), jnp.float32)] * 4,
         [pltpu.VMEM((half, half), jnp.float32), pltpu.VMEM((width, row_count), jnp.float32)],
         0,
         near(own_vectors), near(own_cross), near(codes_other), near(book_other),
     )
-    held, vectors_late = lax.optimization_barrier((parts, vectors))
     vectors_pair = swap(vectors_late, 2)
     vectors_last = swap(vectors_pair, 1)
 
@@ -299,7 +306,7 @@
     received = swap(piece, high_masks[-1])
     own_pair, own_piece = call(
         code_kernel,
-        [pltpu.VMEM((2 * (thin + TAIL), half), jnp.int16), pltpu.VMEM((thin + TAIL, half), jnp.int16)],
+        [pltpu.VMEM((2 * thin + TAIL, half), jnp.int16), pltpu.VMEM((thin + TAIL, half), jnp.int16)],
         [],
         0,
         *map(near, (piece, received, swap(piece, 1), swap(received, 1))),

time: 72.4 us -> 70.7 us (0.977)
  waiting for transfers between devices: 25.8 us -> 23.9 us
  other arithmetic: 0.06 us -> 0.89 us
    ppermute x20, waiting for transfers between devices: 21.6 us -> 20.3 us  [swap(): lax.ppermute(value, ('dp', 'dim'), [(i, i ^ mask) for i in range(count)])]
    convert_element_type x0 -> x1, other arithmetic: none -> 0.84 us  [per_device(): book_other, codes_other = (swap(book, 2), swap(codes.astype(jnp.int16), 2))]
  transfers between devices with their start and end apart: 23 -> 23, of which waited for: 14 -> 14; matrix products, arithmetic and copies ran while one was open for 0% -> 1% of each run, Pallas kernels for 3% -> 3%
where the time goes in v5:
time: 70.7 us; the launch traced here: 70.5 us
  starting transfers between devices  25.2 us (36%)
  waiting for transfers between devices  23.9 us (34%)
  Pallas kernels  19.8 us (28%)
  other arithmetic  0.89 us (1%)
  between operations  0.71 us (1%)
    ppermute x20, starting transfers between devices, swap(): lax.ppermute(value, ('dp', 'dim'), [(i, i ^ mask) for i in range(count)])  22.5 us
    ppermute x20, waiting for transfers between devices, swap(): lax.ppermute(value, ('dp', 'dim'), [(i, i ^ mask) for i in range(count)])  20.3 us
    pallas_call x5, Pallas kernels, call(): pl.pallas_call(kernel, out_shape=outs, in_specs=[pl.BlockSpec(memory_spac...  19.8 us
    ppermute x3, waiting for transfers between devices, swap_by_core(): lax.ppermute(value, ('dp', 'dim'), [(i, i ^ (two if i & 1 else one)) for...  3.57 us
    ppermute x3, starting transfers between devices, swap_by_core(): lax.ppermute(value, ('dp', 'dim'), [(i, i ^ (two if i & 1 else one)) for...  2.68 us
  transfers between devices with their start and end apart: 23, of which 14 were waited for; matrix products, arithmetic and copies ran while one was open for 1% of the time, Pallas kernels for 3%

profile of v5, /device:TPU:0, one launch (start us, length us, event | category | flops | bytes accessed | tf_op | source)
XLA Modules:
  0.0 70.5 jit_solution(10980399193439464660)
XLA Ops:
  1.1 2.6 %collective-permute-start.2 = (bf16[192,256]{1,0:T(8,128)(2,1)}, bf16[192,256]{1,0:T(8,128)(2,1)S(1)}, u32[]{:S(2)}, u32[]{:S(2)}) collective-permute-start(bf16[192,256]{1,0:T(8,128)(2,1)} %bitcast.1), channel_id=1, source_target_pairs={{0,2},{1,3},{2,0},{3,1},{4,6},{5,7},{6,4},{7,5},{8,10},{9,11},{10,... | collective-permute-start | bytes 294920 | tf_op jit(solution)/shard_map/ppermute | solution.py:22
  4.6 1.8 %shard_map.50 = (f32[192,384]{1,0:T(8,128)S(1)}, bf16[384,1024]{1,0:T(8,128)(2,1)S(1)}) custom-call(bf16[192,1024]{1,0:T(8,128)(2,1)} %refs_10_.1, bf16[192,1024]{1,0:T(8,128)(2,1)S(1)} %collective-permute-done.v1.refs_11_, s32[16,1024]{1,0:T(8,128)} %refs_9_.1, bf16[192,256]{1,0:T(8,128)(2,1)} %bitcast.2), custom_call_target="tpu_custom_call" | custom-call | tf_op jit(solution)/shard_map/pallas_call | solution.py:262
  6.5 2.0 %collective-permute-done.1.codes = s16[16,1024]{1,0:T(8,128)(2,1)S(1)} collective-permute-done((s16[16,1024]{1,0:T(8,128)(2,1)S(1)}, s16[16,1024]{1,0:T(8,128)(2,1)S(1)}, u32[]{:S(2)}, u32[]{:S(2)}) %collective-permute-start.1) | collective-permute-done | bytes 32800 | tf_op jit(solution)/shard_map/ppermute | solution.py:22
  9.4 1.6 %collective-permute-start.3 = (f32[96,384]{1,0:T(8,128)S(1)}, f32[96,384]{1,0:T(8,128)S(1)}, u32[]{:S(2)}, u32[]{:S(2)}) collective-permute-start(f32[96,384]{1,0:T(8,128)S(1)} %get-tuple-element.21), channel_id=1, source_target_pairs={{0,4},{1,5},{2,6},{3,7},{4,0},{5,1},{6,2},{7,3},{8,12},{9,13},{10,... | collective-permute-start | bytes 442376 | tf_op jit(solution)/shard_map/ppermute | solution.py:22
  10.9 1.6 %collective-permute-start.4 = (f32[96,384]{1,0:T(8,128)S(1)}, f32[96,384]{1,0:T(8,128)S(1)}, u32[]{:S(2)}, u32[]{:S(2)}) collective-permute-start(f32[96,384]{1,0:T(8,128)S(1)} %get-tuple-element.22), channel_id=1, source_target_pairs={{0,8},{1,9},{2,10},{3,11},{4,12},{5,13},{6,14},{7,15},{8,0},{9,1},... | collective-permute-start | bytes 442376 | tf_op jit(solution)/shard_map/ppermute | solution.py:22
  12.9 1.3 %collective-permute-start.17 = (bf16[192,1024]{1,0:T(8,128)(2,1)S(1)}, bf16[192,1024]{1,0:T(8,128)(2,1)S(1)}, u32[]{:S(2)}, u32[]{:S(2)}) collective-permute-start(bf16[192,1024]{1,0:T(8,128)(2,1)S(1)} %copy-done), channel_id=1, source_target_pairs={{0,2},{1,3},{2,0},{3,1},{4,6},{5,7},{6,4},{7,5},{8,10},{9,11},{10,... | collective-permute-start | bytes 1179656 | tf_op jit(solution)/shard_map/ppermute | solution.py:22
  14.6 2.8 %collective-permute-done.4 = f32[96,384]{1,0:T(8,128)S(1)} collective-permute-done((f32[96,384]{1,0:T(8,128)S(1)}, f32[96,384]{1,0:T(8,128)S(1)}, u32[]{:S(2)}, u32[]{:S(2)}) %collective-permute-start.4) | collective-permute-done | bytes 147488 | tf_op jit(solution)/shard_map/ppermute | solution.py:22
  17.3 1.8 %collective-permute-done.5 = f32[96,384]{1,0:T(8,128)S(1)} collective-permute-done((f32[96,384]{1,0:T(8,128)S(1)}, f32[96,384]{1,0:T(8,128)S(1)}, u32[]{:S(2)}, u32[]{:S(2)}) %collective-permute-start.5) | collective-permute-done | bytes 147488 | tf_op jit(solution)/shard_map/ppermute | solution.py:22
  19.2 2.7 %collective-permute-start.6 = (f32[96,384]{1,0:T(8,128)S(1)}, f32[96,384]{1,0:T(8,128)S(1)}, u32[]{:S(2)}, u32[]{:S(2)}) collective-permute-start(f32[96,384]{1,0:T(8,128)S(1)} %add_add_fusion.kept), channel_id=1, source_target_pairs={{0,16},{1,17},{2,18},{3,19},{4,20},{5,21},{6,22},{7,23},{8,24},{9,... | collective-permute-start | bytes 442376 | tf_op jit(solution)/shard_map/ppermute | solution.py:22
  21.9 5.8 %collective-permute-done.6.received = f32[96,384]{1,0:T(8,128)S(1)} collective-permute-done((f32[96,384]{1,0:T(8,128)S(1)}, f32[96,384]{1,0:T(8,128)S(1)}, u32[]{:S(2)}, u32[]{:S(2)}) %collective-permute-start.6) | collective-permute-done | bytes 147488 | tf_op jit(solution)/shard_map/ppermute | solution.py:22
  29.2 1.1 %collective-permute-start.11 = (s16[208,384]{1,0:T(8,128)(2,1)S(1)}, s16[208,384]{1,0:T(8,128)(2,1)S(1)}, u32[]{:S(2)}, u32[]{:S(2)}) collective-permute-start(s16[208,384]{1,0:T(8,128)(2,1)S(1)} %get-tuple-element.24.refs_0_), channel_id=1, source_target_pairs={{0,10},{1,7},{2,8},{3,5},{4,14},{5,3},{6,12},{7,1},{8,2},{9,15},{1... | collective-permute-start | bytes 479240 | tf_op jit(solution)/shard_map/ppermute | solution.py:27
  31.9 3.6 %collective-permute-start.15 = (s16[112,384]{1,0:T(8,128)(2,1)S(1)}, s16[112,384]{1,0:T(8,128)(2,1)S(1)}, u32[]{:S(2)}, u32[]{:S(2)}) collective-permute-start(s16[112,384]{1,0:T(8,128)(2,1)S(1)} %get-tuple-element.25), channel_id=1, source_target_pairs={{0,14},{1,15},{2,12},{3,13},{4,10},{5,11},{6,8},{7,9},{8,6},{9,7},... | collective-permute-start | bytes 258056 | tf_op jit(solution)/shard_map/ppermute | solution.py:22
  35.4 1.4 %collective-permute-done.11.refs_3_ = s16[208,384]{1,0:T(8,128)(2,1)S(1)} collective-permute-done((s16[208,384]{1,0:T(8,128)(2,1)S(1)}, s16[208,384]{1,0:T(8,128)(2,1)S(1)}, u32[]{:S(2)}, u32[]{:S(2)}) %collective-permute-start.11) | collective-permute-done | bytes 159776 | tf_op jit(solution)/shard_map/ppermute | solution.py:27
  36.9 1.9 %collective-permute-done.10.refs_2_ = s16[208,384]{1,0:T(8,128)(2,1)S(1)} collective-permute-done((s16[208,384]{1,0:T(8,128)(2,1)S(1)}, s16[208,384]{1,0:T(8,128)(2,1)S(1)}, u32[]{:S(2)}, u32[]{:S(2)}) %collective-permute-start.10) | collective-permute-done | bytes 159776 | tf_op jit(solution)/shard_map/ppermute | solution.py:27
  39.0 0.9 %collective-permute-start.12 = (s16[208,384]{1,0:T(8,128)(2,1)S(1)}, s16[208,384]{1,0:T(8,128)(2,1)S(1)}, u32[]{:S(2)}, u32[]{:S(2)}) collective-permute-start(s16[208,384]{1,0:T(8,128)(2,1)S(1)} %collective-permute-done.9.refs_1_), channel_id=1, source_target_pairs={{0,1},{1,0},{2,3},{3,2},{4,5},{5,4},{6,7},{7,6},{8,9},{9,8},{10,11... | collective-permute-start | bytes 479240 | tf_op jit(solution)/shard_map/ppermute | solution.py:22
  40.4 0.9 %collective-permute-done.16.refs_8_ = s16[112,384]{1,0:T(8,128)(2,1)S(1)} collective-permute-done((s16[112,384]{1,0:T(8,128)(2,1)S(1)}, s16[112,384]{1,0:T(8,128)(2,1)S(1)}, u32[]{:S(2)}, u32[]{:S(2)}) %collective-permute-start.16) | collective-permute-done | bytes 86048 | tf_op jit(solution)/shard_map/ppermute | solution.py:22
  41.4 16.1 %shard_map.53 = (f32[192,768]{1,0:T(8,128)}, f32[64,256]{1,0:T(8,128)S(1)}, f32[64,256]{1,0:T(8,128)S(1)}, f32[64,256]{1,0:T(8,128)S(1)}, f32[64,256]{1,0:T(8,128)S(1)}) custom-call(s16[208,384]{1,0:T(8,128)(2,1)S(1)} %get-tuple-element.24.refs_0_, s16[208,384]{1,0:T(8,128)(2,1)S(1)} %collective-permute-done.9.refs_1_, ...), custom_call_target="tpu_custom_call" | custom-call | tf_op jit(solution)/shard_map/pallas_call | solution.py:262
  57.5 1.6 %collective-permute-start.19 = (f32[64,256]{1,0:T(8,128)S(1)}, f32[64,256]{1,0:T(8,128)S(1)}, u32[]{:S(2)}, u32[]{:S(2)}) collective-permute-start(f32[64,256]{1,0:T(8,128)S(1)} %get-tuple-element.29), channel_id=1, source_target_pairs={{0,4},{1,5},{2,6},{3,7},{4,0},{5,1},{6,2},{7,3},{8,12},{9,13},{10,... | collective-permute-start | bytes 196616 | tf_op jit(solution)/shard_map/ppermute | solution.py:22
  59.5 1.5 %collective-permute-start.21 = (f32[64,256]{1,0:T(8,128)S(1)}, f32[64,256]{1,0:T(8,128)S(1)}, u32[]{:S(2)}, u32[]{:S(2)}) collective-permute-start(f32[64,256]{1,0:T(8,128)S(1)} %get-tuple-element.31), channel_id=1, source_target_pairs={{0,12},{1,13},{2,14},{3,15},{4,8},{5,9},{6,10},{7,11},{8,4},{9,5},... | collective-permute-start | bytes 196616 | tf_op jit(solution)/shard_map/ppermute | solution.py:22
  61.0 0.9 %collective-permute-done.19 = f32[64,256]{1,0:T(8,128)S(1)} collective-permute-done((f32[64,256]{1,0:T(8,128)S(1)}, f32[64,256]{1,0:T(8,128)S(1)}, u32[]{:S(2)}, u32[]{:S(2)}) %collective-permute-start.19) | collective-permute-done | bytes 65568 | tf_op jit(solution)/shard_map/ppermute | solution.py:22
  61.9 2.0 %collective-permute-done.20 = f32[64,256]{1,0:T(8,128)S(1)} collective-permute-done((f32[64,256]{1,0:T(8,128)S(1)}, f32[64,256]{1,0:T(8,128)S(1)}, u32[]{:S(2)}, u32[]{:S(2)}) %collective-permute-start.20) | collective-permute-done | bytes 65568 | tf_op jit(solution)/shard_map/ppermute | solution.py:22
  64.7 2.8 %collective-permute-start.22 = (f32[32,256]{1,0:T(8,128)S(1)}, f32[32,256]{1,0:T(8,128)S(1)}, u32[]{:S(2)}, u32[]{:S(2)}) collective-permute-start(f32[32,256]{1,0:T(8,128)S(1)} %get-tuple-element.32), channel_id=1, source_target_pairs={{0,16},{1,17},{2,18},{3,19},{4,20},{5,21},{6,22},{7,23},{8,24},{9,... | collective-permute-start | bytes 98312 | tf_op jit(solution)/shard_map/ppermute | solution.py:22
  67.5 2.1 %collective-permute-done.22.received = f32[32,256]{1,0:T(8,128)S(1)} collective-permute-done((f32[32,256]{1,0:T(8,128)S(1)}, f32[32,256]{1,0:T(8,128)S(1)}, u32[]{:S(2)}, u32[]{:S(2)}) %collective-permute-start.22) | collective-permute-done | bytes 32800 | tf_op jit(solution)/shard_map/ppermute | solution.py:22
  69.6 0.9 %shard_map.54 = f32[32,192]{1,0:T(8,128)} custom-call(f32[32,256]{1,0:T(8,128)S(1)} %get-tuple-element.33.kept, f32[32,256]{1,0:T(8,128)S(1)} %collective-permute-done.22.received), custom_call_target="tpu_custom_call" | custom-call | tf_op jit(solution)/shard_map/pallas_call | solution.py:262
  (33 shorter events, 8.0 us)
Async XLA Ops:
  0.6 4.0 %collective-permute-start = (bf16[192,1024]{1,0:T(8,128)(2,1)}, bf16[192,1024]{1,0:T(8,128)(2,1)S(1)}, u32[]{:S(2)}, u32[]{:S(2)}) collective-permute-start(bf16[192,1024]{1,0:T(8,128)(2,1)} %refs_10_.1), channel_id=1, source_target_pairs={{0,1},{1,0},{2,3},{3,2},{4,5},{5,4},{6,7},{7,6},{8,9},{9,8},{10,11... | collective-permute-start | bytes 1179656 | tf_op jit(solution)/shard_map/ppermute | solution.py:22
  1.1 7.4 %collective-permute-start.2 = (bf16[192,256]{1,0:T(8,128)(2,1)}, bf16[192,256]{1,0:T(8,128)(2,1)S(1)}, u32[]{:S(2)}, u32[]{:S(2)}) collective-permute-start(bf16[192,256]{1,0:T(8,128)(2,1)} %bitcast.1), channel_id=1, source_target_pairs={{0,2},{1,3},{2,0},{3,1},{4,6},{5,7},{6,4},{7,5},{8,10},{9,11},{10,... | collective-permute-start | bytes 294920 | tf_op jit(solution)/shard_map/ppermute | solution.py:22
  4.6 3.9 %collective-permute-start.1 = (s16[16,1024]{1,0:T(8,128)(2,1)S(1)}, s16[16,1024]{1,0:T(8,128)(2,1)S(1)}, u32[]{:S(2)}, u32[]{:S(2)}) collective-permute-start(s16[16,1024]{1,0:T(8,128)(2,1)S(1)} %convert_element_type.3), channel_id=1, source_target_pairs={{0,2},{1,3},{2,0},{3,1},{4,6},{5,7},{6,4},{7,5},{8,10},{9,11},{10,... | collective-permute-start | bytes 98312 | tf_op jit(solution)/shard_map/ppermute | solution.py:22
  8.5 4.4 %copy-start = (bf16[192,1024]{1,0:T(8,128)(2,1)S(1)}, bf16[192,1024]{1,0:T(8,128)(2,1)}, u32[]{:S(2)}) copy-start(bf16[192,1024]{1,0:T(8,128)(2,1)} %refs_10_.1) | copy-start | bytes 1179652
  9.4 5.2 %collective-permute-start.3 = (f32[96,384]{1,0:T(8,128)S(1)}, f32[96,384]{1,0:T(8,128)S(1)}, u32[]{:S(2)}, u32[]{:S(2)}) collective-permute-start(f32[96,384]{1,0:T(8,128)S(1)} %get-tuple-element.21), channel_id=1, source_target_pairs={{0,4},{1,5},{2,6},{3,7},{4,0},{5,1},{6,2},{7,3},{8,12},{9,13},{10,... | collective-permute-start | bytes 442376 | tf_op jit(solution)/shard_map/ppermute | solution.py:22
  10.9 6.4 %collective-permute-start.4 = (f32[96,384]{1,0:T(8,128)S(1)}, f32[96,384]{1,0:T(8,128)S(1)}, u32[]{:S(2)}, u32[]{:S(2)}) collective-permute-start(f32[96,384]{1,0:T(8,128)S(1)} %get-tuple-element.22), channel_id=1, source_target_pairs={{0,8},{1,9},{2,10},{3,11},{4,12},{5,13},{6,14},{7,15},{8,0},{9,1},... | collective-permute-start | bytes 442376 | tf_op jit(solution)/shard_map/ppermute | solution.py:22
  12.5 6.7 %collective-permute-start.5 = (f32[96,384]{1,0:T(8,128)S(1)}, f32[96,384]{1,0:T(8,128)S(1)}, u32[]{:S(2)}, u32[]{:S(2)}) collective-permute-start(f32[96,384]{1,0:T(8,128)S(1)} %get-tuple-element.23), channel_id=1, source_target_pairs={{0,12},{1,13},{2,14},{3,15},{4,8},{5,9},{6,10},{7,11},{8,4},{9,5},... | collective-permute-start | bytes 442376 | tf_op jit(solution)/shard_map/ppermute | solution.py:22
  12.9 14.8 %collective-permute-start.17 = (bf16[192,1024]{1,0:T(8,128)(2,1)S(1)}, bf16[192,1024]{1,0:T(8,128)(2,1)S(1)}, u32[]{:S(2)}, u32[]{:S(2)}) collective-permute-start(bf16[192,1024]{1,0:T(8,128)(2,1)S(1)} %copy-done), channel_id=1, source_target_pairs={{0,2},{1,3},{2,0},{3,1},{4,6},{5,7},{6,4},{7,5},{8,10},{9,11},{10,... | collective-permute-start | bytes 1179656 | tf_op jit(solution)/shard_map/ppermute | solution.py:22
  19.2 8.5 %collective-permute-start.6 = (f32[96,384]{1,0:T(8,128)S(1)}, f32[96,384]{1,0:T(8,128)S(1)}, u32[]{:S(2)}, u32[]{:S(2)}) collective-permute-start(f32[96,384]{1,0:T(8,128)S(1)} %add_add_fusion.kept), channel_id=1, source_target_pairs={{0,16},{1,17},{2,18},{3,19},{4,20},{5,21},{6,22},{7,23},{8,24},{9,... | collective-permute-start | bytes 442376 | tf_op jit(solution)/shard_map/ppermute | solution.py:22
  21.9 6.3 %collective-permute-start.7 = (f32[96,384]{1,0:T(8,128)S(1)}, f32[96,384]{1,0:T(8,128)S(1)}, u32[]{:S(2)}, u32[]{:S(2)}) collective-permute-start(f32[96,384]{1,0:T(8,128)S(1)} %add_add_fusion.kept), channel_id=1, source_target_pairs={{0,1},{1,0},{2,3},{3,2},{4,5},{5,4},{6,7},{7,6},{8,9},{9,8},{10,11... | collective-permute-start | bytes 442376 | tf_op jit(solution)/shard_map/ppermute | solution.py:22
  27.7 1.4 %collective-permute-start.8 = (f32[96,384]{1,0:T(8,128)S(1)}, f32[96,384]{1,0:T(8,128)S(1)}, u32[]{:S(2)}, u32[]{:S(2)}) collective-permute-start(f32[96,384]{1,0:T(8,128)S(1)} %collective-permute-done.6.received), channel_id=1, source_target_pairs={{0,1},{1,0},{2,3},{3,2},{4,5},{5,4},{6,7},{7,6},{8,9},{9,8},{10,11... | collective-permute-start | bytes 442376 | tf_op jit(solution)/shard_map/ppermute | solution.py:22
  27.7 13.6 %collective-permute-start.18 = (bf16[192,1024]{1,0:T(8,128)(2,1)S(1)}, bf16[192,1024]{1,0:T(8,128)(2,1)S(1)}, u32[]{:S(2)}, u32[]{:S(2)}) collective-permute-start(bf16[192,1024]{1,0:T(8,128)(2,1)S(1)} %collective-permute-done.17.refs_12_), channel_id=1, source_target_pairs={{0,1},{1,0},{2,3},{3,2},{4,5},{5,4},{6,7},{7,6},{8,9},{9,8},{10,11... | collective-permute-start | bytes 1179656 | tf_op jit(solution)/shard_map/ppermute | solution.py:22
  29.2 7.7 %collective-permute-start.11 = (s16[208,384]{1,0:T(8,128)(2,1)S(1)}, s16[208,384]{1,0:T(8,128)(2,1)S(1)}, u32[]{:S(2)}, u32[]{:S(2)}) collective-permute-start(s16[208,384]{1,0:T(8,128)(2,1)S(1)} %get-tuple-element.24.refs_0_), channel_id=1, source_target_pairs={{0,10},{1,7},{2,8},{3,5},{4,14},{5,3},{6,12},{7,1},{8,2},{9,15},{1... | collective-permute-start | bytes 479240 | tf_op jit(solution)/shard_map/ppermute | solution.py:27
  30.3 8.4 %collective-permute-start.10 = (s16[208,384]{1,0:T(8,128)(2,1)S(1)}, s16[208,384]{1,0:T(8,128)(2,1)S(1)}, u32[]{:S(2)}, u32[]{:S(2)}) collective-permute-start(s16[208,384]{1,0:T(8,128)(2,1)S(1)} %get-tuple-element.24.refs_0_), channel_id=1, source_target_pairs={{0,2},{1,13},{2,0},{3,15},{4,6},{5,9},{6,4},{7,11},{8,10},{9,5},{1... | collective-permute-start | bytes 479240 | tf_op jit(solution)/shard_map/ppermute | solution.py:27
  31.1 7.9 %collective-permute-start.9 = (s16[208,384]{1,0:T(8,128)(2,1)S(1)}, s16[208,384]{1,0:T(8,128)(2,1)S(1)}, u32[]{:S(2)}, u32[]{:S(2)}) collective-permute-start(s16[208,384]{1,0:T(8,128)(2,1)S(1)} %get-tuple-element.24.refs_0_), channel_id=1, source_target_pairs={{0,4},{1,9},{2,6},{3,11},{4,0},{5,13},{6,2},{7,15},{8,12},{9,1},{1... | collective-permute-start | bytes 479240 | tf_op jit(solution)/shard_map/ppermute | solution.py:27
  31.9 8.1 %collective-permute-start.15 = (s16[112,384]{1,0:T(8,128)(2,1)S(1)}, s16[112,384]{1,0:T(8,128)(2,1)S(1)}, u32[]{:S(2)}, u32[]{:S(2)}) collective-permute-start(s16[112,384]{1,0:T(8,128)(2,1)S(1)} %get-tuple-element.25), channel_id=1, source_target_pairs={{0,14},{1,15},{2,12},{3,13},{4,10},{5,11},{6,8},{7,9},{8,6},{9,7},... | collective-permute-start | bytes 258056 | tf_op jit(solution)/shard_map/ppermute | solution.py:22
  36.9 4.5 %collective-permute-start.14 = (s16[208,384]{1,0:T(8,128)(2,1)S(1)}, s16[208,384]{1,0:T(8,128)(2,1)S(1)}, u32[]{:S(2)}, u32[]{:S(2)}) collective-permute-start(s16[208,384]{1,0:T(8,128)(2,1)S(1)} %collective-permute-done.11.refs_3_), channel_id=1, source_target_pairs={{0,1},{1,0},{2,3},{3,2},{4,5},{5,4},{6,7},{7,6},{8,9},{9,8},{10,11... | collective-permute-start | bytes 479240 | tf_op jit(solution)/shard_map/ppermute | solution.py:22
  38.7 2.6 %collective-permute-start.13 = (s16[208,384]{1,0:T(8,128)(2,1)S(1)}, s16[208,384]{1,0:T(8,128)(2,1)S(1)}, u32[]{:S(2)}, u32[]{:S(2)}) collective-permute-start(s16[208,384]{1,0:T(8,128)(2,1)S(1)} %collective-permute-done.10.refs_2_), channel_id=1, source_target_pairs={{0,1},{1,0},{2,3},{3,2},{4,5},{5,4},{6,7},{7,6},{8,9},{9,8},{10,11... | collective-permute-start | bytes 479240 | tf_op jit(solution)/shard_map/ppermute | solution.py:22
  39.0 2.3 %collective-permute-start.12 = (s16[208,384]{1,0:T(8,128)(2,1)S(1)}, s16[208,384]{1,0:T(8,128)(2,1)S(1)}, u32[]{:S(2)}, u32[]{:S(2)}) collective-permute-start(s16[208,384]{1,0:T(8,128)(2,1)S(1)} %collective-permute-done.9.refs_1_), channel_id=1, source_target_pairs={{0,1},{1,0},{2,3},{3,2},{4,5},{5,4},{6,7},{7,6},{8,9},{9,8},{10,11... | collective-permute-start | bytes 479240 | tf_op jit(solution)/shard_map/ppermute | solution.py:22
  39.9 1.4 %collective-permute-start.16 = (s16[112,384]{1,0:T(8,128)(2,1)S(1)}, s16[112,384]{1,0:T(8,128)(2,1)S(1)}, u32[]{:S(2)}, u32[]{:S(2)}) collective-permute-start(s16[112,384]{1,0:T(8,128)(2,1)S(1)} %collective-permute-done.15.refs_7_), channel_id=1, source_target_pairs={{0,1},{1,0},{2,3},{3,2},{4,5},{5,4},{6,7},{7,6},{8,9},{9,8},{10,11... | collective-permute-start | bytes 258056 | tf_op jit(solution)/shard_map/ppermute | solution.py:22
  57.5 4.4 %collective-permute-start.19 = (f32[64,256]{1,0:T(8,128)S(1)}, f32[64,256]{1,0:T(8,128)S(1)}, u32[]{:S(2)}, u32[]{:S(2)}) collective-permute-start(f32[64,256]{1,0:T(8,128)S(1)} %get-tuple-element.29), channel_id=1, source_target_pairs={{0,4},{1,5},{2,6},{3,7},{4,0},{5,1},{6,2},{7,3},{8,12},{9,13},{10,... | collective-permute-start | bytes 196616 | tf_op jit(solution)/shard_map/ppermute | solution.py:22
  59.1 4.8 %collective-permute-start.20 = (f32[64,256]{1,0:T(8,128)S(1)}, f32[64,256]{1,0:T(8,128)S(1)}, u32[]{:S(2)}, u32[]{:S(2)}) collective-permute-start(f32[64,256]{1,0:T(8,128)S(1)} %get-tuple-element.30), channel_id=1, source_target_pairs={{0,8},{1,9},{2,10},{3,11},{4,12},{5,13},{6,14},{7,15},{8,0},{9,1},... | collective-permute-start | bytes 196616 | tf_op jit(solution)/shard_map/ppermute | solution.py:22
  59.5 5.2 %collective-permute-start.21 = (f32[64,256]{1,0:T(8,128)S(1)}, f32[64,256]{1,0:T(8,128)S(1)}, u32[]{:S(2)}, u32[]{:S(2)}) collective-permute-start(f32[64,256]{1,0:T(8,128)S(1)} %get-tuple-element.31), channel_id=1, source_target_pairs={{0,12},{1,13},{2,14},{3,15},{4,8},{5,9},{6,10},{7,11},{8,4},{9,5},... | collective-permute-start | bytes 196616 | tf_op jit(solution)/shard_map/ppermute | solution.py:22
  64.7 4.9 %collective-permute-start.22 = (f32[32,256]{1,0:T(8,128)S(1)}, f32[32,256]{1,0:T(8,128)S(1)}, u32[]{:S(2)}, u32[]{:S(2)}) collective-permute-start(f32[32,256]{1,0:T(8,128)S(1)} %get-tuple-element.32), channel_id=1, source_target_pairs={{0,16},{1,17},{2,18},{3,19},{4,20},{5,21},{6,22},{7,23},{8,24},{9,... | collective-permute-start | bytes 98312 | tf_op jit(solution)/shard_map/ppermute | solution.py:22

commit v6 on v5

--- a/solution.py
+++ b/solution.py
@@ -127,16 +127,12 @@
     return coded * jnp.exp2(exponent - 15.0)
 
 
-def gram_blocks(size, high, low, whole, write):
+def gram_blocks(size, high, write):
     count = high.shape[0] // size
     for i in range(count):
         a = pl.ds(i * size, size)
         for j in range(i, count):
-            b = pl.ds(j * size, size)
-            block = dot_t(high[a, :], high[b, :])
-            if whole:
-                block = block + (dot_t(high[a, :], low[b, :]) + dot_t(low[a, :], high[b, :]))
-            block = block.astype(jnp.bfloat16)
+            block = dot_t(high[a, :], high[pl.ds(j * size, size), :]).astype(jnp.bfloat16)
             write(i, j, block)
             if i != j:
                 write(j, i, block.T)
@@ -145,7 +141,7 @@
 def refit_kernel(sub_width, *refs):
     pairs, singles, codes, sources = refs[:7], refs[7:9], refs[9], refs[10:14]
     rotation_out, outs = refs[14], refs[15:19]
-    current, halves, gram, vectors, rotated, total, arrived = refs[19:]
+    current, highs, low, gram, vectors, rotated, total, arrived = refs[19:]
     core, pair, quarter, high_part = place()
     dp_count = lax.axis_size("dp")
     thin, half = singles[0].shape[0] - TAIL, singles[0].shape[1]
@@ -176,33 +172,30 @@
     for row in range(0, size, 8):
         value = current[row : row + 8, :]
         squares = squares + value * value
-    magnitude = jnp.sqrt(jnp.sum(squares))
+    scale = 1.0 / jnp.sqrt(jnp.sum(squares))
     for row in range(0, size, block):
-        value = current[row : row + block, :] / magnitude
+        value = current[row : row + block, :] * scale
         current[row : row + block, :] = value
-        halves[0, 0, row : row + block, :], halves[0, 1, row : row + block, :] = split(value)
+        highs[0, row : row + block, :] = value.astype(jnp.bfloat16)
 
     def step(iteration):
-        now, later = iteration % 2, (iteration + 1) % 2
-        high, low = halves.at[now, 0], halves.at[now, 1]
+        high, later = highs.at[iteration % 2], highs.at[(iteration + 1) % 2]
 
         def write(i, j, value):
             gram[pl.ds(i * block, block), pl.ds(j * block, block)] = value
 
-        gram_blocks(block, high, low, iteration == 0, write)
+        gram_blocks(block, high, write)
         for row in range(0, size, block):
             rows = pl.ds(row, block)
-            update = dot(gram[rows, :], high[...]) + dot(gram[rows, :], low[...])
-            value = 1.5 * current[rows, :] - 0.5 * update
+            value = 1.5 * current[rows, :] - 0.5 * dot(gram[rows, :], high[...])
             current[rows, :] = value
-            halves[later, 0, rows, :], halves[later, 1, rows, :] = split(value)
+            later[rows, :], low[rows, :] = split(value)
 
     for iteration in range(NS_STEPS - 1):
         step(iteration)
-    last = (NS_STEPS - 1) % 2
-    high, low = halves.at[last, 0], halves.at[last, 1]
+    high = highs.at[(NS_STEPS - 1) % 2]
     rows = pl.ds(pl.multiple_of(own, 16), width)
-    stacked = halves.at[(NS_STEPS - 2) % 2, 0]
+    stacked = highs.at[NS_STEPS % 2]
 
     def thin_product(product, a_high, a_low):
         stacked[:width, :], stacked[width : 2 * width, :] = a_high, a_low
@@ -322,7 +315,8 @@
         [floats(width, total_width)] + [pltpu.VMEM((centroid_count // 4, columns), jnp.float32)] * 4,
         [
             pltpu.VMEM((total_width, total_width), jnp.float32),
-            pltpu.VMEM((2, 2, total_width, total_width), jnp.bfloat16),
+            pltpu.VMEM((2, total_width, total_width), jnp.bfloat16),
+            pltpu.VMEM((total_width, total_width), jnp.bfloat16),
             pltpu.VMEM((total_width, total_width), jnp.bfloat16),
             pltpu.VMEM((total_width, row_count), jnp.bfloat16),
             pltpu.VMEM((columns, row_count), jnp.bfloat16),

time: 70.7 us -> 66.3 us (0.938)
  Pallas kernels: 19.8 us -> 15.3 us
    pallas_call x5, Pallas kernels: 19.8 us -> 15.3 us  [call(): pl.pallas_call(kernel, out_shape=outs, in_specs=[pl.BlockSpec(memory_spac...]
where the time goes in v6:
time: 66.3 us; the launch traced here: 66 us
  starting transfers between devices  25.2 us (38%)
  waiting for transfers between devices  23.9 us (36%)
  Pallas kernels  15.3 us (23%)
  other arithmetic  0.89 us (1%)
  between operations  0.71 us (1%)
    ppermute x20, starting transfers between devices, swap(): lax.ppermute(value, ('dp', 'dim'), [(i, i ^ mask) for i in range(count)])  22.5 us
    ppermute x20, waiting for transfers between devices, swap(): lax.ppermute(value, ('dp', 'dim'), [(i, i ^ mask) for i in range(count)])  20.3 us
    pallas_call x5, Pallas kernels, call(): pl.pallas_call(kernel, out_shape=outs, in_specs=[pl.BlockSpec(memory_spac...  15.3 us
    ppermute x3, waiting for transfers between devices, swap_by_core(): lax.ppermute(value, ('dp', 'dim'), [(i, i ^ (two if i & 1 else one)) for...  3.57 us
    ppermute x3, starting transfers between devices, swap_by_core(): lax.ppermute(value, ('dp', 'dim'), [(i, i ^ (two if i & 1 else one)) for...  2.68 us
  transfers between devices with their start and end apart: 23, of which 14 were waited for; matrix products, arithmetic and copies ran while one was open for 1% of the time, Pallas kernels for 3%

profile of v6, /device:TPU:0, one launch (start us, length us, event | category | flops | bytes accessed | tf_op | source)
XLA Modules:
  0.0 66.0 jit_solution(6784911586102119550)
XLA Ops:
  1.1 2.6 %collective-permute-start.2 = (bf16[192,256]{1,0:T(8,128)(2,1)}, bf16[192,256]{1,0:T(8,128)(2,1)S(1)}, u32[]{:S(2)}, u32[]{:S(2)}) collective-permute-start(bf16[192,256]{1,0:T(8,128)(2,1)} %bitcast.1), channel_id=1, source_target_pairs={{0,2},{1,3},{2,0},{3,1},{4,6},{5,7},{6,4},{7,5},{8,10},{9,11},{10,... | collective-permute-start | bytes 294920 | tf_op jit(solution)/shard_map/ppermute | solution.py:22
  4.6 1.8 %shard_map.50 = (f32[192,384]{1,0:T(8,128)S(1)}, bf16[384,1024]{1,0:T(8,128)(2,1)S(1)}) custom-call(bf16[192,1024]{1,0:T(8,128)(2,1)} %refs_10_.1, bf16[192,1024]{1,0:T(8,128)(2,1)S(1)} %collective-permute-done.v1.refs_11_, s32[16,1024]{1,0:T(8,128)} %refs_9_.1, bf16[192,256]{1,0:T(8,128)(2,1)} %bitcast.2), custom_call_target="tpu_custom_call" | custom-call | tf_op jit(solution)/shard_map/pallas_call | solution.py:255
  6.5 2.0 %collective-permute-done.1.codes = s16[16,1024]{1,0:T(8,128)(2,1)S(1)} collective-permute-done((s16[16,1024]{1,0:T(8,128)(2,1)S(1)}, s16[16,1024]{1,0:T(8,128)(2,1)S(1)}, u32[]{:S(2)}, u32[]{:S(2)}) %collective-permute-start.1) | collective-permute-done | bytes 32800 | tf_op jit(solution)/shard_map/ppermute | solution.py:22
  9.4 1.6 %collective-permute-start.3 = (f32[96,384]{1,0:T(8,128)S(1)}, f32[96,384]{1,0:T(8,128)S(1)}, u32[]{:S(2)}, u32[]{:S(2)}) collective-permute-start(f32[96,384]{1,0:T(8,128)S(1)} %get-tuple-element.21), channel_id=1, source_target_pairs={{0,4},{1,5},{2,6},{3,7},{4,0},{5,1},{6,2},{7,3},{8,12},{9,13},{10,... | collective-permute-start | bytes 442376 | tf_op jit(solution)/shard_map/ppermute | solution.py:22
  10.9 1.6 %collective-permute-start.4 = (f32[96,384]{1,0:T(8,128)S(1)}, f32[96,384]{1,0:T(8,128)S(1)}, u32[]{:S(2)}, u32[]{:S(2)}) collective-permute-start(f32[96,384]{1,0:T(8,128)S(1)} %get-tuple-element.22), channel_id=1, source_target_pairs={{0,8},{1,9},{2,10},{3,11},{4,12},{5,13},{6,14},{7,15},{8,0},{9,1},... | collective-permute-start | bytes 442376 | tf_op jit(solution)/shard_map/ppermute | solution.py:22
  12.9 1.3 %collective-permute-start.17 = (bf16[192,1024]{1,0:T(8,128)(2,1)S(1)}, bf16[192,1024]{1,0:T(8,128)(2,1)S(1)}, u32[]{:S(2)}, u32[]{:S(2)}) collective-permute-start(bf16[192,1024]{1,0:T(8,128)(2,1)S(1)} %copy-done), channel_id=1, source_target_pairs={{0,2},{1,3},{2,0},{3,1},{4,6},{5,7},{6,4},{7,5},{8,10},{9,11},{10,... | collective-permute-start | bytes 1179656 | tf_op jit(solution)/shard_map/ppermute | solution.py:22
  14.6 2.8 %collective-permute-done.4 = f32[96,384]{1,0:T(8,128)S(1)} collective-permute-done((f32[96,384]{1,0:T(8,128)S(1)}, f32[96,384]{1,0:T(8,128)S(1)}, u32[]{:S(2)}, u32[]{:S(2)}) %collective-permute-start.4) | collective-permute-done | bytes 147488 | tf_op jit(solution)/shard_map/ppermute | solution.py:22
  17.3 1.8 %collective-permute-done.5 = f32[96,384]{1,0:T(8,128)S(1)} collective-permute-done((f32[96,384]{1,0:T(8,128)S(1)}, f32[96,384]{1,0:T(8,128)S(1)}, u32[]{:S(2)}, u32[]{:S(2)}) %collective-permute-start.5) | collective-permute-done | bytes 147488 | tf_op jit(solution)/shard_map/ppermute | solution.py:22
  19.2 2.7 %collective-permute-start.6 = (f32[96,384]{1,0:T(8,128)S(1)}, f32[96,384]{1,0:T(8,128)S(1)}, u32[]{:S(2)}, u32[]{:S(2)}) collective-permute-start(f32[96,384]{1,0:T(8,128)S(1)} %add_add_fusion.kept), channel_id=1, source_target_pairs={{0,16},{1,17},{2,18},{3,19},{4,20},{5,21},{6,22},{7,23},{8,24},{9,... | collective-permute-start | bytes 442376 | tf_op jit(solution)/shard_map/ppermute | solution.py:22
  21.9 5.8 %collective-permute-done.6.received = f32[96,384]{1,0:T(8,128)S(1)} collective-permute-done((f32[96,384]{1,0:T(8,128)S(1)}, f32[96,384]{1,0:T(8,128)S(1)}, u32[]{:S(2)}, u32[]{:S(2)}) %collective-permute-start.6) | collective-permute-done | bytes 147488 | tf_op jit(solution)/shard_map/ppermute | solution.py:22
  29.2 1.1 %collective-permute-start.11 = (s16[208,384]{1,0:T(8,128)(2,1)S(1)}, s16[208,384]{1,0:T(8,128)(2,1)S(1)}, u32[]{:S(2)}, u32[]{:S(2)}) collective-permute-start(s16[208,384]{1,0:T(8,128)(2,1)S(1)} %get-tuple-element.24.refs_0_), channel_id=1, source_target_pairs={{0,10},{1,7},{2,8},{3,5},{4,14},{5,3},{6,12},{7,1},{8,2},{9,15},{1... | collective-permute-start | bytes 479240 | tf_op jit(solution)/shard_map/ppermute | solution.py:27
  31.9 3.6 %collective-permute-start.15 = (s16[112,384]{1,0:T(8,128)(2,1)S(1)}, s16[112,384]{1,0:T(8,128)(2,1)S(1)}, u32[]{:S(2)}, u32[]{:S(2)}) collective-permute-start(s16[112,384]{1,0:T(8,128)(2,1)S(1)} %get-tuple-element.25), channel_id=1, source_target_pairs={{0,14},{1,15},{2,12},{3,13},{4,10},{5,11},{6,8},{7,9},{8,6},{9,7},... | collective-permute-start | bytes 258056 | tf_op jit(solution)/shard_map/ppermute | solution.py:22
  35.4 1.4 %collective-permute-done.11.refs_3_ = s16[208,384]{1,0:T(8,128)(2,1)S(1)} collective-permute-done((s16[208,384]{1,0:T(8,128)(2,1)S(1)}, s16[208,384]{1,0:T(8,128)(2,1)S(1)}, u32[]{:S(2)}, u32[]{:S(2)}) %collective-permute-start.11) | collective-permute-done | bytes 159776 | tf_op jit(solution)/shard_map/ppermute | solution.py:27
  36.9 1.9 %collective-permute-done.10.refs_2_ = s16[208,384]{1,0:T(8,128)(2,1)S(1)} collective-permute-done((s16[208,384]{1,0:T(8,128)(2,1)S(1)}, s16[208,384]{1,0:T(8,128)(2,1)S(1)}, u32[]{:S(2)}, u32[]{:S(2)}) %collective-permute-start.10) | collective-permute-done | bytes 159776 | tf_op jit(solution)/shard_map/ppermute | solution.py:27
  39.0 0.9 %collective-permute-start.12 = (s16[208,384]{1,0:T(8,128)(2,1)S(1)}, s16[208,384]{1,0:T(8,128)(2,1)S(1)}, u32[]{:S(2)}, u32[]{:S(2)}) collective-permute-start(s16[208,384]{1,0:T(8,128)(2,1)S(1)} %collective-permute-done.9.refs_1_), channel_id=1, source_target_pairs={{0,1},{1,0},{2,3},{3,2},{4,5},{5,4},{6,7},{7,6},{8,9},{9,8},{10,11... | collective-permute-start | bytes 479240 | tf_op jit(solution)/shard_map/ppermute | solution.py:22
  40.4 0.9 %collective-permute-done.16.refs_8_ = s16[112,384]{1,0:T(8,128)(2,1)S(1)} collective-permute-done((s16[112,384]{1,0:T(8,128)(2,1)S(1)}, s16[112,384]{1,0:T(8,128)(2,1)S(1)}, u32[]{:S(2)}, u32[]{:S(2)}) %collective-permute-start.16) | collective-permute-done | bytes 86048 | tf_op jit(solution)/shard_map/ppermute | solution.py:22
  41.4 11.7 %shard_map.53 = (f32[192,768]{1,0:T(8,128)}, f32[64,256]{1,0:T(8,128)S(1)}, f32[64,256]{1,0:T(8,128)S(1)}, f32[64,256]{1,0:T(8,128)S(1)}, f32[64,256]{1,0:T(8,128)S(1)}) custom-call(s16[208,384]{1,0:T(8,128)(2,1)S(1)} %get-tuple-element.24.refs_0_, s16[208,384]{1,0:T(8,128)(2,1)S(1)} %collective-permute-done.9.refs_1_, ...), custom_call_target="tpu_custom_call" | custom-call | tf_op jit(solution)/shard_map/pallas_call | solution.py:255
  53.0 1.6 %collective-permute-start.19 = (f32[64,256]{1,0:T(8,128)S(1)}, f32[64,256]{1,0:T(8,128)S(1)}, u32[]{:S(2)}, u32[]{:S(2)}) collective-permute-start(f32[64,256]{1,0:T(8,128)S(1)} %get-tuple-element.29), channel_id=1, source_target_pairs={{0,4},{1,5},{2,6},{3,7},{4,0},{5,1},{6,2},{7,3},{8,12},{9,13},{10,... | collective-permute-start | bytes 196616 | tf_op jit(solution)/shard_map/ppermute | solution.py:22
  55.1 1.5 %collective-permute-start.21 = (f32[64,256]{1,0:T(8,128)S(1)}, f32[64,256]{1,0:T(8,128)S(1)}, u32[]{:S(2)}, u32[]{:S(2)}) collective-permute-start(f32[64,256]{1,0:T(8,128)S(1)} %get-tuple-element.31), channel_id=1, source_target_pairs={{0,12},{1,13},{2,14},{3,15},{4,8},{5,9},{6,10},{7,11},{8,4},{9,5},... | collective-permute-start | bytes 196616 | tf_op jit(solution)/shard_map/ppermute | solution.py:22
  56.6 0.9 %collective-permute-done.19 = f32[64,256]{1,0:T(8,128)S(1)} collective-permute-done((f32[64,256]{1,0:T(8,128)S(1)}, f32[64,256]{1,0:T(8,128)S(1)}, u32[]{:S(2)}, u32[]{:S(2)}) %collective-permute-start.19) | collective-permute-done | bytes 65568 | tf_op jit(solution)/shard_map/ppermute | solution.py:22
  57.5 2.0 %collective-permute-done.20 = f32[64,256]{1,0:T(8,128)S(1)} collective-permute-done((f32[64,256]{1,0:T(8,128)S(1)}, f32[64,256]{1,0:T(8,128)S(1)}, u32[]{:S(2)}, u32[]{:S(2)}) %collective-permute-start.20) | collective-permute-done | bytes 65568 | tf_op jit(solution)/shard_map/ppermute | solution.py:22
  60.3 2.8 %collective-permute-start.22 = (f32[32,256]{1,0:T(8,128)S(1)}, f32[32,256]{1,0:T(8,128)S(1)}, u32[]{:S(2)}, u32[]{:S(2)}) collective-permute-start(f32[32,256]{1,0:T(8,128)S(1)} %get-tuple-element.32), channel_id=1, source_target_pairs={{0,16},{1,17},{2,18},{3,19},{4,20},{5,21},{6,22},{7,23},{8,24},{9,... | collective-permute-start | bytes 98312 | tf_op jit(solution)/shard_map/ppermute | solution.py:22
  63.1 2.1 %collective-permute-done.22.received = f32[32,256]{1,0:T(8,128)S(1)} collective-permute-done((f32[32,256]{1,0:T(8,128)S(1)}, f32[32,256]{1,0:T(8,128)S(1)}, u32[]{:S(2)}, u32[]{:S(2)}) %collective-permute-start.22) | collective-permute-done | bytes 32800 | tf_op jit(solution)/shard_map/ppermute | solution.py:22
  65.2 0.9 %shard_map.54 = f32[32,192]{1,0:T(8,128)} custom-call(f32[32,256]{1,0:T(8,128)S(1)} %get-tuple-element.33.kept, f32[32,256]{1,0:T(8,128)S(1)} %collective-permute-done.22.received), custom_call_target="tpu_custom_call" | custom-call | tf_op jit(solution)/shard_map/pallas_call | solution.py:255
  (33 shorter events, 8.0 us)
Async XLA Ops:
  0.6 4.0 %collective-permute-start = (bf16[192,1024]{1,0:T(8,128)(2,1)}, bf16[192,1024]{1,0:T(8,128)(2,1)S(1)}, u32[]{:S(2)}, u32[]{:S(2)}) collective-permute-start(bf16[192,1024]{1,0:T(8,128)(2,1)} %refs_10_.1), channel_id=1, source_target_pairs={{0,1},{1,0},{2,3},{3,2},{4,5},{5,4},{6,7},{7,6},{8,9},{9,8},{10,11... | collective-permute-start | bytes 1179656 | tf_op jit(solution)/shard_map/ppermute | solution.py:22
  1.1 7.4 %collective-permute-start.2 = (bf16[192,256]{1,0:T(8,128)(2,1)}, bf16[192,256]{1,0:T(8,128)(2,1)S(1)}, u32[]{:S(2)}, u32[]{:S(2)}) collective-permute-start(bf16[192,256]{1,0:T(8,128)(2,1)} %bitcast.1), channel_id=1, source_target_pairs={{0,2},{1,3},{2,0},{3,1},{4,6},{5,7},{6,4},{7,5},{8,10},{9,11},{10,... | collective-permute-start | bytes 294920 | tf_op jit(solution)/shard_map/ppermute | solution.py:22
  4.6 3.9 %collective-permute-start.1 = (s16[16,1024]{1,0:T(8,128)(2,1)S(1)}, s16[16,1024]{1,0:T(8,128)(2,1)S(1)}, u32[]{:S(2)}, u32[]{:S(2)}) collective-permute-start(s16[16,1024]{1,0:T(8,128)(2,1)S(1)} %convert_element_type.3), channel_id=1, source_target_pairs={{0,2},{1,3},{2,0},{3,1},{4,6},{5,7},{6,4},{7,5},{8,10},{9,11},{10,... | collective-permute-start | bytes 98312 | tf_op jit(solution)/shard_map/ppermute | solution.py:22
  8.5 4.4 %copy-start = (bf16[192,1024]{1,0:T(8,128)(2,1)S(1)}, bf16[192,1024]{1,0:T(8,128)(2,1)}, u32[]{:S(2)}) copy-start(bf16[192,1024]{1,0:T(8,128)(2,1)} %refs_10_.1) | copy-start | bytes 1179652
  9.4 5.2 %collective-permute-start.3 = (f32[96,384]{1,0:T(8,128)S(1)}, f32[96,384]{1,0:T(8,128)S(1)}, u32[]{:S(2)}, u32[]{:S(2)}) collective-permute-start(f32[96,384]{1,0:T(8,128)S(1)} %get-tuple-element.21), channel_id=1, source_target_pairs={{0,4},{1,5},{2,6},{3,7},{4,0},{5,1},{6,2},{7,3},{8,12},{9,13},{10,... | collective-permute-start | bytes 442376 | tf_op jit(solution)/shard_map/ppermute | solution.py:22
  10.9 6.4 %collective-permute-start.4 = (f32[96,384]{1,0:T(8,128)S(1)}, f32[96,384]{1,0:T(8,128)S(1)}, u32[]{:S(2)}, u32[]{:S(2)}) collective-permute-start(f32[96,384]{1,0:T(8,128)S(1)} %get-tuple-element.22), channel_id=1, source_target_pairs={{0,8},{1,9},{2,10},{3,11},{4,12},{5,13},{6,14},{7,15},{8,0},{9,1},... | collective-permute-start | bytes 442376 | tf_op jit(solution)/shard_map/ppermute | solution.py:22
  12.5 6.7 %collective-permute-start.5 = (f32[96,384]{1,0:T(8,128)S(1)}, f32[96,384]{1,0:T(8,128)S(1)}, u32[]{:S(2)}, u32[]{:S(2)}) collective-permute-start(f32[96,384]{1,0:T(8,128)S(1)} %get-tuple-element.23), channel_id=1, source_target_pairs={{0,12},{1,13},{2,14},{3,15},{4,8},{5,9},{6,10},{7,11},{8,4},{9,5},... | collective-permute-start | bytes 442376 | tf_op jit(solution)/shard_map/ppermute | solution.py:22
  12.9 14.8 %collective-permute-start.17 = (bf16[192,1024]{1,0:T(8,128)(2,1)S(1)}, bf16[192,1024]{1,0:T(8,128)(2,1)S(1)}, u32[]{:S(2)}, u32[]{:S(2)}) collective-permute-start(bf16[192,1024]{1,0:T(8,128)(2,1)S(1)} %copy-done), channel_id=1, source_target_pairs={{0,2},{1,3},{2,0},{3,1},{4,6},{5,7},{6,4},{7,5},{8,10},{9,11},{10,... | collective-permute-start | bytes 1179656 | tf_op jit(solution)/shard_map/ppermute | solution.py:22
  19.2 8.5 %collective-permute-start.6 = (f32[96,384]{1,0:T(8,128)S(1)}, f32[96,384]{1,0:T(8,128)S(1)}, u32[]{:S(2)}, u32[]{:S(2)}) collective-permute-start(f32[96,384]{1,0:T(8,128)S(1)} %add_add_fusion.kept), channel_id=1, source_target_pairs={{0,16},{1,17},{2,18},{3,19},{4,20},{5,21},{6,22},{7,23},{8,24},{9,... | collective-permute-start | bytes 442376 | tf_op jit(solution)/shard_map/ppermute | solution.py:22
  21.9 6.3 %collective-permute-start.7 = (f32[96,384]{1,0:T(8,128)S(1)}, f32[96,384]{1,0:T(8,128)S(1)}, u32[]{:S(2)}, u32[]{:S(2)}) collective-permute-start(f32[96,384]{1,0:T(8,128)S(1)} %add_add_fusion.kept), channel_id=1, source_target_pairs={{0,1},{1,0},{2,3},{3,2},{4,5},{5,4},{6,7},{7,6},{8,9},{9,8},{10,11... | collective-permute-start | bytes 442376 | tf_op jit(solution)/shard_map/ppermute | solution.py:22
  27.7 1.4 %collective-permute-start.8 = (f32[96,384]{1,0:T(8,128)S(1)}, f32[96,384]{1,0:T(8,128)S(1)}, u32[]{:S(2)}, u32[]{:S(2)}) collective-permute-start(f32[96,384]{1,0:T(8,128)S(1)} %collective-permute-done.6.received), channel_id=1, source_target_pairs={{0,1},{1,0},{2,3},{3,2},{4,5},{5,4},{6,7},{7,6},{8,9},{9,8},{10,11... | collective-permute-start | bytes 442376 | tf_op jit(solution)/shard_map/ppermute | solution.py:22
  27.7 13.6 %collective-permute-start.18 = (bf16[192,1024]{1,0:T(8,128)(2,1)S(1)}, bf16[192,1024]{1,0:T(8,128)(2,1)S(1)}, u32[]{:S(2)}, u32[]{:S(2)}) collective-permute-start(bf16[192,1024]{1,0:T(8,128)(2,1)S(1)} %collective-permute-done.17.refs_12_), channel_id=1, source_target_pairs={{0,1},{1,0},{2,3},{3,2},{4,5},{5,4},{6,7},{7,6},{8,9},{9,8},{10,11... | collective-permute-start | bytes 1179656 | tf_op jit(solution)/shard_map/ppermute | solution.py:22
  29.2 7.7 %collective-permute-start.11 = (s16[208,384]{1,0:T(8,128)(2,1)S(1)}, s16[208,384]{1,0:T(8,128)(2,1)S(1)}, u32[]{:S(2)}, u32[]{:S(2)}) collective-permute-start(s16[208,384]{1,0:T(8,128)(2,1)S(1)} %get-tuple-element.24.refs_0_), channel_id=1, source_target_pairs={{0,10},{1,7},{2,8},{3,5},{4,14},{5,3},{6,12},{7,1},{8,2},{9,15},{1... | collective-permute-start | bytes 479240 | tf_op jit(solution)/shard_map/ppermute | solution.py:27
  30.3 8.4 %collective-permute-start.10 = (s16[208,384]{1,0:T(8,128)(2,1)S(1)}, s16[208,384]{1,0:T(8,128)(2,1)S(1)}, u32[]{:S(2)}, u32[]{:S(2)}) collective-permute-start(s16[208,384]{1,0:T(8,128)(2,1)S(1)} %get-tuple-element.24.refs_0_), channel_id=1, source_target_pairs={{0,2},{1,13},{2,0},{3,15},{4,6},{5,9},{6,4},{7,11},{8,10},{9,5},{1... | collective-permute-start | bytes 479240 | tf_op jit(solution)/shard_map/ppermute | solution.py:27
  31.1 7.9 %collective-permute-start.9 = (s16[208,384]{1,0:T(8,128)(2,1)S(1)}, s16[208,384]{1,0:T(8,128)(2,1)S(1)}, u32[]{:S(2)}, u32[]{:S(2)}) collective-permute-start(s16[208,384]{1,0:T(8,128)(2,1)S(1)} %get-tuple-element.24.refs_0_), channel_id=1, source_target_pairs={{0,4},{1,9},{2,6},{3,11},{4,0},{5,13},{6,2},{7,15},{8,12},{9,1},{1... | collective-permute-start | bytes 479240 | tf_op jit(solution)/shard_map/ppermute | solution.py:27
  31.9 8.1 %collective-permute-start.15 = (s16[112,384]{1,0:T(8,128)(2,1)S(1)}, s16[112,384]{1,0:T(8,128)(2,1)S(1)}, u32[]{:S(2)}, u32[]{:S(2)}) collective-permute-start(s16[112,384]{1,0:T(8,128)(2,1)S(1)} %get-tuple-element.25), channel_id=1, source_target_pairs={{0,14},{1,15},{2,12},{3,13},{4,10},{5,11},{6,8},{7,9},{8,6},{9,7},... | collective-permute-start | bytes 258056 | tf_op jit(solution)/shard_map/ppermute | solution.py:22
  36.9 4.5 %collective-permute-start.14 = (s16[208,384]{1,0:T(8,128)(2,1)S(1)}, s16[208,384]{1,0:T(8,128)(2,1)S(1)}, u32[]{:S(2)}, u32[]{:S(2)}) collective-permute-start(s16[208,384]{1,0:T(8,128)(2,1)S(1)} %collective-permute-done.11.refs_3_), channel_id=1, source_target_pairs={{0,1},{1,0},{2,3},{3,2},{4,5},{5,4},{6,7},{7,6},{8,9},{9,8},{10,11... | collective-permute-start | bytes 479240 | tf_op jit(solution)/shard_map/ppermute | solution.py:22
  38.7 2.6 %collective-permute-start.13 = (s16[208,384]{1,0:T(8,128)(2,1)S(1)}, s16[208,384]{1,0:T(8,128)(2,1)S(1)}, u32[]{:S(2)}, u32[]{:S(2)}) collective-permute-start(s16[208,384]{1,0:T(8,128)(2,1)S(1)} %collective-permute-done.10.refs_2_), channel_id=1, source_target_pairs={{0,1},{1,0},{2,3},{3,2},{4,5},{5,4},{6,7},{7,6},{8,9},{9,8},{10,11... | collective-permute-start | bytes 479240 | tf_op jit(solution)/shard_map/ppermute | solution.py:22
  39.0 2.3 %collective-permute-start.12 = (s16[208,384]{1,0:T(8,128)(2,1)S(1)}, s16[208,384]{1,0:T(8,128)(2,1)S(1)}, u32[]{:S(2)}, u32[]{:S(2)}) collective-permute-start(s16[208,384]{1,0:T(8,128)(2,1)S(1)} %collective-permute-done.9.refs_1_), channel_id=1, source_target_pairs={{0,1},{1,0},{2,3},{3,2},{4,5},{5,4},{6,7},{7,6},{8,9},{9,8},{10,11... | collective-permute-start | bytes 479240 | tf_op jit(solution)/shard_map/ppermute | solution.py:22
  39.9 1.4 %collective-permute-start.16 = (s16[112,384]{1,0:T(8,128)(2,1)S(1)}, s16[112,384]{1,0:T(8,128)(2,1)S(1)}, u32[]{:S(2)}, u32[]{:S(2)}) collective-permute-start(s16[112,384]{1,0:T(8,128)(2,1)S(1)} %collective-permute-done.15.refs_7_), channel_id=1, source_target_pairs={{0,1},{1,0},{2,3},{3,2},{4,5},{5,4},{6,7},{7,6},{8,9},{9,8},{10,11... | collective-permute-start | bytes 258056 | tf_op jit(solution)/shard_map/ppermute | solution.py:22
  53.0 4.4 %collective-permute-start.19 = (f32[64,256]{1,0:T(8,128)S(1)}, f32[64,256]{1,0:T(8,128)S(1)}, u32[]{:S(2)}, u32[]{:S(2)}) collective-permute-start(f32[64,256]{1,0:T(8,128)S(1)} %get-tuple-element.29), channel_id=1, source_target_pairs={{0,4},{1,5},{2,6},{3,7},{4,0},{5,1},{6,2},{7,3},{8,12},{9,13},{10,... | collective-permute-start | bytes 196616 | tf_op jit(solution)/shard_map/ppermute | solution.py:22
  54.7 4.8 %collective-permute-start.20 = (f32[64,256]{1,0:T(8,128)S(1)}, f32[64,256]{1,0:T(8,128)S(1)}, u32[]{:S(2)}, u32[]{:S(2)}) collective-permute-start(f32[64,256]{1,0:T(8,128)S(1)} %get-tuple-element.30), channel_id=1, source_target_pairs={{0,8},{1,9},{2,10},{3,11},{4,12},{5,13},{6,14},{7,15},{8,0},{9,1},... | collective-permute-start | bytes 196616 | tf_op jit(solution)/shard_map/ppermute | solution.py:22
  55.1 5.2 %collective-permute-start.21 = (f32[64,256]{1,0:T(8,128)S(1)}, f32[64,256]{1,0:T(8,128)S(1)}, u32[]{:S(2)}, u32[]{:S(2)}) collective-permute-start(f32[64,256]{1,0:T(8,128)S(1)} %get-tuple-element.31), channel_id=1, source_target_pairs={{0,12},{1,13},{2,14},{3,15},{4,8},{5,9},{6,10},{7,11},{8,4},{9,5},... | collective-permute-start | bytes 196616 | tf_op jit(solution)/shard_map/ppermute | solution.py:22
  60.3 4.9 %collective-permute-start.22 = (f32[32,256]{1,0:T(8,128)S(1)}, f32[32,256]{1,0:T(8,128)S(1)}, u32[]{:S(2)}, u32[]{:S(2)}) collective-permute-start(f32[32,256]{1,0:T(8,128)S(1)} %get-tuple-element.32), channel_id=1, source_target_pairs={{0,16},{1,17},{2,18},{3,19},{4,20},{5,21},{6,22},{7,23},{8,24},{9,... | collective-permute-start | bytes 98312 | tf_op jit(solution)/shard_map/ppermute | solution.py:22

commit v7 on v6

--- a/solution.py
+++ b/solution.py
@@ -237,8 +237,10 @@
     width = out.shape[1]
     row = lax.broadcasted_iota(jnp.int32, (total.shape[1], width), 0)
     column = lax.broadcasted_iota(jnp.int32, (total.shape[1], width), 1)
-    spread = (row == width + column // sub_width).astype(jnp.float32)
-    counts = jnp.dot(total, spread, precision=lax.Precision.HIGHEST)
+    spread = (row == width + column // sub_width).astype(jnp.float32).astype(jnp.bfloat16)
+    upper = jnp.floor(total * (1.0 / 256.0))
+    lower = total - 256.0 * upper
+    counts = 256.0 * dot(upper.astype(jnp.bfloat16), spread) + dot(lower.astype(jnp.bfloat16), spread)
     out[...] = total[:, :width] / jnp.maximum(counts, 1.0)
 
 

time: 66.3 us -> 66.2 us (level)
  no operation moved by 1% of the time
where the time goes in v7:
time: 66.2 us; the launch traced here: 65.9 us
  starting transfers between devices  25.2 us (38%)
  waiting for transfers between devices  23.9 us (36%)
  Pallas kernels  15.2 us (23%)
  other arithmetic  0.89 us (1%)
  between operations  0.71 us (1%)
    ppermute x20, starting transfers between devices, swap(): lax.ppermute(value, ('dp', 'dim'), [(i, i ^ mask) for i in range(count)])  22.5 us
    ppermute x20, waiting for transfers between devices, swap(): lax.ppermute(value, ('dp', 'dim'), [(i, i ^ mask) for i in range(count)])  20.3 us
    pallas_call x5, Pallas kernels, call(): pl.pallas_call(kernel, out_shape=outs, in_specs=[pl.BlockSpec(memory_spac...  15.2 us
    ppermute x3, waiting for transfers between devices, swap_by_core(): lax.ppermute(value, ('dp', 'dim'), [(i, i ^ (two if i & 1 else one)) for...  3.57 us
    ppermute x3, starting transfers between devices, swap_by_core(): lax.ppermute(value, ('dp', 'dim'), [(i, i ^ (two if i & 1 else one)) for...  2.68 us
  transfers between devices with their start and end apart: 23, of which 14 were waited for; matrix products, arithmetic and copies ran while one was open for 1% of the time, Pallas kernels for 3%

profile of v7, /device:TPU:0, one launch (start us, length us, event | category | flops | bytes accessed | tf_op | source)
XLA Modules:
  0.0 65.9 jit_solution(8478540143403161033)
XLA Ops:
  1.1 2.6 %collective-permute-start.2 = (bf16[192,256]{1,0:T(8,128)(2,1)}, bf16[192,256]{1,0:T(8,128)(2,1)S(1)}, u32[]{:S(2)}, u32[]{:S(2)}) collective-permute-start(bf16[192,256]{1,0:T(8,128)(2,1)} %bitcast.1), channel_id=1, source_target_pairs={{0,2},{1,3},{2,0},{3,1},{4,6},{5,7},{6,4},{7,5},{8,10},{9,11},{10,... | collective-permute-start | bytes 294920 | tf_op jit(solution)/shard_map/ppermute | solution.py:22
  4.6 1.8 %shard_map.50 = (f32[192,384]{1,0:T(8,128)S(1)}, bf16[384,1024]{1,0:T(8,128)(2,1)S(1)}) custom-call(bf16[192,1024]{1,0:T(8,128)(2,1)} %refs_10_.1, bf16[192,1024]{1,0:T(8,128)(2,1)S(1)} %collective-permute-done.v1.refs_11_, s32[16,1024]{1,0:T(8,128)} %refs_9_.1, bf16[192,256]{1,0:T(8,128)(2,1)} %bitcast.2), custom_call_target="tpu_custom_call" | custom-call | tf_op jit(solution)/shard_map/pallas_call | solution.py:257
  6.5 2.0 %collective-permute-done.1.codes = s16[16,1024]{1,0:T(8,128)(2,1)S(1)} collective-permute-done((s16[16,1024]{1,0:T(8,128)(2,1)S(1)}, s16[16,1024]{1,0:T(8,128)(2,1)S(1)}, u32[]{:S(2)}, u32[]{:S(2)}) %collective-permute-start.1) | collective-permute-done | bytes 32800 | tf_op jit(solution)/shard_map/ppermute | solution.py:22
  9.4 1.6 %collective-permute-start.3 = (f32[96,384]{1,0:T(8,128)S(1)}, f32[96,384]{1,0:T(8,128)S(1)}, u32[]{:S(2)}, u32[]{:S(2)}) collective-permute-start(f32[96,384]{1,0:T(8,128)S(1)} %get-tuple-element.21), channel_id=1, source_target_pairs={{0,4},{1,5},{2,6},{3,7},{4,0},{5,1},{6,2},{7,3},{8,12},{9,13},{10,... | collective-permute-start | bytes 442376 | tf_op jit(solution)/shard_map/ppermute | solution.py:22
  10.9 1.6 %collective-permute-start.4 = (f32[96,384]{1,0:T(8,128)S(1)}, f32[96,384]{1,0:T(8,128)S(1)}, u32[]{:S(2)}, u32[]{:S(2)}) collective-permute-start(f32[96,384]{1,0:T(8,128)S(1)} %get-tuple-element.22), channel_id=1, source_target_pairs={{0,8},{1,9},{2,10},{3,11},{4,12},{5,13},{6,14},{7,15},{8,0},{9,1},... | collective-permute-start | bytes 442376 | tf_op jit(solution)/shard_map/ppermute | solution.py:22
  12.9 1.3 %collective-permute-start.17 = (bf16[192,1024]{1,0:T(8,128)(2,1)S(1)}, bf16[192,1024]{1,0:T(8,128)(2,1)S(1)}, u32[]{:S(2)}, u32[]{:S(2)}) collective-permute-start(bf16[192,1024]{1,0:T(8,128)(2,1)S(1)} %copy-done), channel_id=1, source_target_pairs={{0,2},{1,3},{2,0},{3,1},{4,6},{5,7},{6,4},{7,5},{8,10},{9,11},{10,... | collective-permute-start | bytes 1179656 | tf_op jit(solution)/shard_map/ppermute | solution.py:22
  14.6 2.8 %collective-permute-done.4 = f32[96,384]{1,0:T(8,128)S(1)} collective-permute-done((f32[96,384]{1,0:T(8,128)S(1)}, f32[96,384]{1,0:T(8,128)S(1)}, u32[]{:S(2)}, u32[]{:S(2)}) %collective-permute-start.4) | collective-permute-done | bytes 147488 | tf_op jit(solution)/shard_map/ppermute | solution.py:22
  17.3 1.8 %collective-permute-done.5 = f32[96,384]{1,0:T(8,128)S(1)} collective-permute-done((f32[96,384]{1,0:T(8,128)S(1)}, f32[96,384]{1,0:T(8,128)S(1)}, u32[]{:S(2)}, u32[]{:S(2)}) %collective-permute-start.5) | collective-permute-done | bytes 147488 | tf_op jit(solution)/shard_map/ppermute | solution.py:22
  19.2 2.7 %collective-permute-start.6 = (f32[96,384]{1,0:T(8,128)S(1)}, f32[96,384]{1,0:T(8,128)S(1)}, u32[]{:S(2)}, u32[]{:S(2)}) collective-permute-start(f32[96,384]{1,0:T(8,128)S(1)} %add_add_fusion.kept), channel_id=1, source_target_pairs={{0,16},{1,17},{2,18},{3,19},{4,20},{5,21},{6,22},{7,23},{8,24},{9,... | collective-permute-start | bytes 442376 | tf_op jit(solution)/shard_map/ppermute | solution.py:22
  21.9 5.8 %collective-permute-done.6.received = f32[96,384]{1,0:T(8,128)S(1)} collective-permute-done((f32[96,384]{1,0:T(8,128)S(1)}, f32[96,384]{1,0:T(8,128)S(1)}, u32[]{:S(2)}, u32[]{:S(2)}) %collective-permute-start.6) | collective-permute-done | bytes 147488 | tf_op jit(solution)/shard_map/ppermute | solution.py:22
  28.2 0.9 %collective-permute-done.8.received_other = f32[96,384]{1,0:T(8,128)S(1)} collective-permute-done((f32[96,384]{1,0:T(8,128)S(1)}, f32[96,384]{1,0:T(8,128)S(1)}, u32[]{:S(2)}, u32[]{:S(2)}) %collective-permute-start.8) | collective-permute-done | bytes 147488 | tf_op jit(solution)/shard_map/ppermute | solution.py:22
  29.2 1.1 %collective-permute-start.11 = (s16[208,384]{1,0:T(8,128)(2,1)S(1)}, s16[208,384]{1,0:T(8,128)(2,1)S(1)}, u32[]{:S(2)}, u32[]{:S(2)}) collective-permute-start(s16[208,384]{1,0:T(8,128)(2,1)S(1)} %get-tuple-element.24.refs_0_), channel_id=1, source_target_pairs={{0,10},{1,7},{2,8},{3,5},{4,14},{5,3},{6,12},{7,1},{8,2},{9,15},{1... | collective-permute-start | bytes 479240 | tf_op jit(solution)/shard_map/ppermute | solution.py:27
  31.9 3.6 %collective-permute-start.15 = (s16[112,384]{1,0:T(8,128)(2,1)S(1)}, s16[112,384]{1,0:T(8,128)(2,1)S(1)}, u32[]{:S(2)}, u32[]{:S(2)}) collective-permute-start(s16[112,384]{1,0:T(8,128)(2,1)S(1)} %get-tuple-element.25), channel_id=1, source_target_pairs={{0,14},{1,15},{2,12},{3,13},{4,10},{5,11},{6,8},{7,9},{8,6},{9,7},... | collective-permute-start | bytes 258056 | tf_op jit(solution)/shard_map/ppermute | solution.py:22
  35.4 1.4 %collective-permute-done.11.refs_3_ = s16[208,384]{1,0:T(8,128)(2,1)S(1)} collective-permute-done((s16[208,384]{1,0:T(8,128)(2,1)S(1)}, s16[208,384]{1,0:T(8,128)(2,1)S(1)}, u32[]{:S(2)}, u32[]{:S(2)}) %collective-permute-start.11) | collective-permute-done | bytes 159776 | tf_op jit(solution)/shard_map/ppermute | solution.py:27
  36.9 1.9 %collective-permute-done.10.refs_2_ = s16[208,384]{1,0:T(8,128)(2,1)S(1)} collective-permute-done((s16[208,384]{1,0:T(8,128)(2,1)S(1)}, s16[208,384]{1,0:T(8,128)(2,1)S(1)}, u32[]{:S(2)}, u32[]{:S(2)}) %collective-permute-start.10) | collective-permute-done | bytes 159776 | tf_op jit(solution)/shard_map/ppermute | solution.py:27
  39.0 0.9 %collective-permute-start.12 = (s16[208,384]{1,0:T(8,128)(2,1)S(1)}, s16[208,384]{1,0:T(8,128)(2,1)S(1)}, u32[]{:S(2)}, u32[]{:S(2)}) collective-permute-start(s16[208,384]{1,0:T(8,128)(2,1)S(1)} %collective-permute-done.9.refs_1_), channel_id=1, source_target_pairs={{0,1},{1,0},{2,3},{3,2},{4,5},{5,4},{6,7},{7,6},{8,9},{9,8},{10,11... | collective-permute-start | bytes 479240 | tf_op jit(solution)/shard_map/ppermute | solution.py:22
  40.4 0.9 %collective-permute-done.16.refs_8_ = s16[112,384]{1,0:T(8,128)(2,1)S(1)} collective-permute-done((s16[112,384]{1,0:T(8,128)(2,1)S(1)}, s16[112,384]{1,0:T(8,128)(2,1)S(1)}, u32[]{:S(2)}, u32[]{:S(2)}) %collective-permute-start.16) | collective-permute-done | bytes 86048 | tf_op jit(solution)/shard_map/ppermute | solution.py:22
  41.4 11.7 %shard_map.53 = (f32[192,768]{1,0:T(8,128)}, f32[64,256]{1,0:T(8,128)S(1)}, f32[64,256]{1,0:T(8,128)S(1)}, f32[64,256]{1,0:T(8,128)S(1)}, f32[64,256]{1,0:T(8,128)S(1)}) custom-call(s16[208,384]{1,0:T(8,128)(2,1)S(1)} %get-tuple-element.24.refs_0_, s16[208,384]{1,0:T(8,128)(2,1)S(1)} %collective-permute-done.9.refs_1_, ...), custom_call_target="tpu_custom_call" | custom-call | tf_op jit(solution)/shard_map/pallas_call | solution.py:257
  53.0 1.6 %collective-permute-start.19 = (f32[64,256]{1,0:T(8,128)S(1)}, f32[64,256]{1,0:T(8,128)S(1)}, u32[]{:S(2)}, u32[]{:S(2)}) collective-permute-start(f32[64,256]{1,0:T(8,128)S(1)} %get-tuple-element.29), channel_id=1, source_target_pairs={{0,4},{1,5},{2,6},{3,7},{4,0},{5,1},{6,2},{7,3},{8,12},{9,13},{10,... | collective-permute-start | bytes 196616 | tf_op jit(solution)/shard_map/ppermute | solution.py:22
  55.1 1.5 %collective-permute-start.21 = (f32[64,256]{1,0:T(8,128)S(1)}, f32[64,256]{1,0:T(8,128)S(1)}, u32[]{:S(2)}, u32[]{:S(2)}) collective-permute-start(f32[64,256]{1,0:T(8,128)S(1)} %get-tuple-element.31), channel_id=1, source_target_pairs={{0,12},{1,13},{2,14},{3,15},{4,8},{5,9},{6,10},{7,11},{8,4},{9,5},... | collective-permute-start | bytes 196616 | tf_op jit(solution)/shard_map/ppermute | solution.py:22
  56.6 0.9 %collective-permute-done.19 = f32[64,256]{1,0:T(8,128)S(1)} collective-permute-done((f32[64,256]{1,0:T(8,128)S(1)}, f32[64,256]{1,0:T(8,128)S(1)}, u32[]{:S(2)}, u32[]{:S(2)}) %collective-permute-start.19) | collective-permute-done | bytes 65568 | tf_op jit(solution)/shard_map/ppermute | solution.py:22
  57.5 2.0 %collective-permute-done.20 = f32[64,256]{1,0:T(8,128)S(1)} collective-permute-done((f32[64,256]{1,0:T(8,128)S(1)}, f32[64,256]{1,0:T(8,128)S(1)}, u32[]{:S(2)}, u32[]{:S(2)}) %collective-permute-start.20) | collective-permute-done | bytes 65568 | tf_op jit(solution)/shard_map/ppermute | solution.py:22
  60.3 2.8 %collective-permute-start.22 = (f32[32,256]{1,0:T(8,128)S(1)}, f32[32,256]{1,0:T(8,128)S(1)}, u32[]{:S(2)}, u32[]{:S(2)}) collective-permute-start(f32[32,256]{1,0:T(8,128)S(1)} %get-tuple-element.32), channel_id=1, source_target_pairs={{0,16},{1,17},{2,18},{3,19},{4,20},{5,21},{6,22},{7,23},{8,24},{9,... | collective-permute-start | bytes 98312 | tf_op jit(solution)/shard_map/ppermute | solution.py:22
  63.1 2.1 %collective-permute-done.22.received = f32[32,256]{1,0:T(8,128)S(1)} collective-permute-done((f32[32,256]{1,0:T(8,128)S(1)}, f32[32,256]{1,0:T(8,128)S(1)}, u32[]{:S(2)}, u32[]{:S(2)}) %collective-permute-start.22) | collective-permute-done | bytes 32800 | tf_op jit(solution)/shard_map/ppermute | solution.py:22
  (33 shorter events, 8.0 us)
Async XLA Ops:
  0.6 4.0 %collective-permute-start = (bf16[192,1024]{1,0:T(8,128)(2,1)}, bf16[192,1024]{1,0:T(8,128)(2,1)S(1)}, u32[]{:S(2)}, u32[]{:S(2)}) collective-permute-start(bf16[192,1024]{1,0:T(8,128)(2,1)} %refs_10_.1), channel_id=1, source_target_pairs={{0,1},{1,0},{2,3},{3,2},{4,5},{5,4},{6,7},{7,6},{8,9},{9,8},{10,11... | collective-permute-start | bytes 1179656 | tf_op jit(solution)/shard_map/ppermute | solution.py:22
  1.1 7.4 %collective-permute-start.2 = (bf16[192,256]{1,0:T(8,128)(2,1)}, bf16[192,256]{1,0:T(8,128)(2,1)S(1)}, u32[]{:S(2)}, u32[]{:S(2)}) collective-permute-start(bf16[192,256]{1,0:T(8,128)(2,1)} %bitcast.1), channel_id=1, source_target_pairs={{0,2},{1,3},{2,0},{3,1},{4,6},{5,7},{6,4},{7,5},{8,10},{9,11},{10,... | collective-permute-start | bytes 294920 | tf_op jit(solution)/shard_map/ppermute | solution.py:22
  4.6 3.9 %collective-permute-start.1 = (s16[16,1024]{1,0:T(8,128)(2,1)S(1)}, s16[16,1024]{1,0:T(8,128)(2,1)S(1)}, u32[]{:S(2)}, u32[]{:S(2)}) collective-permute-start(s16[16,1024]{1,0:T(8,128)(2,1)S(1)} %convert_element_type.3), channel_id=1, source_target_pairs={{0,2},{1,3},{2,0},{3,1},{4,6},{5,7},{6,4},{7,5},{8,10},{9,11},{10,... | collective-permute-start | bytes 98312 | tf_op jit(solution)/shard_map/ppermute | solution.py:22
  8.5 4.4 %copy-start = (bf16[192,1024]{1,0:T(8,128)(2,1)S(1)}, bf16[192,1024]{1,0:T(8,128)(2,1)}, u32[]{:S(2)}) copy-start(bf16[192,1024]{1,0:T(8,128)(2,1)} %refs_10_.1) | copy-start | bytes 1179652
  9.4 5.2 %collective-permute-start.3 = (f32[96,384]{1,0:T(8,128)S(1)}, f32[96,384]{1,0:T(8,128)S(1)}, u32[]{:S(2)}, u32[]{:S(2)}) collective-permute-start(f32[96,384]{1,0:T(8,128)S(1)} %get-tuple-element.21), channel_id=1, source_target_pairs={{0,4},{1,5},{2,6},{3,7},{4,0},{5,1},{6,2},{7,3},{8,12},{9,13},{10,... | collective-permute-start | bytes 442376 | tf_op jit(solution)/shard_map/ppermute | solution.py:22
  10.9 6.4 %collective-permute-start.4 = (f32[96,384]{1,0:T(8,128)S(1)}, f32[96,384]{1,0:T(8,128)S(1)}, u32[]{:S(2)}, u32[]{:S(2)}) collective-permute-start(f32[96,384]{1,0:T(8,128)S(1)} %get-tuple-element.22), channel_id=1, source_target_pairs={{0,8},{1,9},{2,10},{3,11},{4,12},{5,13},{6,14},{7,15},{8,0},{9,1},... | collective-permute-start | bytes 442376 | tf_op jit(solution)/shard_map/ppermute | solution.py:22
  12.5 6.7 %collective-permute-start.5 = (f32[96,384]{1,0:T(8,128)S(1)}, f32[96,384]{1,0:T(8,128)S(1)}, u32[]{:S(2)}, u32[]{:S(2)}) collective-permute-start(f32[96,384]{1,0:T(8,128)S(1)} %get-tuple-element.23), channel_id=1, source_target_pairs={{0,12},{1,13},{2,14},{3,15},{4,8},{5,9},{6,10},{7,11},{8,4},{9,5},... | collective-permute-start | bytes 442376 | tf_op jit(solution)/shard_map/ppermute | solution.py:22
  12.9 14.8 %collective-permute-start.17 = (bf16[192,1024]{1,0:T(8,128)(2,1)S(1)}, bf16[192,1024]{1,0:T(8,128)(2,1)S(1)}, u32[]{:S(2)}, u32[]{:S(2)}) collective-permute-start(bf16[192,1024]{1,0:T(8,128)(2,1)S(1)} %copy-done), channel_id=1, source_target_pairs={{0,2},{1,3},{2,0},{3,1},{4,6},{5,7},{6,4},{7,5},{8,10},{9,11},{10,... | collective-permute-start | bytes 1179656 | tf_op jit(solution)/shard_map/ppermute | solution.py:22
  19.2 8.5 %collective-permute-start.6 = (f32[96,384]{1,0:T(8,128)S(1)}, f32[96,384]{1,0:T(8,128)S(1)}, u32[]{:S(2)}, u32[]{:S(2)}) collective-permute-start(f32[96,384]{1,0:T(8,128)S(1)} %add_add_fusion.kept), channel_id=1, source_target_pairs={{0,16},{1,17},{2,18},{3,19},{4,20},{5,21},{6,22},{7,23},{8,24},{9,... | collective-permute-start | bytes 442376 | tf_op jit(solution)/shard_map/ppermute | solution.py:22
  21.9 6.3 %collective-permute-start.7 = (f32[96,384]{1,0:T(8,128)S(1)}, f32[96,384]{1,0:T(8,128)S(1)}, u32[]{:S(2)}, u32[]{:S(2)}) collective-permute-start(f32[96,384]{1,0:T(8,128)S(1)} %add_add_fusion.kept), channel_id=1, source_target_pairs={{0,1},{1,0},{2,3},{3,2},{4,5},{5,4},{6,7},{7,6},{8,9},{9,8},{10,11... | collective-permute-start | bytes 442376 | tf_op jit(solution)/shard_map/ppermute | solution.py:22
  27.7 1.4 %collective-permute-start.8 = (f32[96,384]{1,0:T(8,128)S(1)}, f32[96,384]{1,0:T(8,128)S(1)}, u32[]{:S(2)}, u32[]{:S(2)}) collective-permute-start(f32[96,384]{1,0:T(8,128)S(1)} %collective-permute-done.6.received), channel_id=1, source_target_pairs={{0,1},{1,0},{2,3},{3,2},{4,5},{5,4},{6,7},{7,6},{8,9},{9,8},{10,11... | collective-permute-start | bytes 442376 | tf_op jit(solution)/shard_map/ppermute | solution.py:22
  27.7 13.6 %collective-permute-start.18 = (bf16[192,1024]{1,0:T(8,128)(2,1)S(1)}, bf16[192,1024]{1,0:T(8,128)(2,1)S(1)}, u32[]{:S(2)}, u32[]{:S(2)}) collective-permute-start(bf16[192,1024]{1,0:T(8,128)(2,1)S(1)} %collective-permute-done.17.refs_12_), channel_id=1, source_target_pairs={{0,1},{1,0},{2,3},{3,2},{4,5},{5,4},{6,7},{7,6},{8,9},{9,8},{10,11... | collective-permute-start | bytes 1179656 | tf_op jit(solution)/shard_map/ppermute | solution.py:22
  29.2 7.7 %collective-permute-start.11 = (s16[208,384]{1,0:T(8,128)(2,1)S(1)}, s16[208,384]{1,0:T(8,128)(2,1)S(1)}, u32[]{:S(2)}, u32[]{:S(2)}) collective-permute-start(s16[208,384]{1,0:T(8,128)(2,1)S(1)} %get-tuple-element.24.refs_0_), channel_id=1, source_target_pairs={{0,10},{1,7},{2,8},{3,5},{4,14},{5,3},{6,12},{7,1},{8,2},{9,15},{1... | collective-permute-start | bytes 479240 | tf_op jit(solution)/shard_map/ppermute | solution.py:27
  30.3 8.4 %collective-permute-start.10 = (s16[208,384]{1,0:T(8,128)(2,1)S(1)}, s16[208,384]{1,0:T(8,128)(2,1)S(1)}, u32[]{:S(2)}, u32[]{:S(2)}) collective-permute-start(s16[208,384]{1,0:T(8,128)(2,1)S(1)} %get-tuple-element.24.refs_0_), channel_id=1, source_target_pairs={{0,2},{1,13},{2,0},{3,15},{4,6},{5,9},{6,4},{7,11},{8,10},{9,5},{1... | collective-permute-start | bytes 479240 | tf_op jit(solution)/shard_map/ppermute | solution.py:27
  31.1 7.9 %collective-permute-start.9 = (s16[208,384]{1,0:T(8,128)(2,1)S(1)}, s16[208,384]{1,0:T(8,128)(2,1)S(1)}, u32[]{:S(2)}, u32[]{:S(2)}) collective-permute-start(s16[208,384]{1,0:T(8,128)(2,1)S(1)} %get-tuple-element.24.refs_0_), channel_id=1, source_target_pairs={{0,4},{1,9},{2,6},{3,11},{4,0},{5,13},{6,2},{7,15},{8,12},{9,1},{1... | collective-permute-start | bytes 479240 | tf_op jit(solution)/shard_map/ppermute | solution.py:27
  31.9 8.1 %collective-permute-start.15 = (s16[112,384]{1,0:T(8,128)(2,1)S(1)}, s16[112,384]{1,0:T(8,128)(2,1)S(1)}, u32[]{:S(2)}, u32[]{:S(2)}) collective-permute-start(s16[112,384]{1,0:T(8,128)(2,1)S(1)} %get-tuple-element.25), channel_id=1, source_target_pairs={{0,14},{1,15},{2,12},{3,13},{4,10},{5,11},{6,8},{7,9},{8,6},{9,7},... | collective-permute-start | bytes 258056 | tf_op jit(solution)/shard_map/ppermute | solution.py:22
  36.9 4.5 %collective-permute-start.14 = (s16[208,384]{1,0:T(8,128)(2,1)S(1)}, s16[208,384]{1,0:T(8,128)(2,1)S(1)}, u32[]{:S(2)}, u32[]{:S(2)}) collective-permute-start(s16[208,384]{1,0:T(8,128)(2,1)S(1)} %collective-permute-done.11.refs_3_), channel_id=1, source_target_pairs={{0,1},{1,0},{2,3},{3,2},{4,5},{5,4},{6,7},{7,6},{8,9},{9,8},{10,11... | collective-permute-start | bytes 479240 | tf_op jit(solution)/shard_map/ppermute | solution.py:22
  38.7 2.6 %collective-permute-start.13 = (s16[208,384]{1,0:T(8,128)(2,1)S(1)}, s16[208,384]{1,0:T(8,128)(2,1)S(1)}, u32[]{:S(2)}, u32[]{:S(2)}) collective-permute-start(s16[208,384]{1,0:T(8,128)(2,1)S(1)} %collective-permute-done.10.refs_2_), channel_id=1, source_target_pairs={{0,1},{1,0},{2,3},{3,2},{4,5},{5,4},{6,7},{7,6},{8,9},{9,8},{10,11... | collective-permute-start | bytes 479240 | tf_op jit(solution)/shard_map/ppermute | solution.py:22
  39.0 2.3 %collective-permute-start.12 = (s16[208,384]{1,0:T(8,128)(2,1)S(1)}, s16[208,384]{1,0:T(8,128)(2,1)S(1)}, u32[]{:S(2)}, u32[]{:S(2)}) collective-permute-start(s16[208,384]{1,0:T(8,128)(2,1)S(1)} %collective-permute-done.9.refs_1_), channel_id=1, source_target_pairs={{0,1},{1,0},{2,3},{3,2},{4,5},{5,4},{6,7},{7,6},{8,9},{9,8},{10,11... | collective-permute-start | bytes 479240 | tf_op jit(solution)/shard_map/ppermute | solution.py:22
  39.9 1.4 %collective-permute-start.16 = (s16[112,384]{1,0:T(8,128)(2,1)S(1)}, s16[112,384]{1,0:T(8,128)(2,1)S(1)}, u32[]{:S(2)}, u32[]{:S(2)}) collective-permute-start(s16[112,384]{1,0:T(8,128)(2,1)S(1)} %collective-permute-done.15.refs_7_), channel_id=1, source_target_pairs={{0,1},{1,0},{2,3},{3,2},{4,5},{5,4},{6,7},{7,6},{8,9},{9,8},{10,11... | collective-permute-start | bytes 258056 | tf_op jit(solution)/shard_map/ppermute | solution.py:22
  53.0 4.4 %collective-permute-start.19 = (f32[64,256]{1,0:T(8,128)S(1)}, f32[64,256]{1,0:T(8,128)S(1)}, u32[]{:S(2)}, u32[]{:S(2)}) collective-permute-start(f32[64,256]{1,0:T(8,128)S(1)} %get-tuple-element.29), channel_id=1, source_target_pairs={{0,4},{1,5},{2,6},{3,7},{4,0},{5,1},{6,2},{7,3},{8,12},{9,13},{10,... | collective-permute-start | bytes 196616 | tf_op jit(solution)/shard_map/ppermute | solution.py:22
  54.7 4.8 %collective-permute-start.20 = (f32[64,256]{1,0:T(8,128)S(1)}, f32[64,256]{1,0:T(8,128)S(1)}, u32[]{:S(2)}, u32[]{:S(2)}) collective-permute-start(f32[64,256]{1,0:T(8,128)S(1)} %get-tuple-element.30), channel_id=1, source_target_pairs={{0,8},{1,9},{2,10},{3,11},{4,12},{5,13},{6,14},{7,15},{8,0},{9,1},... | collective-permute-start | bytes 196616 | tf_op jit(solution)/shard_map/ppermute | solution.py:22
  55.1 5.2 %collective-permute-start.21 = (f32[64,256]{1,0:T(8,128)S(1)}, f32[64,256]{1,0:T(8,128)S(1)}, u32[]{:S(2)}, u32[]{:S(2)}) collective-permute-start(f32[64,256]{1,0:T(8,128)S(1)} %get-tuple-element.31), channel_id=1, source_target_pairs={{0,12},{1,13},{2,14},{3,15},{4,8},{5,9},{6,10},{7,11},{8,4},{9,5},... | collective-permute-start | bytes 196616 | tf_op jit(solution)/shard_map/ppermute | solution.py:22
  60.3 4.9 %collective-permute-start.22 = (f32[32,256]{1,0:T(8,128)S(1)}, f32[32,256]{1,0:T(8,128)S(1)}, u32[]{:S(2)}, u32[]{:S(2)}) collective-permute-start(f32[32,256]{1,0:T(8,128)S(1)} %get-tuple-element.32), channel_id=1, source_target_pairs={{0,16},{1,17},{2,18},{3,19},{4,20},{5,21},{6,22},{7,23},{8,24},{9,... | collective-permute-start | bytes 98312 | tf_op jit(solution)/shard_map/ppermute | solution.py:22
